TPU v7x, 32 devices: a whole 2x2x4 slice. The times are simulated.
32 devices in a mesh: ctx: 2 (over core), exp: 16 (over z, y, x).
Axes of the slice: x: 2, y: 2, z: 4, core: 2. Of those that a mesh axis runs over, the one named last changes fastest.
Arguments:
- inputs: bfloat16 [2, 16, 1024, 768], P(None, 'exp', 'ctx'), may hold values from -6 to 6
- cotangent: bfloat16 [2, 16, 1024, 768], P(None, 'exp', 'ctx'), may hold values from -6 to 6
- doc_ids: int32 [2, 16, 1024], P(None, 'exp'), may hold values from 0 to 3, never falling along the last dimension, each value on 1 to 512 neighbouring positions
- routes: int32 [2, 16, 1024, 2], P(None, 'exp', 'ctx'), may hold values from 0 to 15, all different within a row; in each aligned block of 512 rows (0 to 511, 512 to 1023, ..., all dimensions but the last counted through in order) at most 91 rows name the same one
- query_key_value_weight: bfloat16 [768, 2304], P(('ctx', 'exp')), may hold values from -0.21875 to 0.21875
- output_projection_weight: bfloat16 [768, 768], P(('ctx', 'exp')), may hold values from -0.875 to 0.875
- router: bfloat16 [768, 16], P(('ctx', 'exp')), may hold values from -0.15625 to 0.15625
- attn_gain: bfloat16 [768], P(('ctx', 'exp')), may hold values from 0.5 to 1.5
- expert_gain: bfloat16 [768], P(('ctx', 'exp')), may hold values from 0.5 to 1.5
- position_bias: bfloat16 [12, 32], replicated, may hold values from -3 to 3
- expert_up: bfloat16 [16, 768, 3072], P('exp', 'ctx'), may hold values from -0.21875 to 0.21875
- expert_down: bfloat16 [16, 3072, 768], P('exp', 'ctx'), may hold values from -0.109375 to 0.109375
Outputs:
- activations: bfloat16 [2, 16, 1024, 768], P(None, 'exp', 'ctx')
- input_grad: bfloat16 [2, 16, 1024, 768], P(None, 'exp', 'ctx')
- qkv_weight_grad: float32 [768, 2304], P(('ctx', 'exp'))
- proj_weight_grad: float32 [768, 768], P(('ctx', 'exp'))
- router_grad: float32 [768, 16], P(('ctx', 'exp'))
- attn_gain_grad: float32 [768], P(('ctx', 'exp'))
- expert_gain_grad: float32 [768], P(('ctx', 'exp'))
- pos_bias_grad: float32 [12, 32], replicated
- expert_up_grad: float32 [16, 768, 3072], P('exp', 'ctx')
- expert_down_grad: float32 [16, 3072, 768], P('exp', 'ctx')
Inputs may be any that keep to these rules, and one draw needn't show every extreme that they name: `routes`: each token names 2 different experts. In every aligned block of 512 positions of one sequence in one micro-batch no expert is named more than 91 times, a bound that some block reaches. `doc_ids`: document numbers of a sequence never fall; a document has at most half of 1024 tokens.
All inputs are finite; a program needn't handle non-finite values.
Results may differ from a plain program's by a relative error of at most 0.013.
Values may be sent and summed in bfloat16 or wider, within the bound.
No kernel may reach another device: no remote copies, remote signals or barrier semaphores. Data moves between devices by JAX's collectives and lax.ppermute only.
A program may use at most 320 MiB of HBM per device.

v0:
```python
import math

import jax
import jax.numpy as jnp
from jax import lax
from jax.sharding import PartitionSpec as P

HEADS = 12
HEAD = 64


epsilon = 1e-06
thresholds = (19, 21, 24, 27, 31, 35, 40, 46, 52, 59, 67, 77, 87, 99, 113)


def bucket_of(distance):
    distance = jnp.maximum(distance, 0)
    beyond = jnp.zeros_like(distance)
    for threshold in thresholds:
        beyond = beyond + (distance >= threshold).astype(jnp.int32)
    return jnp.where(distance < 16, distance, 16 + beyond)


def rms_norm(values, gain_vec):
    return (
        values * lax.rsqrt(jnp.mean(values * values, axis=-1, keepdims=True) + epsilon) * gain_vec
    )


def score_block(query_heads, key_rows, query_pos, key_pos, query_docs, key_docs, position_bias):
    length = key_rows.shape[0]
    key_heads = key_rows.reshape(length, HEADS, HEAD)
    raw_scores = (
        jnp.einsum("qhd,khd->hqk", query_heads, key_heads, preferred_element_type=jnp.float32)
        * 0.125
    )
    distance = query_pos[:, None] - key_pos[None, :]
    buckets = bucket_of(distance)
    one_hot_routes = (
        buckets[None] == jnp.arange(position_bias.shape[1], dtype=jnp.int32)[:, None, None]
    ).astype(jnp.bfloat16)
    raw_scores = raw_scores + jnp.einsum(
        "vs,smj->vmj", position_bias, one_hot_routes, preferred_element_type=jnp.float32
    )
    allowed = (distance >= 0) & (query_docs[:, None] == key_docs[None, :])
    return (jnp.where(allowed[None], raw_scores, -1000000000.0), one_hot_routes)


def shards(
    inputs,
    cotangent,
    doc_ids,
    routes,
    query_key_value_weight,
    output_projection_weight,
    router,
    attn_gain,
    expert_gain,
    position_bias,
    expert_up,
    expert_down,
):
    batches = inputs.shape[0]
    local_len = inputs.shape[2]
    model_width = inputs.shape[3]
    per_token = routes.shape[3]
    experts = lax.axis_size("exp")
    capacity = max(2, per_token * local_len * 10 // (7 * experts))
    slot_count = experts * capacity
    seq_len = doc_ids.shape[2]
    key_block = math.gcd(seq_len, 512)
    key_blocks = seq_len // key_block
    hidden_units = expert_up.shape[2]
    qkv_all, proj_all, router_all, attn_scale, expert_scale = (
        lax.all_gather(query_key_value_weight, ("ctx", "exp"), axis=0, tiled=True),
        lax.all_gather(output_projection_weight, ("ctx", "exp"), axis=0, tiled=True),
        lax.all_gather(router, ("ctx", "exp"), axis=0, tiled=True),
        lax.all_gather(attn_gain, ("ctx", "exp"), axis=0, tiled=True),
        lax.all_gather(expert_gain, ("ctx", "exp"), axis=0, tiled=True),
    )
    attn_scale = attn_scale.astype(jnp.float32)
    expert_scale = expert_scale.astype(jnp.float32)
    start_row = lax.axis_index("ctx") * local_len
    query_pos = start_row + jnp.arange(local_len, dtype=jnp.int32)
    block_ids = jnp.arange(key_blocks, dtype=jnp.int32)
    grad_qkv = jnp.zeros((model_width, 3 * model_width), jnp.float32)
    grad_proj = jnp.zeros((model_width, model_width), jnp.float32)
    grad_router = jnp.zeros((model_width, experts), jnp.float32)
    grad_attn = jnp.zeros((model_width,), jnp.float32)
    grad_expert = jnp.zeros((model_width,), jnp.float32)
    grad_bias = jnp.zeros(position_bias.shape, jnp.float32)
    grad_up = jnp.zeros((model_width, hidden_units), jnp.float32)
    grad_down = jnp.zeros((hidden_units, model_width), jnp.float32)
    outputs = []
    input_grads = []
    for batch_index in range(batches):
        whole_up = lax.all_gather(expert_up, "ctx", axis=1, tiled=True)
        whole_down = lax.all_gather(expert_down, "ctx", axis=1, tiled=True)
        expert_in = whole_up[0]
        expert_out = whole_down[0]
        token_rows = inputs[batch_index, 0].astype(jnp.float32)
        seq_docs = doc_ids[batch_index, 0]
        query_docs = lax.dynamic_slice_in_dim(seq_docs, start_row, local_len)
        normalized_input, norm_one_back = jax.vjp(rms_norm, token_rows, attn_scale)
        normed_low = normalized_input.astype(jnp.bfloat16)
        query_key_value = jnp.dot(normed_low, qkv_all, preferred_element_type=jnp.float32).astype(
            jnp.bfloat16
        )
        query_heads = query_key_value[:, :model_width].reshape(local_len, HEADS, HEAD)
        gathered = lax.all_gather(query_key_value[:, model_width:], "ctx", axis=0, tiled=True)
        kv_stack = gathered.reshape(key_blocks, key_block, 2 * model_width)
        doc_stack = seq_docs.reshape(key_blocks, key_block)

        def block_scores(element):
            kv_rows, key_docs, block_index = element
            key_pos = block_index * key_block + jnp.arange(key_block, dtype=jnp.int32)
            return score_block(
                query_heads,
                kv_rows[:, :model_width],
                query_pos,
                key_pos,
                query_docs,
                key_docs,
                position_bias,
            )

        def stats_step(state_pair, element):
            top_score, running_sum = state_pair
            scores, one_hot_routes = block_scores(element)
            new_top = jnp.maximum(top_score, jnp.max(scores, axis=2))
            running_sum = running_sum * jnp.exp(top_score - new_top) + jnp.sum(
                jnp.exp(scores - new_top[:, :, None]), axis=2
            )
            return ((new_top, running_sum), None)

        start_top = jnp.full((HEADS, local_len), -jnp.inf, jnp.float32)
        start_sum = jnp.zeros((HEADS, local_len), jnp.float32)
        (top_score, running_sum), _ = lax.scan(
            stats_step, (start_top, start_sum), (kv_stack, doc_stack, block_ids)
        )
        log_total = top_score + jnp.log(running_sum)

        def value_step(accumulated, element):
            scores, one_hot_routes = block_scores(element)
            probability = jnp.exp(scores - log_total[:, :, None]).astype(jnp.bfloat16)
            value_heads = element[0][:, model_width:].reshape(key_block, HEADS, HEAD)
            return (
                accumulated
                + jnp.einsum(
                    "hqk,khd->qhd", probability, value_heads, preferred_element_type=jnp.float32
                ),
                None,
            )

        start_out = jnp.zeros((local_len, HEADS, HEAD), jnp.float32)
        attention_result, _ = lax.scan(value_step, start_out, (kv_stack, doc_stack, block_ids))
        attended_low = attention_result.reshape(local_len, model_width).astype(jnp.bfloat16)
        hidden_state = token_rows + jnp.dot(
            attended_low, proj_all, preferred_element_type=jnp.float32
        )
        shared, norm_two_back = jax.vjp(rms_norm, hidden_state, expert_scale)
        shared_low = shared.astype(jnp.bfloat16)
        logits = jnp.dot(shared_low, router_all, preferred_element_type=jnp.float32)
        route_ids = routes[batch_index, 0]
        route_hot = route_ids[:, :, None] == jnp.arange(experts, dtype=jnp.int32)[None, None, :]
        chosen = jnp.sum(jnp.where(route_hot, logits[:, None, :], 0.0), axis=2)
        gate_exp = jnp.exp(chosen - jnp.max(chosen, axis=1, keepdims=True))
        gate_values = gate_exp / jnp.sum(gate_exp, axis=1, keepdims=True)
        counts = route_hot.reshape(local_len * per_token, experts).astype(jnp.int32)
        slot_rank = jnp.sum((jnp.cumsum(counts, axis=0) - 1) * counts, axis=1)
        slot_ids = route_ids.reshape(-1) * capacity + slot_rank
        placed_mask = jnp.arange(slot_count, dtype=jnp.int32)[:, None] == slot_ids[None, :]
        placed = placed_mask.astype(jnp.bfloat16)
        spread = jnp.any(placed_mask.reshape(slot_count, local_len, per_token), axis=2).astype(
            jnp.bfloat16
        )
        dispatched = jnp.dot(spread, shared_low, preferred_element_type=jnp.float32).astype(
            jnp.bfloat16
        )
        dispatched = dispatched.reshape(experts, capacity, model_width)
        arrived_rows = lax.all_to_all(dispatched, "exp", split_axis=0, concat_axis=0, tiled=True)
        pre_act = jnp.einsum(
            "scd,df->scf", arrived_rows, expert_in, preferred_element_type=jnp.float32
        )
        activated = jax.nn.gelu(pre_act).astype(jnp.bfloat16)
        expert_result = jnp.einsum(
            "scf,fd->scd", activated, expert_out, preferred_element_type=jnp.float32
        ).astype(jnp.bfloat16)
        expert_result, pre_act, activated, arrived = (
            expert_result,
            pre_act,
            activated,
            arrived_rows,
        )
        returned = lax.all_to_all(
            expert_result, "exp", split_axis=0, concat_axis=0, tiled=True
        ).reshape(slot_count, model_width)
        picked = returned[slot_ids].reshape(local_len, per_token, model_width).astype(jnp.float32)
        mixture = jnp.sum(gate_values[:, :, None] * picked, axis=1)
        outputs.append((hidden_state + mixture).astype(jnp.bfloat16))
        upstream = cotangent[batch_index, 0].astype(jnp.float32)
        gate_grad = jnp.sum(picked * upstream[:, None, :], axis=2)
        chosen_grad = gate_values * (
            gate_grad - jnp.sum(gate_values * gate_grad, axis=1, keepdims=True)
        )
        logit_grad = jnp.sum(jnp.where(route_hot, chosen_grad[:, :, None], 0.0), axis=1).astype(
            jnp.bfloat16
        )
        result_grad = (gate_values[:, :, None] * upstream[:, None, :]).astype(jnp.bfloat16)
        result_grad = result_grad.reshape(local_len * per_token, model_width)
        grad_sent = jnp.dot(placed, result_grad, preferred_element_type=jnp.float32).astype(
            jnp.bfloat16
        )
        grad_sent = grad_sent.reshape(experts, capacity, model_width)
        arrived_grad = lax.all_to_all(grad_sent, "exp", split_axis=0, concat_axis=0, tiled=True)
        act_grad = jnp.einsum(
            "scd,fd->scf", arrived_grad, expert_out, preferred_element_type=jnp.float32
        )
        act_grad, grad_arrived = (act_grad, arrived_grad)
        pre_grad = jax.vjp(jax.nn.gelu, pre_act)[1](act_grad)[0].astype(jnp.bfloat16)
        grad_down = grad_down + jnp.einsum(
            "scf,scd->fd", activated, grad_arrived, preferred_element_type=jnp.float32
        )
        grad_up = grad_up + jnp.einsum(
            "scd,scf->df", arrived, pre_grad, preferred_element_type=jnp.float32
        )
        route_grad = jnp.einsum(
            "scf,df->scd", pre_grad, expert_in, preferred_element_type=jnp.float32
        ).astype(jnp.bfloat16)
        grad_home = lax.all_to_all(
            route_grad, "exp", split_axis=0, concat_axis=0, tiled=True
        ).reshape(slot_count, model_width)
        shared_grad = jnp.sum(
            grad_home[slot_ids].reshape(local_len, per_token, model_width).astype(jnp.float32),
            axis=1,
        )
        shared_grad = shared_grad + jnp.einsum(
            "te,de->td", logit_grad, router_all, preferred_element_type=jnp.float32
        )
        grad_router = grad_router + jnp.einsum(
            "td,te->de", shared_low, logit_grad, preferred_element_type=jnp.float32
        )
        hidden_part, expert_gain_part = norm_two_back(shared_grad)
        grad_expert = grad_expert + expert_gain_part
        hidden_grad = upstream + hidden_part
        branch_grad = hidden_grad.astype(jnp.bfloat16)
        grad_proj = grad_proj + jnp.einsum(
            "tc,td->cd", attended_low, branch_grad, preferred_element_type=jnp.float32
        )
        attended_grad = jnp.einsum(
            "td,cd->tc", branch_grad, proj_all, preferred_element_type=jnp.float32
        )
        attended_grad = attended_grad.astype(jnp.bfloat16).reshape(local_len, HEADS, HEAD)

        def delta_step(accumulated, element):
            scores, one_hot_routes = block_scores(element)
            probability = jnp.exp(scores - log_total[:, :, None])
            value_heads = element[0][:, model_width:].reshape(key_block, HEADS, HEAD)
            prob_grad = jnp.einsum(
                "qhd,khd->hqk", attended_grad, value_heads, preferred_element_type=jnp.float32
            )
            return (accumulated + jnp.sum(probability * prob_grad, axis=2), None)

        delta, _ = lax.scan(
            delta_step, jnp.zeros((HEADS, local_len), jnp.float32), (kv_stack, doc_stack, block_ids)
        )

        def grad_step(state_pair, element):
            query_grad, bias_grad = state_pair
            scores, one_hot_routes = block_scores(element)
            probability = jnp.exp(scores - log_total[:, :, None])
            key_heads = element[0][:, :model_width].reshape(key_block, HEADS, HEAD)
            value_heads = element[0][:, model_width:].reshape(key_block, HEADS, HEAD)
            prob_grad = jnp.einsum(
                "qhd,khd->hqk", attended_grad, value_heads, preferred_element_type=jnp.float32
            )
            scores_gradient = (probability * (prob_grad - delta[:, :, None])).astype(jnp.bfloat16)
            query_grad = query_grad + jnp.einsum(
                "hqk,khd->qhd", scores_gradient, key_heads, preferred_element_type=jnp.float32
            )
            key_grad = (
                jnp.einsum(
                    "hqk,qhd->khd", scores_gradient, query_heads, preferred_element_type=jnp.float32
                )
                * 0.125
            )
            value_grad = jnp.einsum(
                "hqk,qhd->khd",
                probability.astype(jnp.bfloat16),
                attended_grad,
                preferred_element_type=jnp.float32,
            )
            bias_grad = bias_grad + jnp.einsum(
                "geu,peu->gp", scores_gradient, one_hot_routes, preferred_element_type=jnp.float32
            )
            joined = jnp.concatenate(
                [
                    key_grad.reshape(key_block, model_width),
                    value_grad.reshape(key_block, model_width),
                ],
                axis=1,
            )
            return ((query_grad, bias_grad), joined)

        start_query = jnp.zeros((local_len, HEADS, HEAD), jnp.float32)
        (query_grad, bias_step), kv_grads = lax.scan(
            grad_step,
            (start_query, jnp.zeros(position_bias.shape, jnp.float32)),
            (kv_stack, doc_stack, block_ids),
        )
        grad_bias = grad_bias + bias_step
        kv_rows_all = kv_grads.reshape(seq_len, 2 * model_width)
        kv_home = lax.psum_scatter(
            kv_rows_all.astype(jnp.bfloat16), "ctx", scatter_dimension=0, tiled=True
        ).astype(jnp.float32)
        qkv_grad = jnp.concatenate(
            [(query_grad * 0.125).reshape(local_len, model_width), kv_home], axis=1
        ).astype(jnp.bfloat16)
        grad_qkv = grad_qkv + jnp.einsum(
            "td,te->de", normed_low, qkv_grad, preferred_element_type=jnp.float32
        )
        normed_grad = jnp.einsum("te,de->td", qkv_grad, qkv_all, preferred_element_type=jnp.float32)
        input_part, attn_gain_part = norm_one_back(normed_grad)
        grad_attn = grad_attn + attn_gain_part
        input_grads.append((hidden_grad + input_part).astype(jnp.bfloat16))
    qkv_share, proj_share, router_share, attn_share, expert_share = (
        lax.psum_scatter(grad_qkv, ("ctx", "exp"), scatter_dimension=0, tiled=True),
        lax.psum_scatter(grad_proj, ("ctx", "exp"), scatter_dimension=0, tiled=True),
        lax.psum_scatter(grad_router, ("ctx", "exp"), scatter_dimension=0, tiled=True),
        lax.psum_scatter(grad_attn, ("ctx", "exp"), scatter_dimension=0, tiled=True),
        lax.psum_scatter(grad_expert, ("ctx", "exp"), scatter_dimension=0, tiled=True),
    )
    bias_total = lax.psum(grad_bias, ("ctx", "exp"))
    up_share, down_share = (
        lax.psum_scatter(
            grad_up[None].astype(jnp.bfloat16), "ctx", scatter_dimension=1, tiled=True
        ).astype(jnp.float32),
        lax.psum_scatter(
            grad_down[None].astype(jnp.bfloat16), "ctx", scatter_dimension=1, tiled=True
        ).astype(jnp.float32),
    )
    return (
        jnp.stack(outputs)[:, None],
        jnp.stack(input_grads)[:, None],
        qkv_share,
        proj_share,
        router_share,
        attn_share,
        expert_share,
        bias_total,
        up_share,
        down_share,
    )


def solution(mesh):
    placed = (
        P(None, "exp", "ctx", None),
        P(None, "exp", "ctx", None),
        P(None, "exp", None),
        P(None, "exp", "ctx", None),
        P(("ctx", "exp"), None),
        P(("ctx", "exp"), None),
        P(("ctx", "exp"), None),
        P(("ctx", "exp")),
        P(("ctx", "exp")),
        P(),
        P("exp", "ctx", None),
        P("exp", "ctx", None),
    )
    return jax.shard_map(
        shards,
        mesh=mesh,
        in_specs=placed,
        out_specs=(
            P(None, "exp", "ctx", None),
            P(None, "exp", "ctx", None),
            P(("ctx", "exp"), None),
            P(("ctx", "exp"), None),
            P(("ctx", "exp"), None),
            P(("ctx", "exp")),
            P(("ctx", "exp")),
            P(),
            P("exp", "ctx", None),
            P("exp", "ctx", None),
        ),
        check_vma=False,
    )
```

profile of v0, /device:TPU:0, one launch (start us, length us, event | category | flops | bytes accessed | tf_op | source)
XLA Modules:
  0.0 1873.4 jit_solution(13321541030485706818)
XLA Ops:
  9.7 42.1 %all-reduce.6 = (bf16[768]{0:T(1024)(128)(2,1)S(1)}, bf16[768]{0:T(1024)(128)(2,1)S(1)}) all-reduce(bf16[768]{0:T(1024)(128)(2,1)S(1)} %dynamic-update-slice, bf16[768]{0:T(1024)(128)(2,1)S(1)} %dynamic-update-slice.1), channel_id=1, replica_groups=mesh['ctx'=2,'exp'=16] {'ctx','exp'}, use_global_device_ids=true, to_apply=%add | all-reduce | flops 1536 | bytes 6144
  53.5 20.2 %all-gather.8.cloned.1.call-done = bf16[768,2304]{1,0:T(8,128)(2,1)} async-done(((bf16[24,2304]{1,0:T(8,128)(2,1)}), bf16[768,2304]{1,0:T(8,128)(2,1)}) %all-gather.8.cloned.1.call-update) | async-done | bytes 3538960 | tf_op jit(solution)/shard_map/all_gather | solution.py:75
  105.5 93.2 %while.100 = (s32[]{:T(128)}, f32[12,512]{1,0:T(8,128)S(1)}, f32[12,512]{1,0:T(8,128)S(1)}, s32[2]{0:T(128)S(1)}, s32[512]{0:T(512)S(1)}, /*index=5*/s32[2,512]{...) while((s32[]{:T(128)}, f32[12,512]{1,0:T(8,128)S(1)}, ...), condition=%wide.region_4.5_spmd.clone, body=%wide.region_1.4_spmd.clone.sunk | while | flops 645168128 | bytes 86848424 | solution.py:138
  164.3 17.7 copy.418
  198.8 85.5 %while.101 = (s32[]{:T(128)}, f32[512,12,64]{0,2,1:T(8,128)}, bf16[2,512,1536]{1,2,0:T(8,128)(2,1)}, s32[2]{0:T(128)S(1)}, s32[512]{0:T(512)S(1)}, /*index=5*/s3...) while((s32[]{:T(128)}, f32[512,12,64]{0,2,1:T(8,128)}, ...), condition=%wide.region_6.7_spmd.clone, body=%wide.region_5.6_spmd.clone.sunk | while | flops 1045431296 | bytes 66892716 | solution.py:156
  211.2 17.8 copy.420
  253.6 17.8 copy.420
  303.7 105.5 %all-gather = bf16[32,24,16]{1,2,0:T(8,128)(2,1)S(1)} all-gather(bf16[1,24,16]{1,2,0:T(8,128)(2,1)S(1)} %bitcast.743), channel_id=1, replica_groups=mesh['ctx'=2,'exp'=16] {'ctx','exp'}, dimensions={0}, use_global_device_ids=true | all-gather | bytes 25344 | tf_op jit(solution)/shard_map/all_gather | solution.py:77
  444.5 92.6 %while.102 = (s32[]{:T(128)}, f32[12,512]{1,0:T(8,128)S(1)}, f32[12,512]{1,0:T(8,128)S(1)}, s32[2]{0:T(128)S(1)}, s32[512]{0:T(512)S(1)}, /*index=5*/s32[2,512]{...) while((s32[]{:T(128)}, f32[12,512]{1,0:T(8,128)S(1)}, ...), condition=%wide.region_20.21_spmd.clone, body=%wide.region_17.20_spmd.clone.sunk | while | flops 645168128 | bytes 86848424 | solution.py:138
  537.1 18.7 multiply_convert_fusion.1
  575.7 22.0 %fusion.232 = bf16[16,91,3072]{2,1,0:T(8,128)(2,1)S(1)} fusion(f32[16,91,3072]{2,1,0:T(8,128)} %get-tuple-element.1666, bf16[16,91,768]{2,1,0:T(8,128)(2,1)} %all-to-all-done.4, bf16[1,3072,768]{2,1,0:T(8,128)(2,1)} %all-gather.16.cloned.1.call-done), kind=kOutput, calls=%fused_computation.318 | convolution fusion | flops 6959726592 | bytes 33792000 | tf_op jit(solution)/shard_map/scd,fd->scf/dot_general | solution.py:216
  634.0 84.9 %while.103 = (s32[]{:T(128)}, f32[512,12,64]{0,2,1:T(8,128)}, bf16[2,512,1536]{1,2,0:T(8,128)(2,1)}, s32[2]{0:T(128)S(1)}, s32[512]{0:T(512)S(1)}, /*index=5*/s3...) while((s32[]{:T(128)}, f32[512,12,64]{0,2,1:T(8,128)}, ...), condition=%wide.region_22.23_spmd.clone, body=%wide.region_21.22_spmd.clone.sunk | while | flops 1045431296 | bytes 66892716 | solution.py:156
  800.0 28.2 %all-to-all-done.2 = bf16[16,91,768]{2,1,0:T(8,128)(2,1)} async-done(((bf16[16,91,768]{2,1,0:T(8,128)(2,1)}), bf16[16,91,768]{2,1,0:T(8,128)(2,1)}, u32[]{:S(2)}, u32[]{:S(2)}) %all-to-all-start.2) | async-done | bytes 2236448 | tf_op jit(solution)/shard_map/all_to_all | solution.py:181
  897.7 22.2 %fusion.239 = bf16[16,91,3072]{2,1,0:T(8,128)(2,1)S(1)} fusion(f32[16,91,3072]{2,1,0:T(8,128)} %fusion.262, bf16[16,91,768]{2,1,0:T(8,128)(2,1)} %all-to-all-done.6, bf16[1,3072,768]{2,1,0:T(8,128)(2,1)} %all-gather.16.cloned.1.call-done), kind=kOutput, calls=%fused_computation.325 | convolution fusion | flops 6959726592 | bytes 33792000 | tf_op jit(solution)/shard_map/scd,fd->scf/dot_general | solution.py:216
  978.0 24.5 %all-to-all-done.7 = bf16[16,91,768]{2,1,0:T(8,128)(2,1)} async-done(((bf16[16,91,768]{2,1,0:T(8,128)(2,1)}), bf16[16,91,768]{2,1,0:T(8,128)(2,1)}, u32[]{:S(2)}, u32[]{:S(2)}) %all-to-all-start.7) | async-done | bytes 2236448 | tf_op jit(solution)/shard_map/all_to_all | solution.py:230
  1029.7 100.8 %while.104 = (s32[]{:T(128)}, f32[12,512]{1,0:T(8,128)S(1)}, s32[2]{0:T(128)S(1)}, s32[512]{0:T(512)S(1)}, s32[2,512]{1,0:T(2,128)S(1)}, /*index=5*/bf16[2,512,1...) while((s32[]{:T(128)}, f32[12,512]{1,0:T(8,128)S(1)}, ...), condition=%wide.region_39.40_spmd.clone, body=%wide.region_37.39_spmd.clone.sunk | while | flops 1047796736 | bytes 143275008 | solution.py:264
  1132.5 162.7 %while.105 = (s32[]{:T(128)}, f32[512,12,64]{0,2,1:T(8,128)}, f32[12,32]{1,0:T(8,128)S(1)}, bf16[2,512,1536]{2,1,0:T(8,128)(2,1)}, bf16[2,512,1536]{1,2,0:T(8,12...) while((s32[]{:T(128)}, f32[512,12,64]{0,2,1:T(8,128)}, ...), condition=%wide.region_41.42_spmd.clone, body=%wide.region_40.41_spmd.clone.sunk | while | flops 2476476160 | bytes 212148848 | solution.py:306
  1299.0 100.9 %while.106 = (s32[]{:T(128)}, f32[12,512]{1,0:T(8,128)S(1)}, s32[2]{0:T(128)S(1)}, s32[512]{0:T(512)S(1)}, s32[2,512]{1,0:T(2,128)S(1)}, /*index=5*/bf16[2,512,1...) while((s32[]{:T(128)}, f32[12,512]{1,0:T(8,128)S(1)}, ...), condition=%wide.region_51.52_spmd.clone, body=%wide.region_49.51_spmd.clone.sunk | while | flops 1047796736 | bytes 143275008 | solution.py:264
  1402.0 163.8 %while.107 = (s32[]{:T(128)}, f32[512,12,64]{0,2,1:T(8,128)}, f32[12,32]{1,0:T(8,128)S(1)}, bf16[2,512,1536]{2,1,0:T(8,128)(2,1)}, bf16[2,512,1536]{1,2,0:T(8,12...) while((s32[]{:T(128)}, f32[512,12,64]{0,2,1:T(8,128)}, ...), condition=%wide.region_53.54_spmd.clone, body=%wide.region_52.53_spmd.clone.sunk | while | flops 2476476160 | bytes 212148848 | solution.py:306
  1415.5 17.8 copy.434
  1496.0 17.7 copy.434
  1670.9 44.2 %all-reduce.5 = (f32[768,16]{0,1:T(8,128)S(1)}, f32[768]{0:T(1024)S(1)}, f32[768]{0:T(1024)S(1)}, f32[12,32]{1,0:T(8,128)}) all-reduce(f32[768,16]{0,1:T(8,128)S(1)} %convolution_add_fusion.4, f32[768]{0:T(1024)S(1)} %add.1246, f32[768]{0:T(1024)S(1)} %add.1247, ...), channel_id=6, replica_groups=mesh['ctx'=2,'exp'=16] {'ctx','exp'}, use_global_device_ids=true, to_apply=%region_58.59.clone | all-reduce | flops 14208 | bytes 113664
  1721.4 19.9 %reduce-scatter.14.cloned.1.call-done = f32[24,768]{1,0:T(8,128)} async-done(((f32[768,768]{1,0:T(8,128)}), f32[24,768]{1,0:T(8,128)}) %reduce-scatter.14.cloned.1.call-update) | async-done | bytes 73744 | tf_op jit(solution)/shard_map/reduce_scatter | solution.py:328
  1741.4 125.0 %reduce-scatter.12.cloned.1.call-done = f32[24,2304]{1,0:T(8,128)} async-done(((f32[768,2304]{1,0:T(8,128)}), f32[24,2304]{1,0:T(8,128)}) %reduce-scatter.12.cloned.1.call-update) | async-done | bytes 221200 | tf_op jit(solution)/shard_map/reduce_scatter | solution.py:327
  (785 shorter events, 1282.9 us)
Async XLA Ops:
  7.2 66.6 %all-gather.8.cloned.1.call-start = ((), (), s32[]{:S(2)}) async-start(), calls=%async_computation.14 | async-start | bytes 3649536 | tf_op jit(solution)/shard_map/all_gather | solution.py:75
  7.9 92.9 %all-gather.10.cloned.1.call-start = ((), (), s32[]{:S(2)}) async-start(), calls=%async_computation.15 | async-start | bytes 4718592 | tf_op jit(solution)/shard_map/all_gather | solution.py:110
  80.8 205.3 %all-gather.12.cloned.1.call-start = ((), (), s32[]{:S(2)}) async-start(), calls=%async_computation.16 | async-start | bytes 1216512 | tf_op jit(solution)/shard_map/all_gather | solution.py:76
  81.5 353.6 %all-gather.18.cloned.1.call-start = ((), (), s32[]{:S(2)}) async-start(), calls=%async_computation.19 | async-start | bytes 4718592 | tf_op jit(solution)/shard_map/all_gather | solution.py:110
  88.4 448.6 %all-gather.14.cloned.1.call-start = ((), (), s32[]{:S(2)}) async-start(), calls=%async_computation.17 | async-start | bytes 7077888 | tf_op jit(solution)/shard_map/all_gather | solution.py:97
  296.9 112.6 %copy-start.33 = (s32[1,1,512,2]{3,2,1,0:T(8,128)S(1)}, s32[1,1,512,2]{3,2,1,0:T(8,128)}, u32[]{:S(2)}) copy-start(s32[1,1,512,2]{3,2,1,0:T(8,128)} %copy-done.32) | copy-start | bytes 12292
  296.9 142.9 %all-to-all-start = ((bf16[16,91,768]{2,1,0:T(8,128)(2,1)}), bf16[16,91,768]{2,1,0:T(8,128)(2,1)}, u32[]{:S(2)}, u32[]{:S(2)}) async-start(bf16[16,91,768]{2,1,0:T(8,128)(2,1)} %reshape.1671), calls=%async_computation | async-start | bytes 4718592 | tf_op jit(solution)/shard_map/all_to_all | solution.py:181
  302.6 107.0 %copy-start.44 = (bf16[2,1,512,768]{3,2,1,0:T(8,128)(2,1)S(1)}, bf16[2,1,512,768]{3,2,1,0:T(8,128)(2,1)}, u32[]{:S(2)}) copy-start(bf16[2,1,512,768]{3,2,1,0:T(8,128)(2,1)} %param.29) | copy-start | bytes 4718596
  302.6 253.1 %all-gather.16.cloned.1.call-start = ((), (), s32[]{:S(2)}) async-start(), calls=%async_computation.18 | async-start | bytes 7077888 | tf_op jit(solution)/shard_map/all_gather | solution.py:98
  303.4 120.1 %copy-start.30 = (s32[1,1,512,2]{3,2,1,0:T(8,128)}, s32[1,1,512,2]{3,2,1,0:T(8,128)S(1)}, u32[]{:S(2)}) copy-start(s32[1,1,512,2]{3,2,1,0:T(8,128)S(1)} %copy.366) | copy-start | bytes 12292
  303.7 119.5 %copy-start.93 = (s32[1024]{0:T(1024)}, s32[1024]{0:T(1024)S(1)}, u32[]{:S(2)}) copy-start(s32[1024]{0:T(1024)S(1)} %eq.368) | copy-start | bytes 12292
  439.8 128.5 %all-to-all-start.4 = ((bf16[16,91,768]{2,1,0:T(8,128)(2,1)}), bf16[16,91,768]{2,1,0:T(8,128)(2,1)}, u32[]{:S(2)}, u32[]{:S(2)}) async-start(bf16[16,91,768]{2,1,0:T(8,128)(2,1)} %reshape.1678), calls=%async_computation.4 | async-start | bytes 4718592 | tf_op jit(solution)/shard_map/all_to_all | solution.py:215
  568.3 54.7 %all-to-all-start.1 = ((bf16[16,91,768]{2,1,0:T(8,128)(2,1)}), bf16[16,91,768]{2,1,0:T(8,128)(2,1)S(1)}, u32[]{:S(2)}, u32[]{:S(2)}) async-start(bf16[16,91,768]{2,1,0:T(8,128)(2,1)} %fusion.278), calls=%async_computation.1 | async-start | bytes 4718592 | tf_op jit(solution)/shard_map/all_to_all | solution.py:195
  623.0 123.8 %all-to-all-start.5 = ((bf16[16,91,768]{2,1,0:T(8,128)(2,1)}), bf16[16,91,768]{2,1,0:T(8,128)(2,1)}, u32[]{:S(2)}, u32[]{:S(2)}) async-start(bf16[16,91,768]{2,1,0:T(8,128)(2,1)} %fusion.272), calls=%async_computation.5 | async-start | bytes 4718592 | tf_op jit(solution)/shard_map/all_to_all | solution.py:230
  774.2 54.0 %all-to-all-start.2 = ((bf16[16,91,768]{2,1,0:T(8,128)(2,1)}), bf16[16,91,768]{2,1,0:T(8,128)(2,1)}, u32[]{:S(2)}, u32[]{:S(2)}) async-start(bf16[16,91,768]{2,1,0:T(8,128)(2,1)} %reshape.1676), calls=%async_computation.2 | async-start | bytes 4718592 | tf_op jit(solution)/shard_map/all_to_all | solution.py:181
  828.2 58.2 %all-to-all-start.6 = ((bf16[16,91,768]{2,1,0:T(8,128)(2,1)}), bf16[16,91,768]{2,1,0:T(8,128)(2,1)}, u32[]{:S(2)}, u32[]{:S(2)}) async-start(bf16[16,91,768]{2,1,0:T(8,128)(2,1)} %reshape.1682), calls=%async_computation.7 | async-start | bytes 4718592 | tf_op jit(solution)/shard_map/all_to_all | solution.py:215
  886.4 58.2 %all-to-all-start.3 = ((bf16[16,91,768]{2,1,0:T(8,128)(2,1)}), bf16[16,91,768]{2,1,0:T(8,128)(2,1)}, u32[]{:S(2)}, u32[]{:S(2)}) async-start(bf16[16,91,768]{2,1,0:T(8,128)(2,1)} %fusion.281), calls=%async_computation.3 | async-start | bytes 4718592 | tf_op jit(solution)/shard_map/all_to_all | solution.py:195
  944.6 57.9 %all-to-all-start.7 = ((bf16[16,91,768]{2,1,0:T(8,128)(2,1)}), bf16[16,91,768]{2,1,0:T(8,128)(2,1)}, u32[]{:S(2)}, u32[]{:S(2)}) async-start(bf16[16,91,768]{2,1,0:T(8,128)(2,1)} %fusion.275), calls=%async_computation.8 | async-start | bytes 4718592 | tf_op jit(solution)/shard_map/all_to_all | solution.py:230
  955.4 680.4 %reduce-scatter.8.cloned.1.call-start = ((), (), s32[]{:S(2)}) async-start(), calls=%async_computation.20 | async-start | bytes 4718592 | tf_op jit(solution)/shard_map/reduce_scatter | solution.py:313
  1399.9 242.5 %reduce-scatter.10.cloned.1.call-start = ((), (), s32[]{:S(2)}) async-start(), calls=%async_computation.21 | async-start | bytes 4718592 | tf_op jit(solution)/shard_map/reduce_scatter | solution.py:313
  1565.8 90.5 %reduce-scatter.18.cloned.1.call-start = ((), (), s32[]{:S(2)}) async-start(), calls=%async_computation.25 | async-start | bytes 7077888 | tf_op jit(solution)/shard_map/reduce_scatter | solution.py:338
  1594.5 66.1 %reduce-scatter.16.cloned.1.call-start = ((), (), s32[]{:S(2)}) async-start(), calls=%async_computation.24 | async-start | bytes 7077888 | tf_op jit(solution)/shard_map/reduce_scatter | solution.py:335
  1619.6 121.8 %reduce-scatter.14.cloned.1.call-start = ((), (), s32[]{:S(2)}) async-start(), calls=%async_computation.23 | async-start | bytes 2433024 | tf_op jit(solution)/shard_map/reduce_scatter | solution.py:328
  1625.2 241.2 %reduce-scatter.12.cloned.1.call-start = ((), (), s32[]{:S(2)}) async-start(), calls=%async_computation.22 | async-start | bytes 7299072 | tf_op jit(solution)/shard_map/reduce_scatter | solution.py:327
  (150 other events, 1200.3 us)
Sparse Core Ops, SparseCore 0:
  10.9 62.8 all-gather.7
  80.9 10.9 all-gather.9
  94.8 55.2 all-gather.11
  151.5 11.0 all-gather.17
  164.0 15.5 all-gather.13
  304.7 15.6 all-gather.15
  1400.1 15.9 reduce-scatter.7
  1565.9 15.1 reduce-scatter.9
  1594.6 16.3 reduce-scatter.17
  1619.7 15.4 reduce-scatter.15
  1641.1 100.2 reduce-scatter.13
  1748.4 117.8 reduce-scatter.11
where the time goes:
time: 1890 us; the launch traced here: 1870 us
  matrix products  642 us (34%)
  local copies, waits for them, and re-layouts  533 us (28%)
  waiting for transfers between devices  260 us (14%)
  blocking collectives  192 us (10%)
  other arithmetic  147 us (8%)
  starting transfers between devices  70.4 us (4%)
    dot_general x16, local copies, waits for them, and re-layouts, score_block(): jnp.einsum('vs,smj->vmj', position_bias, one_hot_routes, preferred_elemen...  283 us
    dot_general x16, matrix products, score_block(): jnp.einsum('vs,smj->vmj', position_bias, one_hot_routes, preferred_elemen...  137 us
    reduce_scatter x1, waiting for transfers between devices, shards(): lax.psum_scatter(grad_qkv, ('ctx', 'exp'), scatter_dimension=0, tiled=True)  125 us
    all_gather x1, blocking collectives, shards(): lax.all_gather(router, ('ctx', 'exp'), axis=0, tiled=True)  106 us
    dot_general x12, matrix products, score_block(): jnp.einsum('qhd,khd->hqk', query_heads, key_heads, preferred_element_type...  95.7 us
    unnamed x2, blocking collectives  86.2 us
    convert_element_type x4, local copies, waits for them, and re-layouts, grad_step(): (probability * (prob_grad - delta[:, :, None])).astype(jnp.bfloat16)  58.3 us
    dot_general x2, matrix products, shards(): jnp.einsum('scd,fd->scf', arrived_grad, expert_out, preferred_element_typ...  44.2 us
  transfers between devices with their start and end apart: 20, of which 8 were waited for; matrix products, arithmetic and copies ran while one was open for 47% of the time, Pallas kernels for 0%

commit v1 on v0

v1 whole, which is shorter than its diff:
```python
import functools

import jax
import jax.numpy as jnp
from jax import lax
from jax.experimental import pallas as pl
from jax.experimental.pallas import tpu as pltpu
from jax.sharding import PartitionSpec as P

HEADS = 12
HEAD = 64
PAIRS = HEADS // 2
TILE = 128
BACK = 512
SPAN = BACK // TILE + 1
MASKED = -1000000000.0

epsilon = 1e-06
thresholds = (19, 21, 24, 27, 31, 35, 40, 46, 52, 59, 67, 77, 87, 99, 113)
bf16 = jnp.bfloat16
f32 = jnp.float32


def bucket_of(distance):
    distance = jnp.maximum(distance, 0)
    beyond = jnp.zeros_like(distance)
    for threshold in thresholds:
        beyond = beyond + (distance >= threshold).astype(jnp.int32)
    return jnp.where(distance < 16, distance, 16 + beyond)


def mm(a, b, dims):
    return lax.dot_general(a, b, (dims, ((), ())), preferred_element_type=f32)


def stack_heads(rows):
    lane = lax.broadcasted_iota(jnp.int32, rows.shape, 1)
    zero = jnp.zeros_like(rows)
    return jnp.concatenate(
        [jnp.where(lane < HEAD, rows, zero), jnp.where(lane >= HEAD, rows, zero)], axis=0
    )


def fold_heads(wide):
    return jnp.concatenate([wide[:HEAD, :TILE], wide[HEAD:, TILE:]], axis=0)


def fill_mask(mask, qd_ref, kd_ref):
    for qi in range(qd_ref.shape[1] // TILE):
        docs_row = qd_ref[:, qi * TILE : (qi + 1) * TILE]
        for j in range(SPAN):
            kt = (qi + j) * TILE
            column = jnp.broadcast_to(kd_ref[:, kt : kt + TILE], (TILE, TILE)).T
            mask[qi, j * TILE : (j + 1) * TILE, :] = jnp.where(
                column == docs_row, 0.0, MASKED
            ).astype(f32)


def fill_bias(bias, bv_ref):
    for head in range(2):
        for d in range(2):
            row = jnp.broadcast_to(bv_ref[0, 2 * head + d : 2 * head + d + 1, :], (TILE, 2 * TILE))
            rolled = pltpu.roll(row, 0, 1, stride=1, stride_axis=0)
            bias[d, :, head * TILE : (head + 1) * TILE] = rolled[:, :TILE]


def masked_scores(scores, mask, bias, qi, tiles):
    parts = []
    for j in range(tiles):
        d = tiles - 1 - j
        off = (SPAN - tiles + j) * TILE
        m = mask[qi, off : off + TILE, :]
        x = scores[j * TILE : (j + 1) * TILE] + jnp.concatenate([m, m], axis=1)
        if d < 2:
            x = x + bias[d]
        parts.append(x)
    return parts


def fwd_kernel(tiles, q_ref, k_ref, v_ref, kp_ref, vp_ref, qd_ref, kd_ref, bv_ref, o_ref, lse_ref,
               kwin, vwin_t, bias, mask):
    @pl.when(pl.program_id(0) == 0)
    def _():
        fill_mask(mask, qd_ref, kd_ref)

    fill_bias(bias, bv_ref)
    kwin[:BACK] = kp_ref[...]
    kwin[BACK:] = k_ref[...]
    for t in range(BACK // TILE):
        vwin_t[:, t * TILE : (t + 1) * TILE] = vp_ref[t * TILE : (t + 1) * TILE, :].T
    for t in range(q_ref.shape[0] // TILE):
        at = BACK + t * TILE
        vwin_t[:, at : at + TILE] = v_ref[t * TILE : (t + 1) * TILE, :].T

    def step(qi, carry):
        q0 = pl.multiple_of(qi * TILE, TILE)
        q2 = stack_heads(q_ref[pl.ds(q0, TILE), :] * 0.125)

        def branch(count):
            def go():
                lo = pl.multiple_of((qi + SPAN - count) * TILE, TILE)
                keys = kwin[pl.ds(lo, count * TILE), :]
                parts = masked_scores(mm(keys, q2, ((1,), (1,))), mask, bias, qi, count)
                top = functools.reduce(jnp.maximum, parts)
                top = jnp.max(top, axis=0, keepdims=True)
                probs = [jnp.exp(x - top) for x in parts]
                total = jnp.sum(functools.reduce(jnp.add, probs), axis=0, keepdims=True)
                low = jnp.concatenate([p.astype(bf16) for p in probs], axis=0)
                out = fold_heads(mm(vwin_t[:, pl.ds(lo, count * TILE)], low, ((1,), (0,))))
                inv = 1.0 / total
                row = lax.broadcasted_iota(jnp.int32, (TILE, TILE), 0)
                out = out * jnp.where(row < HEAD, inv[:, :TILE], inv[:, TILE:])
                o_ref[pl.ds(q0, TILE), :] = out.T.astype(bf16)
                lse_ref[0, pl.ds(qi, 1), :] = top + jnp.log(total)
                return 0

            return go

        lax.switch(tiles[qi] - 1, [branch(c) for c in range(1, SPAN + 1)])
        return carry

    lax.fori_loop(0, q_ref.shape[0] // TILE, step, 0)


def bwd_kernel(tiles, q_ref, k_ref, v_ref, kp_ref, vp_ref, qd_ref, kd_ref, bv_ref, o_ref, do_ref,
               lse_ref, dq_ref, dk_ref, dv_ref, dkp_ref, dvp_ref, near_ref,
               kwin, kwin_t, vwin, dk, dv, near, bias, mask):
    @pl.when(pl.program_id(0) == 0)
    def _():
        fill_mask(mask, qd_ref, kd_ref)

    fill_bias(bias, bv_ref)
    kwin[:BACK] = kp_ref[...]
    kwin[BACK:] = k_ref[...]
    vwin[:BACK] = vp_ref[...]
    vwin[BACK:] = v_ref[...]
    for t in range(kwin.shape[0] // TILE):
        kwin_t[:, t * TILE : (t + 1) * TILE] = kwin[t * TILE : (t + 1) * TILE, :].T
    dk[...] = jnp.zeros_like(dk)
    dv[...] = jnp.zeros_like(dv)
    near[...] = jnp.zeros_like(near)

    def step(qi, carry):
        q0 = pl.multiple_of(qi * TILE, TILE)
        q2 = stack_heads(q_ref[pl.ds(q0, TILE), :] * 0.125)
        do = do_ref[pl.ds(q0, TILE), :]
        do2 = stack_heads(do)
        lse = lse_ref[0, pl.ds(qi, 1), :]
        prod = (do.astype(f32) * o_ref[pl.ds(q0, TILE), :].astype(f32)).T
        delta = jnp.concatenate(
            [jnp.sum(prod[:HEAD], axis=0, keepdims=True),
             jnp.sum(prod[HEAD:], axis=0, keepdims=True)],
            axis=1,
        )

        def branch(count):
            def go():
                lo = pl.multiple_of((qi + SPAN - count) * TILE, TILE)
                rows = pl.ds(lo, count * TILE)
                parts = masked_scores(
                    mm(kwin[rows, :], q2, ((1,), (1,))), mask, bias, qi, count
                )
                prob_grad = mm(vwin[rows, :], do2, ((1,), (1,)))
                lows = []
                grads = []
                for j in range(count):
                    prob = jnp.exp(parts[j] - lse)
                    grad = prob * (prob_grad[j * TILE : (j + 1) * TILE] - delta)
                    if j == count - 1:
                        near[...] += grad
                    elif j == count - 2:
                        r = lax.broadcasted_iota(jnp.int32, grad.shape, 0)
                        c = lax.broadcasted_iota(jnp.int32, grad.shape, 1)
                        c = jnp.where(c >= TILE, c - TILE, c)
                        near[...] += jnp.where(c < r, grad, 0.0)
                    lows.append(prob.astype(bf16))
                    grads.append(grad.astype(bf16))
                low = jnp.concatenate(lows, axis=0)
                score_grad = jnp.concatenate(grads, axis=0)
                dk[rows, :] += mm(score_grad, q2, ((1,), (0,)))
                dv[rows, :] += mm(low, do2, ((1,), (0,)))
                dq = fold_heads(mm(kwin_t[:, rows], score_grad, ((1,), (0,))))
                dq_ref[pl.ds(q0, TILE), :] = (dq.T * 0.125).astype(bf16)
                return 0

            return go

        lax.switch(tiles[qi] - 1, [branch(c) for c in range(1, SPAN + 1)])
        return carry

    lax.fori_loop(0, q_ref.shape[0] // TILE, step, 0)
    dkp_ref[...] = dk[:BACK].astype(bf16)
    dk_ref[...] = dk[BACK:].astype(bf16)
    dvp_ref[...] = dv[:BACK].astype(bf16)
    dv_ref[...] = dv[BACK:].astype(bf16)
    for head in range(2):
        at = slice(head * TILE, (head + 1) * TILE)
        turned = near[:, at]
        r = lax.broadcasted_iota(jnp.int32, turned.shape, 0)
        bit = 1
        while bit < TILE:
            turned = jnp.where((r & bit) > 0, pltpu.roll(turned, TILE - bit, 1), turned)
            bit *= 2
        near_ref[0, :, at] = jnp.sum(turned, axis=0, keepdims=True)


def attention_specs(length):
    full = lambda p, *_: (0, 0)
    lanes = lambda off: (lambda p, *_: (0, p + off))
    return [
        pl.BlockSpec((length, TILE), lanes(0)),
        pl.BlockSpec((length, TILE), lanes(PAIRS)),
        pl.BlockSpec((length, TILE), lanes(2 * PAIRS)),
        pl.BlockSpec((BACK, TILE), lanes(0)),
        pl.BlockSpec((BACK, TILE), lanes(PAIRS)),
        pl.BlockSpec((1, length), full),
        pl.BlockSpec((1, BACK + length), full),
        pl.BlockSpec((1, 4, 2 * TILE), lambda p, *_: (p, 0, 0)),
    ]


def attend(tiles, qkv, kv_back, query_docs, key_docs, bias_rows):
    length = qkv.shape[0]
    width = HEADS * HEAD
    blocks = length // TILE
    return pl.pallas_call(
        fwd_kernel,
        grid_spec=pltpu.PrefetchScalarGridSpec(
            num_scalar_prefetch=1,
            grid=(PAIRS,),
            in_specs=attention_specs(length),
            out_specs=[
                pl.BlockSpec((length, TILE), lambda p, *_: (0, p)),
                pl.BlockSpec((1, blocks, 2 * TILE), lambda p, *_: (p, 0, 0)),
            ],
            scratch_shapes=[
                pltpu.VMEM((BACK + length, TILE), bf16),
                pltpu.VMEM((TILE, BACK + length), bf16),
                pltpu.VMEM((2, TILE, 2 * TILE), f32),
                pltpu.VMEM((blocks, SPAN * TILE, TILE), f32),
            ],
        ),
        out_shape=[
            jax.ShapeDtypeStruct((length, width), bf16),
            jax.ShapeDtypeStruct((PAIRS, blocks, 2 * TILE), f32),
        ],
        compiler_params=pltpu.CompilerParams(vmem_limit_bytes=32 * 2**20),
        cost_estimate=pl.CostEstimate(
            flops=4 * 2 * HEADS * length * BACK * 128, bytes_accessed=6 * 2**20,
            transcendentals=HEADS * length * BACK,
        ),
        name="attend",
    )(tiles, qkv, qkv, qkv, kv_back, kv_back, query_docs, key_docs, bias_rows)


def attend_back(tiles, qkv, kv_back, query_docs, key_docs, bias_rows, out, out_grad, lse):
    length = qkv.shape[0]
    width = HEADS * HEAD
    blocks = length // TILE
    own = pl.BlockSpec((length, TILE), lambda p, *_: (0, p))
    back = pl.BlockSpec((BACK, TILE), lambda p, *_: (0, p))
    rows = jax.ShapeDtypeStruct((length, width), bf16)
    back_rows = jax.ShapeDtypeStruct((BACK, width), bf16)
    return pl.pallas_call(
        bwd_kernel,
        grid_spec=pltpu.PrefetchScalarGridSpec(
            num_scalar_prefetch=1,
            grid=(PAIRS,),
            in_specs=attention_specs(length)
            + [own, own, pl.BlockSpec((1, blocks, 2 * TILE), lambda p, *_: (p, 0, 0))],
            out_specs=[own, own, own, back, back,
                       pl.BlockSpec((1, 1, 2 * TILE), lambda p, *_: (p, 0, 0))],
            scratch_shapes=[
                pltpu.VMEM((BACK + length, TILE), bf16),
                pltpu.VMEM((TILE, BACK + length), bf16),
                pltpu.VMEM((BACK + length, TILE), bf16),
                pltpu.VMEM((BACK + length, TILE), f32),
                pltpu.VMEM((BACK + length, TILE), f32),
                pltpu.VMEM((TILE, 2 * TILE), f32),
                pltpu.VMEM((2, TILE, 2 * TILE), f32),
                pltpu.VMEM((blocks, SPAN * TILE, TILE), f32),
            ],
        ),
        out_shape=[rows, rows, rows, back_rows, back_rows,
                   jax.ShapeDtypeStruct((PAIRS, 1, 2 * TILE), f32)],
        compiler_params=pltpu.CompilerParams(vmem_limit_bytes=32 * 2**20),
        cost_estimate=pl.CostEstimate(
            flops=10 * 2 * HEADS * length * BACK * 128, bytes_accessed=12 * 2**20,
            transcendentals=HEADS * length * BACK,
        ),
        name="attend_back",
    )(tiles, qkv, qkv, qkv, kv_back, kv_back, query_docs, key_docs, bias_rows, out, out_grad, lse)


def is_power(n):
    return n & (n - 1) == 0


def rounds_of(size):
    bits = [1 << b for b in range(size.bit_length() - 1)]
    return bits[::-1]


def swap(x, axis, bit):
    size = lax.axis_size(axis)
    return lax.ppermute(x, axis, [(i, i ^ bit) for i in range(size)])


def gather_rows(x):
    if not (is_power(lax.axis_size("ctx")) and is_power(lax.axis_size("exp"))):
        return lax.all_gather(x, ("ctx", "exp"), axis=0, tiled=True)
    for axis in ("exp", "ctx"):
        me = lax.axis_index(axis)
        held = x[None]
        for bit in rounds_of(lax.axis_size(axis)):
            other = swap(held, axis, bit)
            high = (me & bit) > 0
            first, second = jnp.where(high, other, held), jnp.where(high, held, other)
            held = jnp.stack([first, second], axis=1).reshape((-1,) + x.shape)
        x = held.reshape((-1,) + x.shape[1:])
    return x


def pair_rows(x, axis):
    if lax.axis_size("ctx") != 2:
        return lax.all_gather(x, "ctx", axis=axis, tiled=True)
    other = swap(x, "ctx", 1)
    high = lax.axis_index("ctx") > 0
    return jnp.concatenate(
        [jnp.where(high, other, x), jnp.where(high, x, other)], axis=axis
    )


def send_half(x, axis):
    ways = lax.axis_size("ctx")
    if ways != 2:
        return lax.psum_scatter(x.astype(bf16), "ctx", scatter_dimension=axis, tiled=True).astype(f32)
    part = x.shape[axis] // 2
    me = lax.axis_index("ctx")
    mine = lax.dynamic_slice_in_dim(x, me * part, part, axis)
    theirs = lax.dynamic_slice_in_dim(x, (1 - me) * part, part, axis)
    return mine + swap(theirs.astype(bf16), "ctx", 1).astype(f32)


def scatter_sum(x):
    x = send_half(x, 0)
    ways = lax.axis_size("exp")
    parts = lax.all_to_all(x.astype(bf16), "exp", split_axis=0, concat_axis=0, tiled=True)
    return jnp.sum(parts.reshape(ways, -1, x.shape[1]).astype(f32), axis=0)


def shards(
    inputs,
    cotangent,
    doc_ids,
    routes,
    query_key_value_weight,
    output_projection_weight,
    router,
    attn_gain,
    expert_gain,
    position_bias,
    expert_up,
    expert_down,
):
    batches = inputs.shape[0]
    length = inputs.shape[2]
    width = inputs.shape[3]
    top = routes.shape[3]
    ways = lax.axis_size("ctx")
    experts = lax.axis_size("exp")
    capacity = max(2, top * length * 10 // (7 * experts))
    room = (capacity + 1 + 15) // 16 * 16
    slots = experts * room
    seq_len = doc_ids.shape[2]
    hidden_units = expert_up.shape[2]
    buckets = position_bias.shape[1]
    me = lax.axis_index("ctx")

    wide = 4 * width
    pad = -(experts + 2) % 128
    packed = jnp.concatenate(
        [
            query_key_value_weight,
            output_projection_weight,
            router,
            attn_gain[:, None],
            expert_gain[:, None],
            jnp.zeros((router.shape[0], pad), bf16),
        ],
        axis=1,
    )
    packed = gather_rows(packed)
    qkv_all = packed[:, : 3 * width]
    proj_all = packed[:, 3 * width : wide]
    router_all = packed[:, wide : wide + experts]
    gains = packed[:, wide + experts : wide + experts + 2].astype(f32)
    attn_scale = gains[:, 0]
    expert_scale = gains[:, 1]
    up_all = pair_rows(expert_up[0], 0)
    down_all = pair_rows(expert_down[0], 0)

    distance = jnp.arange(2 * TILE, dtype=jnp.int32)
    hot_bucket = (
        bucket_of(distance)[None, :] == jnp.arange(buckets, dtype=jnp.int32)[:, None]
    ).astype(f32)
    by_distance = jnp.sum(
        position_bias.astype(f32)[:, :, None] * hot_bucket[None], axis=1
    ) - position_bias.astype(f32)[:, buckets - 1 :]
    close = jnp.where(distance < TILE, by_distance, MASKED)
    beside = jnp.roll(by_distance, -TILE, axis=1)
    bias_rows = jnp.stack([close, beside], axis=1).reshape(PAIRS, 4, 2 * TILE)

    def norm_stats(values):
        return lax.rsqrt(jnp.mean(values * values, axis=-1, keepdims=True) + epsilon)

    earlier = jnp.tril(jnp.ones((length, length), bf16), -1)
    state = []
    for b in range(batches):
        rows = inputs[b, 0].astype(f32)
        inv_one = norm_stats(rows)
        normed = (rows * inv_one * attn_scale).astype(bf16)
        qkv = mm(normed, qkv_all, ((1,), (0,))).astype(bf16)
        own_kv = qkv[:, width:]
        docs = doc_ids[b, 0].astype(f32)
        padded = jnp.concatenate([jnp.full((BACK,), -1.0, f32), docs])
        key_docs = lax.dynamic_slice_in_dim(padded, me * length, BACK + length)
        query_docs = key_docs[BACK:]
        if ways == 2:
            kv_back = lax.ppermute(own_kv, "ctx", [(0, 1)])
        else:
            every = lax.all_gather(own_kv, "ctx", axis=0, tiled=True)
            every = jnp.concatenate([jnp.zeros((BACK, 2 * width), bf16), every], axis=0)
            kv_back = lax.dynamic_slice_in_dim(every, me * length, BACK, 0)
        firsts = query_docs[::TILE]
        start = jnp.sum((key_docs[None, :] < firsts[:, None]).astype(jnp.int32), axis=1)
        tiles = jnp.arange(length // TILE, dtype=jnp.int32) + SPAN - start // TILE
        tiles = jnp.clip(tiles, 1, SPAN)
        view = (tiles, qkv, kv_back, query_docs[None], key_docs[None], bias_rows)
        attended, lse = attend(*view)
        hidden = rows + mm(attended, proj_all, ((1,), (0,)))
        inv_two = norm_stats(hidden)
        shared = (hidden * inv_two * expert_scale).astype(bf16)
        logits = mm(shared, router_all, ((1,), (0,)))
        route_ids = routes[b, 0]
        hot = route_ids[:, :, None] == jnp.arange(experts, dtype=jnp.int32)[None, None, :]
        chosen = jnp.sum(jnp.where(hot, logits[:, None, :], 0.0), axis=2)
        gate_exp = jnp.exp(chosen - jnp.max(chosen, axis=1, keepdims=True))
        gates = gate_exp / jnp.sum(gate_exp, axis=1, keepdims=True)
        used = jnp.any(hot, axis=1)
        rank = mm(earlier, used.astype(bf16), ((1,), (0,))).astype(jnp.int32)
        slot = jnp.sum(jnp.where(hot, rank[:, None, :], 0), axis=2) + route_ids * room
        slot_rows = jnp.arange(slots, dtype=jnp.int32)
        holds = [slot[None, :, k] == slot_rows[:, None] for k in range(top)]
        spread = functools.reduce(jnp.logical_or, holds).astype(bf16)
        picks = [(slot[:, k : k + 1] == slot_rows[None, :]).astype(bf16) for k in range(top)]

        cot = cotangent[b, 0]
        cot_sent = mm(spread, cot, ((1,), (0,))).astype(bf16).reshape(experts, room, width)
        cot_here = lax.all_to_all(cot_sent, "exp", split_axis=0, concat_axis=0, tiled=True)

        gate_slots = sum(
            jnp.sum(jnp.where(holds[k], gates[None, :, k], 0.0), axis=1) for k in range(top)
        ).reshape(experts, 1, room)
        gate_high = gate_slots.astype(bf16)
        gate_low = (gate_slots - gate_high.astype(f32)).astype(bf16)
        gate_row = jnp.concatenate(
            [gate_high, gate_low, jnp.zeros((experts, 1, width - 2 * room), bf16)], axis=2
        )
        sent = mm(spread, shared, ((1,), (0,))).astype(bf16).reshape(experts, room, width)
        at_gate = lax.broadcasted_iota(jnp.int32, (1, room, 1), 1) == capacity
        sent = jnp.where(at_gate, gate_row, sent)
        here = lax.all_to_all(sent, "exp", split_axis=0, concat_axis=0, tiled=True)
        state.append(
            dict(rows=rows, inv_one=inv_one, normed=normed, view=view, attended=attended, lse=lse,
                 hidden=hidden, inv_two=inv_two, shared=shared, gates=gates, hot=hot,
                 spread=spread, picks=picks, cot=cot, cot_here=cot_here, here=here)
        )

    grad_up = jnp.zeros((width, hidden_units), f32)
    grad_down = jnp.zeros((hidden_units, width), f32)
    for s in state:
        packet = s["here"]
        gate_row = packet[:, capacity, : 2 * room].astype(f32)
        gate = (gate_row[:, :room] + gate_row[:, room:])[:, :, None]
        real = lax.broadcasted_iota(jnp.int32, (1, room, 1), 1) < capacity
        gate = jnp.where(real, gate, 0.0).reshape(slots, 1)
        x = packet.reshape(slots, width)
        up = s["cot_here"].reshape(slots, width).astype(f32)
        pre = mm(x, up_all, ((1,), (0,)))
        act = jax.nn.gelu(pre).astype(bf16)
        result = (mm(act, down_all, ((1,), (0,))) * gate).astype(bf16)
        s["back"] = lax.all_to_all(
            result.reshape(experts, room, width), "exp", split_axis=0, concat_axis=0, tiled=True
        )
        result_grad = (up * gate).astype(bf16)
        act_grad = mm(result_grad, down_all, ((1,), (1,)))
        pre_grad = jax.vjp(jax.nn.gelu, pre)[1](act_grad)[0].astype(bf16)
        route_grad = mm(pre_grad, up_all, ((1,), (1,))).astype(bf16)
        s["grad_back"] = lax.all_to_all(
            route_grad.reshape(experts, room, width), "exp", split_axis=0, concat_axis=0, tiled=True
        )
        grad_down = grad_down + mm(act, result_grad, ((0,), (0,)))
        grad_up = grad_up + mm(x, pre_grad, ((0,), (0,)))
    up_share = send_half(grad_up, 0)[None]
    down_share = send_half(grad_down, 0)[None]

    outputs = []
    input_grads = []
    grad_qkv = jnp.zeros((width, 3 * width), f32)
    grad_proj = jnp.zeros((width, width), f32)
    grad_router = jnp.zeros((width, experts), f32)
    grad_attn = jnp.zeros((width,), f32)
    grad_expert = jnp.zeros((width,), f32)
    grad_near = jnp.zeros((PAIRS, 1, 2 * TILE), f32)
    for s in state:
        upstream = s["cot"].astype(f32)
        returned = s["back"].reshape(slots, width)
        picked = [mm(p, returned, ((1,), (0,))) for p in s["picks"]]
        outputs.append((s["hidden"] + functools.reduce(jnp.add, picked)).astype(bf16))
        scaled = jnp.stack([jnp.sum(p * upstream, axis=1) for p in picked], axis=1)
        chosen_grad = scaled - s["gates"] * jnp.sum(scaled, axis=1, keepdims=True)
        logit_grad = jnp.sum(jnp.where(s["hot"], chosen_grad[:, :, None], 0.0), axis=1).astype(bf16)
        every_pick = functools.reduce(jnp.add, s["picks"])
        shared_grad = mm(every_pick, s["grad_back"].reshape(slots, width), ((1,), (0,)))
        shared_grad = shared_grad + mm(logit_grad, router_all, ((1,), (1,)))
        grad_router = grad_router + mm(s["shared"], logit_grad, ((0,), (0,)))
        unit = s["hidden"] * s["inv_two"]
        grad_expert = grad_expert + jnp.sum(shared_grad * unit, axis=0)
        inner = shared_grad * expert_scale
        hidden_grad = upstream + s["inv_two"] * (
            inner - unit * jnp.mean(inner * unit, axis=1, keepdims=True)
        )
        branch_grad = hidden_grad.astype(bf16)
        grad_proj = grad_proj + mm(s["attended"], branch_grad, ((0,), (0,)))
        attended_grad = mm(branch_grad, proj_all, ((1,), (1,))).astype(bf16)
        dq, dk, dv, dkp, dvp, near = attend_back(
            *s["view"], s["attended"], attended_grad, s["lse"]
        )
        grad_near = grad_near + near
        back = jnp.concatenate([dkp, dvp], axis=1)
        own = jnp.concatenate([dk, dv], axis=1).astype(f32)
        if ways == 2:
            own = own + lax.ppermute(back, "ctx", [(1, 0)]).astype(f32)
        else:
            every = jnp.zeros((BACK + seq_len, 2 * width), bf16)
            every = lax.dynamic_update_slice_in_dim(every, back, me * length, 0)
            own = own + lax.psum_scatter(
                every[BACK:], "ctx", scatter_dimension=0, tiled=True
            ).astype(f32)
        qkv_grad = jnp.concatenate([dq, own.astype(bf16)], axis=1)
        grad_qkv = grad_qkv + mm(s["normed"], qkv_grad, ((0,), (0,)))
        normed_grad = mm(qkv_grad, qkv_all, ((1,), (1,)))
        unit = s["rows"] * s["inv_one"]
        grad_attn = grad_attn + jnp.sum(normed_grad * unit, axis=0)
        inner = normed_grad * attn_scale
        input_part = s["inv_one"] * (inner - unit * jnp.mean(inner * unit, axis=1, keepdims=True))
        input_grads.append((hidden_grad + input_part).astype(bf16))

    by_distance = grad_near.reshape(HEADS, TILE)
    hot_near = jnp.where(
        jnp.arange(buckets)[:, None] < buckets - 1, hot_bucket[:, :TILE], 0.0
    )
    grad_bias = jnp.sum(by_distance[:, None, :] * hot_near[None], axis=2)
    far = jnp.where(jnp.arange(buckets) == buckets - 1, 1.0, 0.0)
    grad_bias = grad_bias - jnp.sum(grad_bias, axis=1, keepdims=True) * far
    bias_total = lax.psum(grad_bias, ("ctx", "exp"))
    total = scatter_sum(
        jnp.concatenate(
            [
                grad_qkv,
                grad_proj,
                grad_router,
                grad_attn[:, None],
                grad_expert[:, None],
                jnp.zeros((width, pad), f32),
            ],
            axis=1,
        )
    )
    return (
        jnp.stack(outputs)[:, None],
        jnp.stack(input_grads)[:, None],
        total[:, : 3 * width],
        total[:, 3 * width : wide],
        total[:, wide : wide + experts],
        total[:, wide + experts],
        total[:, wide + experts + 1],
        bias_total,
        up_share,
        down_share,
    )


def solution(mesh):
    placed = (
        P(None, "exp", "ctx", None),
        P(None, "exp", "ctx", None),
        P(None, "exp", None),
        P(None, "exp", "ctx", None),
        P(("ctx", "exp"), None),
        P(("ctx", "exp"), None),
        P(("ctx", "exp"), None),
        P(("ctx", "exp")),
        P(("ctx", "exp")),
        P(),
        P("exp", "ctx", None),
        P("exp", "ctx", None),
    )
    return jax.shard_map(
        shards,
        mesh=mesh,
        in_specs=placed,
        out_specs=(
            P(None, "exp", "ctx", None),
            P(None, "exp", "ctx", None),
            P(("ctx", "exp"), None),
            P(("ctx", "exp"), None),
            P(("ctx", "exp"), None),
            P(("ctx", "exp")),
            P(("ctx", "exp")),
            P(),
            P("exp", "ctx", None),
            P("exp", "ctx", None),
        ),
        check_vma=False,
    )
```

time: 1890 us -> 862 us (0.46)
  local copies, waits for them, and re-layouts: 533 us -> 45.8 us
  matrix products: 642 us -> 268 us
  waiting for transfers between devices: 260 us -> 166 us
  other arithmetic: 147 us -> 58.7 us
  Pallas kernels: 0 us -> 80.1 us
  blocking collectives: 192 us -> 130 us
  starting transfers between devices: 70.4 us -> 103 us
    dot_general x90 -> x42, matrix products: 642 us -> 268 us  [mm(): return lax.dot_general(a, b, (dims, ((), ())), preferred_element_type=f32)]
    dot_general x16 -> x0, local copies, waits for them, and re-layouts: 283 us -> none  [score_block(): jnp.einsum('vs,smj->vmj', position_bias, one_hot_routes, preferred_elemen...]
    reduce_scatter x6 -> x0, waiting for transfers between devices: 145 us -> none  [the longest x1 125 us: shards(): lax.psum_scatter(grad_qkv, ('ctx', 'exp'), scatter_dimension=0, tiled=True)]
    all_gather x1 -> x0, blocking collectives: 106 us -> none  [shards(): lax.all_gather(router, ('ctx', 'exp'), axis=0, tiled=True)]
    unnamed x2 -> x0, blocking collectives: 86.2 us -> none
    pallas_call x0 -> x4, Pallas kernels: none -> 80.1 us  [the longest x2 46.2 us: attend_back(): pl.pallas_call(bwd_kernel, grid_spec=pltpu.PrefetchScalarGridSpec(num_sca...]
    convert_element_type x10 -> x3, local copies, waits for them, and re-layouts: 80.8 us -> 8.75 us  [send_half(): return mine + swap(theirs.astype(bf16), 'ctx', 1).astype(f32)]
    psum x0 -> x1, blocking collectives: none -> 65.5 us  [shards(): bias_total = lax.psum(grad_bias, ('ctx', 'exp'))]
  transfers between devices with their start and end apart: 20 -> 22, of which waited for: 8 -> 11; matrix products, arithmetic and copies ran while one was open for 47% -> 33% of each run, Pallas kernels for 0% -> 5%
where the time goes in v1:
time: 862 us; the launch traced here: 855 us
  matrix products  268 us (31%)
  waiting for transfers between devices  166 us (19%)
  blocking collectives  130 us (15%)
  starting transfers between devices  103 us (12%)
  Pallas kernels  80.1 us (9%)
  other arithmetic  58.7 us (7%)
  local copies, waits for them, and re-layouts  45.8 us (5%)
    dot_general x42, matrix products, mm(): return lax.dot_general(a, b, (dims, ((), ())), preferred_element_type=f32)  268 us
    psum x1, blocking collectives, shards(): bias_total = lax.psum(grad_bias, ('ctx', 'exp'))  65.5 us
    all_to_all x1, blocking collectives, shards(): here = lax.all_to_all(sent, 'exp', split_axis=0, concat_axis=0, tiled=True)  64.6 us
    ppermute x10, waiting for transfers between devices, swap(): return lax.ppermute(x, axis, [(i, i ^ bit) for i in range(size)])  55.4 us
    pallas_call x2, Pallas kernels, attend_back(): pl.pallas_call(bwd_kernel, grid_spec=pltpu.PrefetchScalarGridSpec(num_sca...  46.2 us
    pallas_call x2, Pallas kernels, attend(): pl.pallas_call(fwd_kernel, grid_spec=pltpu.PrefetchScalarGridSpec(num_sca...  33.9 us
    all_to_all x2, waiting for transfers between devices, shards(): lax.all_to_all(result.reshape(experts, room, width), 'exp', split_axis=0,...  31 us
    all_to_all x2, waiting for transfers between devices, shards(): lax.all_to_all(route_grad.reshape(experts, room, width), 'exp', split_axi...  30.9 us
  transfers between devices with their start and end apart: 22, of which 11 were waited for; matrix products, arithmetic and copies ran while one was open for 33% of the time, Pallas kernels for 5%

profile of v1, /device:TPU:0, one launch (start us, length us, event | category | flops | bytes accessed | tf_op | source)
XLA Modules:
  0.0 855.1 jit_solution(14233833305940928601)
XLA Ops:
  25.4 12.8 %collective-permute-done.2 = bf16[4,24,3200]{2,1,0:T(8,128)(2,1)S(1)} collective-permute-done((bf16[4,24,3200]{2,1,0:T(8,128)(2,1)S(1)}, bf16[4,24,3200]{2,1,0:T(8,128)(2,1)S(1)}, u32[]{:S(2)}, u32[]{:S(2)}) %collective-permute-start.2) | collective-permute-done | bytes 614432 | tf_op jit(solution)/shard_map/ppermute | solution.py:306
  40.6 24.5 %collective-permute-done.3 = bf16[8,24,3200]{2,1,0:T(8,128)(2,1)S(1)} collective-permute-done((bf16[8,24,3200]{2,1,0:T(8,128)(2,1)S(1)}, bf16[8,24,3200]{2,1,0:T(8,128)(2,1)S(1)}, u32[]{:S(2)}, u32[]{:S(2)}) %collective-permute-start.3) | collective-permute-done | bytes 1228832 | tf_op jit(solution)/shard_map/ppermute | solution.py:306
  95.0 17.0 %attend.3 = (bf16[512,768]{1,0:T(8,128)(2,1)S(1)}, f32[6,4,256]{2,1,0:T(4,128)S(1)}) custom-call(s32[4]{0:T(128)S(1)} %subtract_clamp_fusion.tiles, bf16[512,2304]{1,0:T(8,128)(2,1)S(1)} %copy-done.1, bf16[512,2304]{1,0:T(8,128)(2,1)S(1)} %copy-done.1, bf16[512,2304]{1,0:T(8,128)(2,1)S(1)} %copy-done.1, ...), custom_call_target="tpu_custom_call" | custom-call | flops 3221225472 | bytes 6291456 | tf_op jit(solution)/shard_map/attend/pallas_call | solution.py:226
  114.4 17.0 %attend.2 = (bf16[512,768]{1,0:T(8,128)(2,1)S(1)}, f32[6,4,256]{2,1,0:T(4,128)S(1)}) custom-call(s32[4]{0:T(128)S(1)} %subtract_clamp_fusion.1.tiles, bf16[512,2304]{1,0:T(8,128)(2,1)S(1)} %convolution_convert_fusion.1.q_ref.k_ref.v_ref, bf16[512,2304]{1,0:T(8,128)(2,1)S(1)} %convolution_convert_fusion.1.q_ref.k_ref.v_ref, ...), custom_call_target="tpu_custom_call" | custom-call | flops 3221225472 | bytes 6291456 | tf_op jit(solution)/shard_map/attend/pallas_call | solution.py:226
  152.3 64.6 %all_to_all.49 = bf16[16,96,768]{2,1,0:T(8,128)(2,1)} all-to-all(bf16[16,96,768]{2,1,0:T(8,128)(2,1)S(1)} %get-tuple-element.182), channel_id=1, replica_groups=mesh['ctx'=2,'exp'=16] {'exp'}, dimensions={0} | all-to-all | bytes 4718592 | tf_op jit(solution)/shard_map/all_to_all | solution.py:473
  238.7 30.4 %all-to-all-done.2 = bf16[16,96,768]{2,1,0:T(8,128)(2,1)} async-done(((bf16[16,96,768]{2,1,0:T(8,128)(2,1)}), bf16[16,96,768]{2,1,0:T(8,128)(2,1)}, u32[]{:S(2)}, u32[]{:S(2)}) %all-to-all-start.2) | async-done | bytes 2359328 | tf_op jit(solution)/shard_map/all_to_all | solution.py:473
  282.1 18.8 %multiply_convert_fusion.1 = (bf16[1536,3072]{1,0:T(8,128)(2,1)}, f32[1536,3072]{1,0:T(8,128)}) fusion(bf16[1536,768]{1,0:T(8,128)(2,1)} %bitcast.228, bf16[384,3072]{1,0:T(8,128)(2,1)} %get-tuple-element.141, bf16[384,3072]{1,0:T(8,128)(2,1)} %get-tuple-element.140), kind=kOutput, calls=%fused_computation.19 | convolution fusion | flops 7299661824 | bytes 35389440 | tf_op jit(solution)/shard_map/dot_general | solution.py:33
  301.1 13.9 %fusion.164 = f32[1536,3072]{1,0:T(8,128)} fusion(bf16[1536,768]{1,0:T(8,128)(2,1)} %bitcast.51, bf16[384,3072]{1,0:T(8,128)(2,1)} %get-tuple-element.141, bf16[384,3072]{1,0:T(8,128)(2,1)} %get-tuple-element.140), kind=kOutput, calls=%fused_computation.340 | convolution fusion | flops 7257194496 | bytes 25952256 | tf_op jit(solution)/shard_map/dot_general | solution.py:33
  315.0 16.3 %multiply_convert_fusion.2 = bf16[1536,768]{1,0:T(8,128)(2,1)} fusion(f32[1536]{0:T(1024)S(1)} %mul.452, bf16[1536,768]{1,0:T(8,128)(2,1)S(1)} %copy-done.61, bf16[1536,768]{1,0:T(8,128)(2,1)S(1)} %copy-done.57, f32[1536,3072]{1,0:T(8,128)} %fusion.164), kind=kOutput, calls=%fused_computation.37 | convolution fusion | flops 7302021120 | bytes 25958400 | tf_op jit(solution)/shard_map/dot_general | solution.py:33
  343.1 24.9 %fusion.6 = bf16[1536,3072]{1,0:T(8,128)(2,1)} fusion(f32[1536,3072]{1,0:T(8,128)} %get-tuple-element.189, bf16[1536,768]{1,0:T(8,128)(2,1)S(1)} %fusion.15, bf16[1536,768]{1,0:T(8,128)(2,1)S(1)} %copy-done.62, bf16[1536,768]{1,0:T(8,128)(2,1)S(1)} %copy-done.58), kind=kOutput, calls=%fused_computation.10 | convolution fusion | flops 7351566336 | bytes 35389440 | tf_op jit(solution)/shard_map/dot_general | solution.py:33
  368.1 18.5 %all-to-all-done.6 = bf16[16,96,768]{2,1,0:T(8,128)(2,1)} async-done(((bf16[16,96,768]{2,1,0:T(8,128)(2,1)}), bf16[16,96,768]{2,1,0:T(8,128)(2,1)}, u32[]{:S(2)}, u32[]{:S(2)}) %all-to-all-start.6) | async-done | bytes 2359328 | tf_op jit(solution)/shard_map/all_to_all | solution.py:460
  397.5 12.7 %convolution_convert_fusion.3 = bf16[1536,768]{1,0:T(8,128)(2,1)} fusion(bf16[1536,3072]{1,0:T(8,128)(2,1)} %fusion.6, bf16[384,3072]{1,0:T(8,128)(2,1)} %get-tuple-element.141, bf16[384,3072]{1,0:T(8,128)(2,1)} %get-tuple-element.140), kind=kOutput, calls=%fused_computation.42 | convolution fusion | flops 7258374144 | bytes 16515072 | tf_op jit(solution)/shard_map/dot_general | solution.py:33
  431.8 12.6 %all-to-all-done.3 = bf16[16,96,768]{2,1,0:T(8,128)(2,1)} async-done(((bf16[16,96,768]{2,1,0:T(8,128)(2,1)}), bf16[16,96,768]{2,1,0:T(8,128)(2,1)}, u32[]{:S(2)}, u32[]{:S(2)}) %all-to-all-start.3) | async-done | bytes 2359328 | tf_op jit(solution)/shard_map/all_to_all | solution.py:493
  459.2 24.9 %fusion.13 = bf16[1536,3072]{1,0:T(8,128)(2,1)} fusion(f32[1536,3072]{1,0:T(8,128)} %fusion.164, bf16[1536,768]{1,0:T(8,128)(2,1)S(1)} %fusion.14, bf16[1536,768]{1,0:T(8,128)(2,1)S(1)} %copy-done.64, bf16[1536,768]{1,0:T(8,128)(2,1)S(1)} %copy-done.60), kind=kOutput, calls=%fused_computation.17 | convolution fusion | flops 7351566336 | bytes 35389440 | tf_op jit(solution)/shard_map/dot_general | solution.py:33
  484.1 18.3 %all-to-all-done.1 = bf16[16,96,768]{2,1,0:T(8,128)(2,1)} async-done(((bf16[16,96,768]{2,1,0:T(8,128)(2,1)}), bf16[16,96,768]{2,1,0:T(8,128)(2,1)}, u32[]{:S(2)}, u32[]{:S(2)}) %all-to-all-start.1) | async-done | bytes 2359328 | tf_op jit(solution)/shard_map/all_to_all | solution.py:493
  513.3 12.7 %convolution_convert_fusion.2 = bf16[1536,768]{1,0:T(8,128)(2,1)} fusion(bf16[1536,3072]{1,0:T(8,128)(2,1)} %fusion.13, bf16[384,3072]{1,0:T(8,128)(2,1)} %get-tuple-element.141, bf16[384,3072]{1,0:T(8,128)(2,1)} %get-tuple-element.140), kind=kOutput, calls=%fused_computation.41 | convolution fusion | flops 7258374144 | bytes 16515072 | tf_op jit(solution)/shard_map/dot_general | solution.py:33
  525.9 17.9 %convolution_add_fusion.1 = f32[3072,768]{1,0:T(8,128)} fusion(f32[3072,768]{1,0:T(8,128)} %fusion.172, bf16[1536,768]{1,0:T(8,128)(2,1)S(1)} %copy-done.52, f32[1536,3072]{1,0:T(8,128)} %fusion.164), kind=kOutput, calls=%fused_computation.21 | convolution fusion | flops 7292583936 | bytes 40108032 | tf_op jit(solution)/shard_map/dot_general | solution.py:33
  543.8 16.5 %all-to-all-done.5 = bf16[16,96,768]{2,1,0:T(8,128)(2,1)} async-done(((bf16[16,96,768]{2,1,0:T(8,128)(2,1)}), bf16[16,96,768]{2,1,0:T(8,128)(2,1)}, u32[]{:S(2)}, u32[]{:S(2)}) %all-to-all-start.5) | async-done | bytes 2359328 | tf_op jit(solution)/shard_map/all_to_all | solution.py:500
  571.5 13.0 %fusion.171 = f32[768,3072]{1,0:T(8,128)} fusion(bf16[1536,768]{1,0:T(8,128)(2,1)} %bitcast.229, bf16[1536,3072]{1,0:T(8,128)(2,1)} %fusion.6), kind=kOutput, calls=%fused_computation.347 | convolution fusion | flops 7247757312 | bytes 21233664 | tf_op jit(solution)/shard_map/dot_general | solution.py:33
  604.1 14.3 %all-to-all-done.7 = bf16[16,96,768]{2,1,0:T(8,128)(2,1)} async-done(((bf16[16,96,768]{2,1,0:T(8,128)(2,1)}), bf16[16,96,768]{2,1,0:T(8,128)(2,1)}, u32[]{:S(2)}, u32[]{:S(2)}) %all-to-all-start.7) | async-done | bytes 2359328 | tf_op jit(solution)/shard_map/all_to_all | solution.py:500
  632.4 23.0 %attend_back.3 = (bf16[512,768]{1,0:T(8,128)(2,1)S(1)}, bf16[512,768]{1,0:T(8,128)(2,1)S(1)}, bf16[512,768]{1,0:T(8,128)(2,1)S(1)}, bf16[512,768]{1,0:T(8,128)(2...) custom-call(s32[4]{0:T(128)S(1)} %subtract_clamp_fusion.tiles, bf16[512,2304]{1,0:T(8,128)(2,1)S(1)} %copy-done.2, ...), custom_call_target="tpu_custom_call" | custom-call | flops 8053063680 | bytes 12582912 | tf_op jit(solution)/shard_map/attend_back/pallas_call | solution.py:264
  658.9 23.2 %attend_back.2 = (bf16[512,768]{1,0:T(8,128)(2,1)S(1)}, bf16[512,768]{1,0:T(8,128)(2,1)S(1)}, bf16[512,768]{1,0:T(8,128)(2,1)S(1)}, bf16[512,768]{1,0:T(8,128)(2...) custom-call(s32[4]{0:T(128)S(1)} %copy-done.24, ...), custom_call_target="tpu_custom_call" | custom-call | flops 8053063680 | bytes 12582912 | tf_op jit(solution)/shard_map/attend_back/pallas_call | solution.py:264
  734.1 12.8 %convolution_add_fusion.2 = f32[768,3072]{1,0:T(8,128)S(1)} fusion(f32[768,3072]{1,0:T(8,128)} %fusion.171, bf16[1536,768]{1,0:T(8,128)(2,1)} %bitcast.51, bf16[1536,3072]{1,0:T(8,128)(2,1)} %fusion.13), kind=kOutput, calls=%fused_computation.22 | convolution fusion | flops 7250116608 | bytes 30670848 | tf_op jit(solution)/shard_map/dot_general | solution.py:33
  777.9 65.5 %psum.7 = f32[12,32]{1,0:T(8,128)} all-reduce(f32[12,32]{1,0:T(8,128)S(1)} %multiply_subtract_fusion), channel_id=1, replica_groups=mesh['ctx'=2,'exp'=16] {'ctx','exp'}, use_global_device_ids=true, to_apply=%region_38.39 | all-reduce | flops 384 | bytes 3072 | tf_op jit(solution)/shard_map/psum | solution.py:567
  (446 shorter events, 326.1 us)
Async XLA Ops:
  3.9 11.4 %collective-permute-start = (bf16[1,24,3200]{2,1,0:T(8,128)(2,1)S(1)}, bf16[1,24,3200]{2,1,0:T(8,128)(2,1)S(1)}, u32[]{:S(2)}, u32[]{:S(2)}) collective-permute-start(bf16[1,24,3200]{2,1,0:T(8,128)(2,1)S(1)} %bitcast.240), channel_id=1, source_target_pairs={{0,8},{1,9},{2,10},{3,11},{4,12},{5,13},{6,14},{7,15},{8,0},{9,1},... | collective-permute-start | bytes 460808 | tf_op jit(solution)/shard_map/ppermute | solution.py:306
  15.4 8.5 collective-permute-start.1
  24.1 14.2 %collective-permute-start.2 = (bf16[4,24,3200]{2,1,0:T(8,128)(2,1)S(1)}, bf16[4,24,3200]{2,1,0:T(8,128)(2,1)S(1)}, u32[]{:S(2)}, u32[]{:S(2)}) collective-permute-start(bf16[4,24,3200]{2,1,0:T(8,128)(2,1)S(1)} %bitcast.227), channel_id=1, source_target_pairs={{0,2},{1,3},{2,0},{3,1},{4,6},{5,7},{6,4},{7,5},{8,10},{9,11},{10,... | collective-permute-start | bytes 1843208 | tf_op jit(solution)/shard_map/ppermute | solution.py:306
  38.6 26.4 %collective-permute-start.3 = (bf16[8,24,3200]{2,1,0:T(8,128)(2,1)S(1)}, bf16[8,24,3200]{2,1,0:T(8,128)(2,1)S(1)}, u32[]{:S(2)}, u32[]{:S(2)}) collective-permute-start(bf16[8,24,3200]{2,1,0:T(8,128)(2,1)S(1)} %bitcast.226), channel_id=1, source_target_pairs={{0,1},{1,0},{2,3},{3,2},{4,5},{5,4},{6,7},{7,6},{8,9},{9,8},{10,11... | collective-permute-start | bytes 3686408 | tf_op jit(solution)/shard_map/ppermute | solution.py:306
  67.3 5.0 collective-permute-start.4
  83.7 9.6 %collective-permute-start.8 = (bf16[512,1536]{1,0:T(8,128)(2,1)}, bf16[512,1536]{1,0:T(8,128)(2,1)}, u32[]{:S(2)}, u32[]{:S(2)}) collective-permute-start(bf16[512,1536]{1,0:T(8,128)(2,1)} %slice.198), channel_id=1, source_target_pairs={{0,16},{1,17},{2,18},{3,19},{4,20},{5,21},{6,22},{7,23},{8,24},{9,... | collective-permute-start | bytes 4718600 | tf_op jit(solution)/shard_map/ppermute | solution.py:430
  90.4 24.0 %collective-permute-start.5 = (bf16[512,1536]{1,0:T(8,128)(2,1)}, bf16[512,1536]{1,0:T(8,128)(2,1)}, u32[]{:S(2)}, u32[]{:S(2)}) collective-permute-start(bf16[512,1536]{1,0:T(8,128)(2,1)} %slice.184), channel_id=1, source_target_pairs={{0,16},{1,17},{2,18},{3,19},{4,20},{5,21},{6,22},{7,23},{8,24},{9,... | collective-permute-start | bytes 4718600 | tf_op jit(solution)/shard_map/ppermute | solution.py:430
  93.1 539.2 %copy-start.19 = (f32[6,4,256]{2,1,0:T(4,128)}, f32[6,4,256]{2,1,0:T(4,128)S(1)}, u32[]{:S(2)}) copy-start(f32[6,4,256]{2,1,0:T(4,128)S(1)} %reshape.595.bv_ref) | copy-start | bytes 73732
  93.2 133.1 %copy-start.102 = (s32[512,1]{0,1:T(1,128)}, s32[512,1]{0,1:T(1,128)S(1)}, u32[]{:S(2)}) copy-start(s32[512,1]{0,1:T(1,128)S(1)} %get-tuple-element.176) | copy-start | bytes 6148
  216.9 52.3 %all-to-all-start.2 = ((bf16[16,96,768]{2,1,0:T(8,128)(2,1)}), bf16[16,96,768]{2,1,0:T(8,128)(2,1)}, u32[]{:S(2)}, u32[]{:S(2)}) async-start(bf16[16,96,768]{2,1,0:T(8,128)(2,1)} %get-tuple-element.183), calls=%async_computation.2 | async-start | bytes 4718592 | tf_op jit(solution)/shard_map/all_to_all | solution.py:473
  221.5 7.9 collective-permute-start.7
  221.7 12.0 %collective-permute-start.6 = (bf16[384,3072]{1,0:T(8,128)(2,1)}, bf16[384,3072]{1,0:T(8,128)(2,1)}, u32[]{:S(2)}, u32[]{:S(2)}) collective-permute-start(bf16[384,3072]{1,0:T(8,128)(2,1)} %bitcast.237), channel_id=1, source_target_pairs={{0,16},{16,0},{1,17},{17,1},{2,18},{18,2},{3,19},{19,3},{4,20},{20... | collective-permute-start | bytes 7077896 | tf_op jit(solution)/shard_map/ppermute | solution.py:306
  269.1 62.2 %all-to-all-start.4 = ((bf16[16,96,768]{2,1,0:T(8,128)(2,1)}), bf16[16,96,768]{2,1,0:T(8,128)(2,1)}, u32[]{:S(2)}, u32[]{:S(2)}) async-start(bf16[16,96,768]{2,1,0:T(8,128)(2,1)} %bitcast.232), calls=%async_computation.4 | async-start | bytes 4718592 | tf_op jit(solution)/shard_map/all_to_all | solution.py:460
  331.4 55.1 %all-to-all-start.6 = ((bf16[16,96,768]{2,1,0:T(8,128)(2,1)}), bf16[16,96,768]{2,1,0:T(8,128)(2,1)}, u32[]{:S(2)}, u32[]{:S(2)}) async-start(bf16[16,96,768]{2,1,0:T(8,128)(2,1)} %bitcast.230), calls=%async_computation.6 | async-start | bytes 4718592 | tf_op jit(solution)/shard_map/all_to_all | solution.py:460
  386.5 57.9 %all-to-all-start.3 = ((bf16[16,96,768]{2,1,0:T(8,128)(2,1)}), bf16[16,96,768]{2,1,0:T(8,128)(2,1)}, u32[]{:S(2)}, u32[]{:S(2)}) async-start(bf16[16,96,768]{2,1,0:T(8,128)(2,1)} %bitcast.234), calls=%async_computation.3 | async-start | bytes 4718592 | tf_op jit(solution)/shard_map/all_to_all | solution.py:493
  444.4 58.0 %all-to-all-start.1 = ((bf16[16,96,768]{2,1,0:T(8,128)(2,1)}), bf16[16,96,768]{2,1,0:T(8,128)(2,1)}, u32[]{:S(2)}, u32[]{:S(2)}) async-start(bf16[16,96,768]{2,1,0:T(8,128)(2,1)} %bitcast.235), calls=%async_computation.1 | async-start | bytes 4718592 | tf_op jit(solution)/shard_map/all_to_all | solution.py:493
  502.4 57.9 %all-to-all-start.5 = ((bf16[16,96,768]{2,1,0:T(8,128)(2,1)}), bf16[16,96,768]{2,1,0:T(8,128)(2,1)}, u32[]{:S(2)}, u32[]{:S(2)}) async-start(bf16[16,96,768]{2,1,0:T(8,128)(2,1)} %bitcast.233), calls=%async_computation.5 | async-start | bytes 4718592 | tf_op jit(solution)/shard_map/all_to_all | solution.py:500
  560.3 58.1 %all-to-all-start.7 = ((bf16[16,96,768]{2,1,0:T(8,128)(2,1)}), bf16[16,96,768]{2,1,0:T(8,128)(2,1)}, u32[]{:S(2)}, u32[]{:S(2)}) async-start(bf16[16,96,768]{2,1,0:T(8,128)(2,1)} %bitcast.231), calls=%async_computation.7 | async-start | bytes 4718592 | tf_op jit(solution)/shard_map/all_to_all | solution.py:500
  657.5 32.5 %collective-permute-start.10 = (bf16[512,1536]{1,0:T(8,128)(2,1)}, bf16[512,1536]{1,0:T(8,128)(2,1)}, u32[]{:S(2)}, u32[]{:S(2)}) collective-permute-start(bf16[512,1536]{1,0:T(8,128)(2,1)} %pad_maximum_fusion.7), channel_id=1, source_target_pairs={{16,0},{17,1},{18,2},{19,3},{20,4},{21,5},{22,6},{23,7},{24,8},{25... | collective-permute-start | bytes 4718600 | tf_op jit(solution)/shard_map/ppermute | solution.py:544
  683.4 15.2 %collective-permute-start.9 = (bf16[512,1536]{1,0:T(8,128)(2,1)}, bf16[512,1536]{1,0:T(8,128)(2,1)}, u32[]{:S(2)}, u32[]{:S(2)}) collective-permute-start(bf16[512,1536]{1,0:T(8,128)(2,1)} %pad_maximum_fusion.6), channel_id=1, source_target_pairs={{16,0},{17,1},{18,2},{19,3},{20,4},{21,5},{22,6},{23,7},{24,8},{25... | collective-permute-start | bytes 4718600 | tf_op jit(solution)/shard_map/ppermute | solution.py:544
  725.4 24.0 %collective-permute-start.11 = (bf16[384,3200]{1,0:T(8,128)(2,1)}, bf16[384,3200]{1,0:T(8,128)(2,1)}, u32[]{:S(2)}, u32[]{:S(2)}) collective-permute-start(bf16[384,3200]{1,0:T(8,128)(2,1)} %dynamic-slice_convert_fusion), channel_id=1, source_target_pairs={{0,16},{16,0},{1,17},{17,1},{2,18},{18,2},{3,19},{19,3},{4,20},{20... | collective-permute-start | bytes 7372808 | tf_op jit(solution)/shard_map/ppermute | solution.py:306
  734.0 31.7 %collective-permute-start.13 = (bf16[1536,768]{1,0:T(8,128)(2,1)S(1)}, bf16[1536,768]{1,0:T(8,128)(2,1)}, u32[]{:S(2)}, u32[]{:S(2)}) collective-permute-start(bf16[1536,768]{1,0:T(8,128)(2,1)S(1)} %dynamic-slice_convert_fusion.1), channel_id=1, source_target_pairs={{0,16},{16,0},{1,17},{17,1},{2,18},{18,2},{3,19},{19,3},{4,20},{20... | collective-permute-start | bytes 7077896 | tf_op jit(solution)/shard_map/ppermute | solution.py:306
  748.8 22.9 %collective-permute-start.12 = (bf16[384,3072]{1,0:T(8,128)(2,1)}, bf16[384,3072]{1,0:T(8,128)(2,1)}, u32[]{:S(2)}, u32[]{:S(2)}) collective-permute-start(bf16[384,3072]{1,0:T(8,128)(2,1)} %dynamic-slice_convert_fusion.2), channel_id=1, source_target_pairs={{0,16},{16,0},{1,17},{17,1},{2,18},{18,2},{3,19},{19,3},{4,20},{20... | collective-permute-start | bytes 7077896 | tf_op jit(solution)/shard_map/ppermute | solution.py:306
  754.5 95.4 %all-to-all-start.8 = ((bf16[16,24,3200]{2,1,0:T(8,128)(2,1)}), bf16[16,24,3200]{2,1,0:T(8,128)(2,1)}, u32[]{:S(2)}, u32[]{:S(2)}) async-start(bf16[16,24,3200]{2,1,0:T(8,128)(2,1)} %bitcast.210), calls=%async_computation.8 | async-start | bytes 4915200 | tf_op jit(solution)/shard_map/all_to_all | solution.py:348
  (115 other events, 1715.1 us)

commit v2 on v1

--- a/solution.py
+++ b/solution.py
@@ -1,4 +1,5 @@
 import functools
+import math
 
 import jax
 import jax.numpy as jnp
@@ -123,7 +124,7 @@
 
 
 def bwd_kernel(tiles, q_ref, k_ref, v_ref, kp_ref, vp_ref, qd_ref, kd_ref, bv_ref, o_ref, do_ref,
-               lse_ref, dq_ref, dk_ref, dv_ref, dkp_ref, dvp_ref, near_ref,
+               lse_ref, dq_ref, own_ref, back_ref, near_ref,
                kwin, kwin_t, vwin, dk, dv, near, bias, mask):
     @pl.when(pl.program_id(0) == 0)
     def _():
@@ -189,10 +190,9 @@
         return carry
 
     lax.fori_loop(0, q_ref.shape[0] // TILE, step, 0)
-    dkp_ref[...] = dk[:BACK].astype(bf16)
-    dk_ref[...] = dk[BACK:].astype(bf16)
-    dvp_ref[...] = dv[:BACK].astype(bf16)
-    dv_ref[...] = dv[BACK:].astype(bf16)
+    for i, total in enumerate((dk, dv)):
+        back_ref[i] = total[:BACK].astype(bf16)
+        own_ref[i] = total[BACK:].astype(bf16)
     for head in range(2):
         at = slice(head * TILE, (head + 1) * TILE)
         turned = near[:, at]
@@ -209,8 +209,8 @@
     lanes = lambda off: (lambda p, *_: (0, p + off))
     return [
         pl.BlockSpec((length, TILE), lanes(0)),
+        pl.BlockSpec((length, TILE), lanes(0)),
         pl.BlockSpec((length, TILE), lanes(PAIRS)),
-        pl.BlockSpec((length, TILE), lanes(2 * PAIRS)),
         pl.BlockSpec((BACK, TILE), lanes(0)),
         pl.BlockSpec((BACK, TILE), lanes(PAIRS)),
         pl.BlockSpec((1, length), full),
@@ -219,8 +219,8 @@
     ]
 
 
-def attend(tiles, qkv, kv_back, query_docs, key_docs, bias_rows):
-    length = qkv.shape[0]
+def attend(tiles, queries, kv, kv_back, query_docs, key_docs, bias_rows):
+    length = queries.shape[0]
     width = HEADS * HEAD
     blocks = length // TILE
     return pl.pallas_call(
@@ -250,17 +250,15 @@
             transcendentals=HEADS * length * BACK,
         ),
         name="attend",
-    )(tiles, qkv, qkv, qkv, kv_back, kv_back, query_docs, key_docs, bias_rows)
-
-
-def attend_back(tiles, qkv, kv_back, query_docs, key_docs, bias_rows, out, out_grad, lse):
-    length = qkv.shape[0]
+    )(tiles, queries, kv, kv, kv_back, kv_back, query_docs, key_docs, bias_rows)
+
+
+def attend_back(tiles, queries, kv, kv_back, query_docs, key_docs, bias_rows, out, out_grad, lse):
+    length = queries.shape[0]
     width = HEADS * HEAD
     blocks = length // TILE
     own = pl.BlockSpec((length, TILE), lambda p, *_: (0, p))
-    back = pl.BlockSpec((BACK, TILE), lambda p, *_: (0, p))
-    rows = jax.ShapeDtypeStruct((length, width), bf16)
-    back_rows = jax.ShapeDtypeStruct((BACK, width), bf16)
+    both = lambda n: pl.BlockSpec((2, n, TILE), lambda p, *_: (0, 0, p))
     return pl.pallas_call(
         bwd_kernel,
         grid_spec=pltpu.PrefetchScalarGridSpec(
@@ -268,7 +266,7 @@
             grid=(PAIRS,),
             in_specs=attention_specs(length)
             + [own, own, pl.BlockSpec((1, blocks, 2 * TILE), lambda p, *_: (p, 0, 0))],
-            out_specs=[own, own, own, back, back,
+            out_specs=[own, both(length), both(BACK),
                        pl.BlockSpec((1, 1, 2 * TILE), lambda p, *_: (p, 0, 0))],
             scratch_shapes=[
                 pltpu.VMEM((BACK + length, TILE), bf16),
@@ -281,24 +279,139 @@
                 pltpu.VMEM((blocks, SPAN * TILE, TILE), f32),
             ],
         ),
-        out_shape=[rows, rows, rows, back_rows, back_rows,
-                   jax.ShapeDtypeStruct((PAIRS, 1, 2 * TILE), f32)],
+        out_shape=[
+            jax.ShapeDtypeStruct((length, width), bf16),
+            jax.ShapeDtypeStruct((2, length, width), bf16),
+            jax.ShapeDtypeStruct((2, BACK, width), bf16),
+            jax.ShapeDtypeStruct((PAIRS, 1, 2 * TILE), f32),
+        ],
         compiler_params=pltpu.CompilerParams(vmem_limit_bytes=32 * 2**20),
         cost_estimate=pl.CostEstimate(
             flops=10 * 2 * HEADS * length * BACK * 128, bytes_accessed=12 * 2**20,
             transcendentals=HEADS * length * BACK,
         ),
         name="attend_back",
-    )(tiles, qkv, qkv, qkv, kv_back, kv_back, query_docs, key_docs, bias_rows, out, out_grad, lse)
-
-
-def is_power(n):
-    return n & (n - 1) == 0
-
-
-def rounds_of(size):
-    bits = [1 << b for b in range(size.bit_length() - 1)]
-    return bits[::-1]
+    )(tiles, queries, kv, kv, kv_back, kv_back, query_docs, key_docs, bias_rows, out, out_grad, lse)
+
+
+GELU_A = 0.7978845608028654
+GELU_B = 0.044715
+
+
+def expert_kernel(more, capacity, room, chunk, x_ref, cot_ref, up_ref, down_ref, *refs):
+    if more:
+        up_before, down_before, *refs = refs
+    out_ref, du_ref, dd_ref, y_sum, back_sum, x, result_grad, gate, act_all, pre_grad_all = refs
+    rows, width = x.shape
+    step = pl.program_id(0)
+
+    @pl.when(step == 0)
+    def _():
+        lane = lax.broadcasted_iota(jnp.int32, (1, TILE), 1)
+        for e in range(rows // room):
+            at = e * room
+            x[at : at + room, :] = x_ref[e]
+            line = x_ref[e, capacity : capacity + 1, : 2 * TILE].astype(f32)
+            line = jnp.where(lane < capacity, line[:, :TILE] + line[:, TILE:], 0.0)
+            column = jnp.broadcast_to(line, (TILE, TILE)).T[:room]
+            gate[at : at + room, :] = column
+            for c in range(0, width, TILE):
+                result_grad[at : at + room, c : c + TILE] = (
+                    cot_ref[e, :, c : c + TILE].astype(f32) * column
+                ).astype(bf16)
+        y_sum[...] = jnp.zeros_like(y_sum)
+        back_sum[...] = jnp.zeros_like(back_sum)
+
+    def part(i, carry):
+        r = pl.ds(pl.multiple_of(i * chunk, chunk), chunk)
+        pre = mm(x[r, :], up_ref[...], ((1,), (0,)))
+        act_grad = mm(result_grad[r, :], down_ref[...], ((1,), (1,)))
+        square = pre * pre
+        half = 0.5 + 0.5 * jnp.tanh(pre * (GELU_A + (GELU_A * GELU_B) * square))
+        act = (pre * half).astype(bf16)
+        slope = 2.0 * GELU_A + (6.0 * GELU_A * GELU_B) * square
+        pre_grad = (act_grad * (half * (1.0 + pre * (1.0 - half) * slope))).astype(bf16)
+        act_all[r, :] = act
+        pre_grad_all[r, :] = pre_grad
+        y_sum[r, :] += mm(act, down_ref[...], ((1,), (0,)))
+        back_sum[r, :] += mm(pre_grad, up_ref[...], ((1,), (1,)))
+        return carry
+
+    lax.fori_loop(0, rows // chunk, part, 0)
+    dd = mm(act_all[...], result_grad[...], ((0,), (0,)))
+    du = mm(x[...], pre_grad_all[...], ((0,), (0,)))
+    if more:
+        dd = dd + down_before[...]
+        du = du + up_before[...]
+    dd_ref[...] = dd
+    du_ref[...] = du
+
+    @pl.when(step == pl.num_programs(0) - 1)
+    def _():
+        for e in range(rows // room):
+            at = e * room
+            for c in range(0, width, TILE):
+                scaled = y_sum[at : at + room, c : c + TILE] * gate[at : at + room, :]
+                out_ref[e, :room, c : c + TILE] = scaled.astype(bf16)
+            out_ref[e, room:, :] = back_sum[at : at + room, :].astype(bf16)
+
+
+def run_experts(x, cot, batch, up, down, before, capacity):
+    sources, room, width = x.shape
+    rows = sources * room
+    hidden = up.shape[1]
+    part = math.gcd(hidden, 512)
+    chunk = rows // 2 if rows % 32 == 0 else rows
+    once = pl.Buffered(1)
+    columns = pl.BlockSpec((width, part), lambda t: (0, t))
+    lines = pl.BlockSpec((part, width), lambda t: (t, 0))
+    more = len(before) > 0
+    return pl.pallas_call(
+        functools.partial(expert_kernel, more, capacity, room, chunk),
+        grid=(hidden // part,),
+        in_specs=[
+            pl.BlockSpec((sources, room, width), lambda t: (0, 0, 0), pipeline_mode=once),
+            pl.BlockSpec((sources, room, width), lambda t: (0, batch, 0), pipeline_mode=once),
+            columns,
+            lines,
+        ]
+        + ([columns, lines] if more else []),
+        out_specs=[
+            pl.BlockSpec((sources, 2 * room, width), lambda t: (0, 0, 0), pipeline_mode=once),
+            columns,
+            lines,
+        ],
+        out_shape=[
+            jax.ShapeDtypeStruct((sources, 2 * room, width), bf16),
+            jax.ShapeDtypeStruct((width, hidden), f32),
+            jax.ShapeDtypeStruct((hidden, width), f32),
+        ],
+        scratch_shapes=[
+            pltpu.VMEM((rows, width), f32),
+            pltpu.VMEM((rows, width), f32),
+            pltpu.VMEM((rows, width), bf16),
+            pltpu.VMEM((rows, width), bf16),
+            pltpu.VMEM((rows, TILE), f32),
+            pltpu.VMEM((rows, part), bf16),
+            pltpu.VMEM((rows, part), bf16),
+        ],
+        input_output_aliases={4: 1, 5: 2} if more else {},
+        compiler_params=pltpu.CompilerParams(vmem_limit_bytes=60 * 2**20),
+        cost_estimate=pl.CostEstimate(
+            flops=12 * rows * width * hidden, bytes_accessed=40 * 2**20,
+            transcendentals=rows * hidden,
+        ),
+        name="experts",
+    )(x, cot, up, down, *before)
+
+
+def bits_of(axis):
+    return [1 << b for b in range(lax.axis_size(axis).bit_length() - 1)][::-1]
+
+
+def power_of_two(axis):
+    size = lax.axis_size(axis)
+    return size & (size - 1) == 0
 
 
 def swap(x, axis, bit):
@@ -306,29 +419,49 @@
     return lax.ppermute(x, axis, [(i, i ^ bit) for i in range(size)])
 
 
-def gather_rows(x):
-    if not (is_power(lax.axis_size("ctx")) and is_power(lax.axis_size("exp"))):
-        return lax.all_gather(x, ("ctx", "exp"), axis=0, tiled=True)
-    for axis in ("exp", "ctx"):
-        me = lax.axis_index(axis)
-        held = x[None]
-        for bit in rounds_of(lax.axis_size(axis)):
-            other = swap(held, axis, bit)
-            high = (me & bit) > 0
-            first, second = jnp.where(high, other, held), jnp.where(high, held, other)
-            held = jnp.stack([first, second], axis=1).reshape((-1,) + x.shape)
-        x = held.reshape((-1,) + x.shape[1:])
-    return x
+def ordered(x, other, axis, bit):
+    high = (lax.axis_index(axis) & bit) > 0
+    return jnp.where(high, other, x), jnp.where(high, x, other)
+
+
+def after(x, *others):
+    return lax.optimization_barrier((x, *others))[0]
+
+
+def gather_rows(left, right):
+    if not (power_of_two("ctx") and power_of_two("exp")):
+        return [lax.all_gather(x, ("ctx", "exp"), axis=0, tiled=True) for x in (left, right)]
+    bits = bits_of("exp")
+    last = bits[-2:]
+    parts = [left, right]
+    held = [x[None] for x in parts]
+    for bit in bits[:-2]:
+        got = [swap(h, "exp", bit) for h in held]
+        held = [
+            jnp.stack(ordered(h, g, "exp", bit), axis=1).reshape((-1,) + h.shape[1:])
+            for h, g in zip(held, got)
+        ]
+    got = [swap(h, "exp", bit) for h, bit in zip(held, last)]
+    held = [jnp.stack(ordered(h, g, "exp", bit), axis=1) for h, g, bit in zip(held, got, last)]
+    got = [swap(h, "exp", bit) for h, bit in zip(held, last[::-1])]
+    held = [
+        jnp.stack(ordered(h, g, "exp", bit), axis=at)
+        for h, g, bit, at in zip(held, got, last[::-1], (2, 1))
+    ]
+    held = [h.reshape(-1, h.shape[-1]) for h in held]
+    for bit in bits_of("ctx"):
+        got = [swap(h, "ctx", bit) for h in held]
+        held = [
+            jnp.stack(ordered(h, g, "ctx", bit), axis=0).reshape(-1, h.shape[-1])
+            for h, g in zip(held, got)
+        ]
+    return held
 
 
 def pair_rows(x, axis):
     if lax.axis_size("ctx") != 2:
         return lax.all_gather(x, "ctx", axis=axis, tiled=True)
-    other = swap(x, "ctx", 1)
-    high = lax.axis_index("ctx") > 0
-    return jnp.concatenate(
-        [jnp.where(high, other, x), jnp.where(high, x, other)], axis=axis
-    )
+    return jnp.concatenate(ordered(x, swap(x, "ctx", 1), "ctx", 1), axis=axis)
 
 
 def send_half(x, axis):
@@ -342,11 +475,37 @@
     return mine + swap(theirs.astype(bf16), "ctx", 1).astype(f32)
 
 
-def scatter_sum(x):
-    x = send_half(x, 0)
-    ways = lax.axis_size("exp")
-    parts = lax.all_to_all(x.astype(bf16), "exp", split_axis=0, concat_axis=0, tiled=True)
-    return jnp.sum(parts.reshape(ways, -1, x.shape[1]).astype(f32), axis=0)
+def halve(x, axis, bit, dim):
+    side = ((lax.axis_index(axis) & bit) > 0).astype(jnp.int32)
+    mine = lax.dynamic_index_in_dim(x, side, dim, keepdims=False)
+    theirs = lax.dynamic_index_in_dim(x, 1 - side, dim, keepdims=False)
+    return mine + swap(theirs.astype(bf16), axis, bit).astype(f32)
+
+
+def scatter_sum(left, right):
+    if not (power_of_two("exp") and lax.axis_size("ctx") == 2 and lax.axis_size("exp") > 3):
+        return [
+            lax.psum_scatter(x, ("ctx", "exp"), scatter_dimension=0, tiled=True)
+            for x in (left, right)
+        ]
+    bits = bits_of("exp")
+    held = [send_half(x, 0) for x in (left, right)]
+    held = [h.reshape((-1, 2, 2, h.shape[0] // lax.axis_size("exp"), h.shape[1])) for h in held]
+    high, low = bits[-2:]
+    held = [halve(held[0], "exp", high, 1), halve(held[1], "exp", low, 2)]
+    held = [halve(held[0], "exp", low, 1), halve(held[1], "exp", high, 1)]
+    for bit in bits[:-2][::-1]:
+        held = [halve(h.reshape((-1, 2) + h.shape[1:]), "exp", bit, 1) for h in held]
+    return [h.reshape(h.shape[-2:]) for h in held]
+
+
+def total_of(x):
+    if not (power_of_two("ctx") and power_of_two("exp")):
+        return lax.psum(x, ("ctx", "exp"))
+    for axis in ("ctx", "exp"):
+        for bit in bits_of(axis):
+            x = x + swap(x, axis, bit)
+    return x
 
 
 def shards(
@@ -373,32 +532,59 @@
     room = (capacity + 1 + 15) // 16 * 16
     slots = experts * room
     seq_len = doc_ids.shape[2]
-    hidden_units = expert_up.shape[2]
     buckets = position_bias.shape[1]
     me = lax.axis_index("ctx")
 
-    wide = 4 * width
+    expert_ids = jnp.arange(experts, dtype=jnp.int32)
+    slot_rows = jnp.arange(slots, dtype=jnp.int32)
+    earlier = jnp.tril(jnp.ones((length, length), bf16), -1)
+    hots, slot_of, holds, spreads = [], [], [], []
+    for b in range(batches):
+        route_ids = routes[b, 0]
+        hot = route_ids[:, :, None] == expert_ids[None, None, :]
+        used = jnp.any(hot, axis=1)
+        rank = mm(earlier, used.astype(bf16), ((1,), (0,))).astype(jnp.int32)
+        slot = jnp.sum(jnp.where(hot, rank[:, None, :], 0), axis=2) + route_ids * room
+        hold = [slot[None, :, k] == slot_rows[:, None] for k in range(top)]
+        hots.append(hot)
+        slot_of.append(slot)
+        holds.append(hold)
+        spreads.append(functools.reduce(jnp.logical_or, hold).astype(bf16))
+
+    def dispatch(b, rows):
+        sent = mm(spreads[b], rows, ((1,), (0,))).astype(bf16)
+        return sent.reshape(experts, room, width)
+
+    def cross(x):
+        return lax.all_to_all(x, "exp", split_axis=0, concat_axis=0, tiled=True)
+
     pad = -(experts + 2) % 128
-    packed = jnp.concatenate(
-        [
-            query_key_value_weight,
-            output_projection_weight,
-            router,
-            attn_gain[:, None],
-            expert_gain[:, None],
-            jnp.zeros((router.shape[0], pad), bf16),
-        ],
-        axis=1,
+    left, right = gather_rows(
+        jnp.concatenate([query_key_value_weight[:, :width], output_projection_weight], axis=1),
+        jnp.concatenate(
+            [
+                query_key_value_weight[:, width:],
+                router,
+                attn_gain[:, None],
+                expert_gain[:, None],
+                jnp.zeros((router.shape[0], pad), bf16),
+            ],
+            axis=1,
+        ),
     )
-    packed = gather_rows(packed)
-    qkv_all = packed[:, : 3 * width]
-    proj_all = packed[:, 3 * width : wide]
-    router_all = packed[:, wide : wide + experts]
-    gains = packed[:, wide + experts : wide + experts + 2].astype(f32)
+    query_weight = left[:, :width]
+    proj_weight = left[:, width:]
+    kv_weight = right[:, : 2 * width]
+    router_all = right[:, 2 * width : 2 * width + experts]
+    gains = right[:, 2 * width + experts : 2 * width + experts + 2].astype(f32)
     attn_scale = gains[:, 0]
     expert_scale = gains[:, 1]
     up_all = pair_rows(expert_up[0], 0)
     down_all = pair_rows(expert_down[0], 0)
+
+    cots = [cotangent[b, 0] for b in range(batches)]
+    sent = jnp.concatenate([dispatch(b, cots[b]) for b in range(batches)], axis=1)
+    cot_here = cross(after(sent, left, right))
 
     distance = jnp.arange(2 * TILE, dtype=jnp.int32)
     hot_bucket = (
@@ -414,178 +600,142 @@
     def norm_stats(values):
         return lax.rsqrt(jnp.mean(values * values, axis=-1, keepdims=True) + epsilon)
 
-    earlier = jnp.tril(jnp.ones((length, length), bf16), -1)
     state = []
     for b in range(batches):
         rows = inputs[b, 0].astype(f32)
         inv_one = norm_stats(rows)
         normed = (rows * inv_one * attn_scale).astype(bf16)
-        qkv = mm(normed, qkv_all, ((1,), (0,))).astype(bf16)
-        own_kv = qkv[:, width:]
+        kv = mm(normed, kv_weight, ((1,), (0,))).astype(bf16)
+        queries = mm(normed, query_weight, ((1,), (0,))).astype(bf16)
         docs = doc_ids[b, 0].astype(f32)
         padded = jnp.concatenate([jnp.full((BACK,), -1.0, f32), docs])
         key_docs = lax.dynamic_slice_in_dim(padded, me * length, BACK + length)
         query_docs = key_docs[BACK:]
         if ways == 2:
-            kv_back = lax.ppermute(own_kv, "ctx", [(0, 1)])
+            kv_back = lax.ppermute(kv, "ctx", [(0, 1)])
         else:
-            every = lax.all_gather(own_kv, "ctx", axis=0, tiled=True)
+            every = lax.all_gather(kv, "ctx", axis=0, tiled=True)
             every = jnp.concatenate([jnp.zeros((BACK, 2 * width), bf16), every], axis=0)
             kv_back = lax.dynamic_slice_in_dim(every, me * length, BACK, 0)
         firsts = query_docs[::TILE]
         start = jnp.sum((key_docs[None, :] < firsts[:, None]).astype(jnp.int32), axis=1)
         tiles = jnp.arange(length // TILE, dtype=jnp.int32) + SPAN - start // TILE
         tiles = jnp.clip(tiles, 1, SPAN)
-        view = (tiles, qkv, kv_back, query_docs[None], key_docs[None], bias_rows)
-        attended, lse = attend(*view)
-        hidden = rows + mm(attended, proj_all, ((1,), (0,)))
+        view = (tiles, queries, kv, kv_back, query_docs[None], key_docs[None], bias_rows)
+        state.append(dict(rows=rows, inv_one=inv_one, normed=normed, view=view))
+
+    last = cot_here
+    for b, s in enumerate(state):
+        attended, lse = attend(*s["view"])
+        hidden = s["rows"] + mm(attended, proj_weight, ((1,), (0,)))
         inv_two = norm_stats(hidden)
         shared = (hidden * inv_two * expert_scale).astype(bf16)
         logits = mm(shared, router_all, ((1,), (0,)))
-        route_ids = routes[b, 0]
-        hot = route_ids[:, :, None] == jnp.arange(experts, dtype=jnp.int32)[None, None, :]
+        hot = hots[b]
         chosen = jnp.sum(jnp.where(hot, logits[:, None, :], 0.0), axis=2)
         gate_exp = jnp.exp(chosen - jnp.max(chosen, axis=1, keepdims=True))
         gates = gate_exp / jnp.sum(gate_exp, axis=1, keepdims=True)
-        used = jnp.any(hot, axis=1)
-        rank = mm(earlier, used.astype(bf16), ((1,), (0,))).astype(jnp.int32)
-        slot = jnp.sum(jnp.where(hot, rank[:, None, :], 0), axis=2) + route_ids * room
-        slot_rows = jnp.arange(slots, dtype=jnp.int32)
-        holds = [slot[None, :, k] == slot_rows[:, None] for k in range(top)]
-        spread = functools.reduce(jnp.logical_or, holds).astype(bf16)
-        picks = [(slot[:, k : k + 1] == slot_rows[None, :]).astype(bf16) for k in range(top)]
-
-        cot = cotangent[b, 0]
-        cot_sent = mm(spread, cot, ((1,), (0,))).astype(bf16).reshape(experts, room, width)
-        cot_here = lax.all_to_all(cot_sent, "exp", split_axis=0, concat_axis=0, tiled=True)
-
         gate_slots = sum(
-            jnp.sum(jnp.where(holds[k], gates[None, :, k], 0.0), axis=1) for k in range(top)
+            jnp.sum(jnp.where(holds[b][k], gates[None, :, k], 0.0), axis=1) for k in range(top)
         ).reshape(experts, 1, room)
+        gate_slots = jnp.pad(gate_slots, ((0, 0), (0, 0), (0, TILE - room)))
         gate_high = gate_slots.astype(bf16)
         gate_low = (gate_slots - gate_high.astype(f32)).astype(bf16)
         gate_row = jnp.concatenate(
-            [gate_high, gate_low, jnp.zeros((experts, 1, width - 2 * room), bf16)], axis=2
+            [gate_high, gate_low, jnp.zeros((experts, 1, width - 2 * TILE), bf16)], axis=2
         )
-        sent = mm(spread, shared, ((1,), (0,))).astype(bf16).reshape(experts, room, width)
         at_gate = lax.broadcasted_iota(jnp.int32, (1, room, 1), 1) == capacity
-        sent = jnp.where(at_gate, gate_row, sent)
-        here = lax.all_to_all(sent, "exp", split_axis=0, concat_axis=0, tiled=True)
-        state.append(
-            dict(rows=rows, inv_one=inv_one, normed=normed, view=view, attended=attended, lse=lse,
-                 hidden=hidden, inv_two=inv_two, shared=shared, gates=gates, hot=hot,
-                 spread=spread, picks=picks, cot=cot, cot_here=cot_here, here=here)
-        )
-
-    grad_up = jnp.zeros((width, hidden_units), f32)
-    grad_down = jnp.zeros((hidden_units, width), f32)
-    for s in state:
-        packet = s["here"]
-        gate_row = packet[:, capacity, : 2 * room].astype(f32)
-        gate = (gate_row[:, :room] + gate_row[:, room:])[:, :, None]
-        real = lax.broadcasted_iota(jnp.int32, (1, room, 1), 1) < capacity
-        gate = jnp.where(real, gate, 0.0).reshape(slots, 1)
-        x = packet.reshape(slots, width)
-        up = s["cot_here"].reshape(slots, width).astype(f32)
-        pre = mm(x, up_all, ((1,), (0,)))
-        act = jax.nn.gelu(pre).astype(bf16)
-        result = (mm(act, down_all, ((1,), (0,))) * gate).astype(bf16)
-        s["back"] = lax.all_to_all(
-            result.reshape(experts, room, width), "exp", split_axis=0, concat_axis=0, tiled=True
-        )
-        result_grad = (up * gate).astype(bf16)
-        act_grad = mm(result_grad, down_all, ((1,), (1,)))
-        pre_grad = jax.vjp(jax.nn.gelu, pre)[1](act_grad)[0].astype(bf16)
-        route_grad = mm(pre_grad, up_all, ((1,), (1,))).astype(bf16)
-        s["grad_back"] = lax.all_to_all(
-            route_grad.reshape(experts, room, width), "exp", split_axis=0, concat_axis=0, tiled=True
-        )
-        grad_down = grad_down + mm(act, result_grad, ((0,), (0,)))
-        grad_up = grad_up + mm(x, pre_grad, ((0,), (0,)))
+        sent = jnp.where(at_gate, gate_row, dispatch(b, shared))
+        s.update(attended=attended, lse=lse, hidden=hidden, inv_two=inv_two, shared=shared,
+                 gates=gates, here=cross(after(sent, last)))
+        last = s["here"]
+
+    grads = ()
+    for b, s in enumerate(state):
+        out, *grads = run_experts(s["here"], cot_here, b, up_all, down_all, grads, capacity)
+        s["back"] = cross(after(out, last))
+        last = s["back"]
+    grad_up, grad_down = grads
     up_share = send_half(grad_up, 0)[None]
     down_share = send_half(grad_down, 0)[None]
 
     outputs = []
     input_grads = []
-    grad_qkv = jnp.zeros((width, 3 * width), f32)
-    grad_proj = jnp.zeros((width, width), f32)
-    grad_router = jnp.zeros((width, experts), f32)
-    grad_attn = jnp.zeros((width,), f32)
-    grad_expert = jnp.zeros((width,), f32)
-    grad_near = jnp.zeros((PAIRS, 1, 2 * TILE), f32)
-    for s in state:
-        upstream = s["cot"].astype(f32)
-        returned = s["back"].reshape(slots, width)
-        picked = [mm(p, returned, ((1,), (0,))) for p in s["picks"]]
+    parts = []
+    for b, s in enumerate(state):
+        upstream = cots[b].astype(f32)
+        packet = after(s["back"], *input_grads)
+        returned = packet[:, :room].reshape(slots, width)
+        grad_rows = packet[:, room:].reshape(slots, width)
+        slot = slot_of[b]
+        picks = [(slot[:, k : k + 1] == slot_rows[None, :]).astype(bf16) for k in range(top)]
+        picked = [mm(p, returned, ((1,), (0,))) for p in picks]
         outputs.append((s["hidden"] + functools.reduce(jnp.add, picked)).astype(bf16))
         scaled = jnp.stack([jnp.sum(p * upstream, axis=1) for p in picked], axis=1)
         chosen_grad = scaled - s["gates"] * jnp.sum(scaled, axis=1, keepdims=True)
-        logit_grad = jnp.sum(jnp.where(s["hot"], chosen_grad[:, :, None], 0.0), axis=1).astype(bf16)
-        every_pick = functools.reduce(jnp.add, s["picks"])
-        shared_grad = mm(every_pick, s["grad_back"].reshape(slots, width), ((1,), (0,)))
+        logit_grad = jnp.sum(jnp.where(hots[b], chosen_grad[:, :, None], 0.0), axis=1).astype(bf16)
+        shared_grad = mm(functools.reduce(jnp.add, picks), grad_rows, ((1,), (0,)))
         shared_grad = shared_grad + mm(logit_grad, router_all, ((1,), (1,)))
-        grad_router = grad_router + mm(s["shared"], logit_grad, ((0,), (0,)))
+        grad_router = mm(s["shared"], logit_grad, ((0,), (0,)))
         unit = s["hidden"] * s["inv_two"]
-        grad_expert = grad_expert + jnp.sum(shared_grad * unit, axis=0)
+        grad_expert = jnp.sum(shared_grad * unit, axis=0)
         inner = shared_grad * expert_scale
         hidden_grad = upstream + s["inv_two"] * (
             inner - unit * jnp.mean(inner * unit, axis=1, keepdims=True)
         )
         branch_grad = hidden_grad.astype(bf16)
-        grad_proj = grad_proj + mm(s["attended"], branch_grad, ((0,), (0,)))
-        attended_grad = mm(branch_grad, proj_all, ((1,), (1,))).astype(bf16)
-        dq, dk, dv, dkp, dvp, near = attend_back(
-            *s["view"], s["attended"], attended_grad, s["lse"]
-        )
-        grad_near = grad_near + near
-        back = jnp.concatenate([dkp, dvp], axis=1)
-        own = jnp.concatenate([dk, dv], axis=1).astype(f32)
+        grad_proj = mm(s["attended"], branch_grad, ((0,), (0,)))
+        attended_grad = mm(branch_grad, proj_weight, ((1,), (1,))).astype(bf16)
+        dq, own, back, near = attend_back(*s["view"], s["attended"], attended_grad, s["lse"])
         if ways == 2:
-            own = own + lax.ppermute(back, "ctx", [(1, 0)]).astype(f32)
+            got = lax.ppermute(back, "ctx", [(1, 0)])
         else:
-            every = jnp.zeros((BACK + seq_len, 2 * width), bf16)
-            every = lax.dynamic_update_slice_in_dim(every, back, me * length, 0)
-            own = own + lax.psum_scatter(
-                every[BACK:], "ctx", scatter_dimension=0, tiled=True
-            ).astype(f32)
-        qkv_grad = jnp.concatenate([dq, own.astype(bf16)], axis=1)
-        grad_qkv = grad_qkv + mm(s["normed"], qkv_grad, ((0,), (0,)))
-        normed_grad = mm(qkv_grad, qkv_all, ((1,), (1,)))
+            every = jnp.zeros((2, BACK + seq_len, width), bf16)
+            every = lax.dynamic_update_slice_in_dim(every, back, me * length, 1)
+            got = lax.psum_scatter(every[:, BACK:], "ctx", scatter_dimension=1, tiled=True)
+        both = (own.astype(f32) + got.astype(f32)).astype(bf16)
+        dkv = jnp.concatenate([both[0], both[1]], axis=1)
+        normed = s["normed"]
+        grad_query = mm(normed, dq, ((0,), (0,)))
+        grad_kv = mm(normed, dkv, ((0,), (0,)))
+        normed_grad = mm(dq, query_weight, ((1,), (1,))) + mm(dkv, kv_weight, ((1,), (1,)))
         unit = s["rows"] * s["inv_one"]
-        grad_attn = grad_attn + jnp.sum(normed_grad * unit, axis=0)
+        grad_attn = jnp.sum(normed_grad * unit, axis=0)
         inner = normed_grad * attn_scale
         input_part = s["inv_one"] * (inner - unit * jnp.mean(inner * unit, axis=1, keepdims=True))
         input_grads.append((hidden_grad + input_part).astype(bf16))
-
-    by_distance = grad_near.reshape(HEADS, TILE)
+        parts.append((grad_query, grad_kv, grad_proj, grad_router, grad_attn, grad_expert, near))
+
+    grad_query, grad_kv, grad_proj, grad_router, grad_attn, grad_expert, near = (
+        functools.reduce(jnp.add, p) for p in zip(*parts)
+    )
     hot_near = jnp.where(
         jnp.arange(buckets)[:, None] < buckets - 1, hot_bucket[:, :TILE], 0.0
     )
-    grad_bias = jnp.sum(by_distance[:, None, :] * hot_near[None], axis=2)
+    grad_bias = jnp.sum(near.reshape(HEADS, 1, TILE) * hot_near[None], axis=2)
     far = jnp.where(jnp.arange(buckets) == buckets - 1, 1.0, 0.0)
-    grad_bias = grad_bias - jnp.sum(grad_bias, axis=1, keepdims=True) * far
-    bias_total = lax.psum(grad_bias, ("ctx", "exp"))
-    total = scatter_sum(
+    bias_total = total_of(grad_bias - jnp.sum(grad_bias, axis=1, keepdims=True) * far)
+    left, right = scatter_sum(
+        jnp.concatenate([grad_query, grad_proj], axis=1),
         jnp.concatenate(
             [
-                grad_qkv,
-                grad_proj,
+                grad_kv,
                 grad_router,
                 grad_attn[:, None],
                 grad_expert[:, None],
                 jnp.zeros((width, pad), f32),
             ],
             axis=1,
-        )
+        ),
     )
     return (
         jnp.stack(outputs)[:, None],
         jnp.stack(input_grads)[:, None],
-        total[:, : 3 * width],
-        total[:, 3 * width : wide],
-        total[:, wide : wide + experts],
-        total[:, wide + experts],
-        total[:, wide + experts + 1],
+        jnp.concatenate([left[:, :width], right[:, : 2 * width]], axis=1),
+        left[:, width:],
+        right[:, 2 * width : 2 * width + experts],
+        right[:, 2 * width + experts],
+        right[:, 2 * width + experts + 1],
         bias_total,
         up_share,
         down_share,

time: 862 us -> 700 us (0.81)
  matrix products: 268 us -> 62.3 us
  blocking collectives: 130 us -> 0 us
  Pallas kernels: 80.1 us -> 195 us
  starting transfers between devices: 103 us -> 132 us
  waiting for transfers between devices: 166 us -> 180 us
  local copies, waits for them, and re-layouts: 45.8 us -> 54.5 us
    dot_general x42 -> x36, matrix products: 268 us -> 62.3 us  [mm(): return lax.dot_general(a, b, (dims, ((), ())), preferred_element_type=f32)]
    pallas_call x0 -> x2, Pallas kernels: none -> 115 us  [run_experts(): pl.pallas_call(functools.partial(expert_kernel, more, capacity, room, chu...]
    psum x1 -> x0, blocking collectives: 65.5 us -> none  [shards(): bias_total = lax.psum(grad_bias, ('ctx', 'exp'))]
    all_to_all x1 -> x0, blocking collectives: 64.6 us -> none  [shards(): here = lax.all_to_all(sent, 'exp', split_axis=0, concat_axis=0, tiled=True)]
    ppermute x10 -> x29, starting transfers between devices: 14.6 us -> 44.5 us  [swap(): return lax.ppermute(x, axis, [(i, i ^ bit) for i in range(size)])]
    concatenate x2 -> x4, other arithmetic: 2.52 us -> 13 us  [the longest x2 7.37 us: pair_rows(): return jnp.concatenate(ordered(x, swap(x, 'ctx', 1), 'ctx', 1), axis=axis)]
    ppermute x10 -> x29, waiting for transfers between devices: 55.4 us -> 65.5 us  [swap(): return lax.ppermute(x, axis, [(i, i ^ bit) for i in range(size)])]
    all_to_all x8 -> x5, waiting for transfers between devices: 111 us -> 115 us  [cross(): return lax.all_to_all(x, 'exp', split_axis=0, concat_axis=0, tiled=True)]
  transfers between devices with their start and end apart: 22 -> 38, of which waited for: 11 -> 17; matrix products, arithmetic and copies ran while one was open for 33% -> 21% of each run, Pallas kernels for 5% -> 25%
where the time goes in v2:
time: 700 us; the launch traced here: 690 us
  Pallas kernels  195 us (28%)
  waiting for transfers between devices  180 us (26%)
  starting transfers between devices  132 us (19%)
  other arithmetic  63.1 us (9%)
  matrix products  62.3 us (9%)
  local copies, waits for them, and re-layouts  54.5 us (8%)
    pallas_call x2, Pallas kernels, run_experts(): pl.pallas_call(functools.partial(expert_kernel, more, capacity, room, chu...  115 us
    all_to_all x5, waiting for transfers between devices, cross(): return lax.all_to_all(x, 'exp', split_axis=0, concat_axis=0, tiled=True)  115 us
    all_to_all x5, starting transfers between devices, cross(): return lax.all_to_all(x, 'exp', split_axis=0, concat_axis=0, tiled=True)  79.2 us
    ppermute x29, waiting for transfers between devices, swap(): return lax.ppermute(x, axis, [(i, i ^ bit) for i in range(size)])  65.5 us
    dot_general x36, matrix products, mm(): return lax.dot_general(a, b, (dims, ((), ())), preferred_element_type=f32)  62.3 us
    pallas_call x2, Pallas kernels, attend_back(): pl.pallas_call(bwd_kernel, grid_spec=pltpu.PrefetchScalarGridSpec(num_sca...  45.9 us
    ppermute x29, starting transfers between devices, swap(): return lax.ppermute(x, axis, [(i, i ^ bit) for i in range(size)])  44.5 us
    pallas_call x2, Pallas kernels, attend(): pl.pallas_call(fwd_kernel, grid_spec=pltpu.PrefetchScalarGridSpec(num_sca...  33.6 us
  transfers between devices with their start and end apart: 38, of which 17 were waited for; matrix products, arithmetic and copies ran while one was open for 21% of the time, Pallas kernels for 25%

profile of v2, /device:TPU:0, one launch (start us, length us, event | category | flops | bytes accessed | tf_op | source)
XLA Modules:
  0.0 690.0 jit_solution(6781703746390962388)
XLA Ops:
  41.9 9.6 %collective-permute-done.8 = bf16[4,2,24,1536]{3,2,0,1:T(8,128)(2,1)S(1)} collective-permute-done((bf16[4,2,24,1536]{3,2,0,1:T(8,128)(2,1)S(1)}, bf16[4,2,24,1536]{3,2,0,1:T(8,128)(2,1)S(1)}, u32[]{:S(2)}, u32[]{:S(2)}) %collective-permute-start.8) | collective-permute-done | bytes 589856 | tf_op jit(solution)/shard_map/ppermute | solution.py:419
  64.6 6.9 all-to-all-start
  88.2 17.2 %attend.3 = (bf16[512,768]{1,0:T(8,128)(2,1)S(1)}, f32[6,4,256]{2,1,0:T(4,128)S(1)}) custom-call(s32[4]{0:T(128)S(1)} %subtract_clamp_fusion.tiles, bf16[512,768]{1,0:T(8,128)(2,1)S(1)} %convolution_convert_fusion.8.q_ref, bf16[512,1536]{1,0:T(8,128)(2,1)S(1)} %convolution_convert_fusion.4.k_ref.v_ref, ...), custom_call_target="tpu_custom_call" | custom-call | flops 3221225472 | bytes 6291456 | tf_op jit(solution)/shard_map/attend/pallas_call | solution.py:226
  105.4 16.4 %attend.2 = (bf16[512,768]{1,0:T(8,128)(2,1)S(1)}, f32[6,4,256]{2,1,0:T(4,128)S(1)}) custom-call(s32[4]{0:T(128)S(1)} %subtract_clamp_fusion.1.tiles, bf16[512,768]{1,0:T(8,128)(2,1)S(1)} %convolution_convert_fusion.9.q_ref, bf16[512,1536]{1,0:T(8,128)(2,1)} %convolution_convert_fusion.5.k_ref.v_ref, ...), custom_call_target="tpu_custom_call" | custom-call | flops 3221225472 | bytes 6291456 | tf_op jit(solution)/shard_map/attend/pallas_call | solution.py:226
  136.4 26.2 %all-to-all-done.cot_ref = bf16[16,192,768]{2,1,0:T(8,128)(2,1)} async-done(((bf16[16,192,768]{2,1,0:T(8,128)(2,1)}), bf16[16,192,768]{2,1,0:T(8,128)(2,1)}, u32[]{:S(2)}, u32[]{:S(2)}) %all-to-all-start) | async-done | bytes 4718624 | tf_op jit(solution)/shard_map/all_to_all | solution.py:559
  162.7 33.0 %all-to-all-start.1 = ((bf16[16,96,768]{2,1,0:T(8,128)(2,1)}), bf16[16,96,768]{2,1,0:T(8,128)(2,1)}, u32[]{:S(2)}, u32[]{:S(2)}) async-start(bf16[16,96,768]{2,1,0:T(8,128)(2,1)} %get-tuple-element.36), calls=%async_computation.1 | async-start | bytes 4718592 | tf_op jit(solution)/shard_map/all_to_all | solution.py:559
  203.5 39.4 %all-to-all-done.1.x_ref = bf16[16,96,768]{2,1,0:T(8,128)(2,1)} async-done(((bf16[16,96,768]{2,1,0:T(8,128)(2,1)}), bf16[16,96,768]{2,1,0:T(8,128)(2,1)}, u32[]{:S(2)}, u32[]{:S(2)}) %all-to-all-start.1) | async-done | bytes 2359328 | tf_op jit(solution)/shard_map/all_to_all | solution.py:559
  243.0 10.9 %all-to-all-start.2 = ((bf16[16,96,768]{2,1,0:T(8,128)(2,1)}), bf16[16,96,768]{2,1,0:T(8,128)(2,1)}, u32[]{:S(2)}, u32[]{:S(2)}) async-start(bf16[16,96,768]{2,1,0:T(8,128)(2,1)} %get-tuple-element.39), calls=%async_computation.2 | async-start | bytes 4718592 | tf_op jit(solution)/shard_map/all_to_all | solution.py:559
  258.7 57.1 %experts.2 = (bf16[16,192,768]{2,1,0:T(8,128)(2,1)}, f32[768,3072]{1,0:T(8,128)}, f32[3072,768]{1,0:T(8,128)}) custom-call(bf16[16,96,768]{2,1,0:T(8,128)(2,1)} %all-to-all-done.1.x_ref, bf16[16,192,768]{2,1,0:T(8,128)(2,1)} %all-to-all-done.cot_ref, bf16[768,3072]{1,0:T(8,128)(2,1)} %pad_maximum_fusion.1.up_ref, bf16[3072,768]{1,0:T(8,128)(2,1)} %pad_maximum_fusion.2.down_ref), custom_call_target="tpu_custom_call" | custom-call | flops 43486543872 | bytes 41943040 | tf_op jit(solution)/shard_map/experts/pallas_call | solution.py:369
  315.9 6.9 %all-to-all-start.3 = ((bf16[16,192,768]{2,1,0:T(8,128)(2,1)}), bf16[16,192,768]{2,1,0:T(8,128)(2,1)}, u32[]{:S(2)}, u32[]{:S(2)}) async-start(bf16[16,192,768]{2,1,0:T(8,128)(2,1)} %get-tuple-element.40), calls=%async_computation.3 | async-start | bytes 9437184 | tf_op jit(solution)/shard_map/all_to_all | solution.py:559
  322.8 58.1 %experts.3 = (bf16[16,192,768]{2,1,0:T(8,128)(2,1)}, f32[768,3072]{1,0:T(8,128)}, f32[3072,768]{1,0:T(8,128)}) custom-call(bf16[16,96,768]{2,1,0:T(8,128)(2,1)} %all-to-all-done.2.x_ref, bf16[16,192,768]{2,1,0:T(8,128)(2,1)} %all-to-all-done.cot_ref, bf16[768,3072]{1,0:T(8,128)(2,1)} %pad_maximum_fusion.1.up_ref, ...), custom_call_target="tpu_custom_call", output_to_operand_aliasing={{1}: (4, {}), {2}: (5, {})} | custom-call | flops 43486543872 | bytes 41943040 | tf_op jit(solution)/shard_map/experts/pallas_call | solution.py:369
  380.9 29.3 %all-to-all-done.3 = bf16[16,192,768]{2,1,0:T(8,128)(2,1)} async-done(((bf16[16,192,768]{2,1,0:T(8,128)(2,1)}), bf16[16,192,768]{2,1,0:T(8,128)(2,1)}, u32[]{:S(2)}, u32[]{:S(2)}) %all-to-all-start.3) | async-done | bytes 4718624 | tf_op jit(solution)/shard_map/all_to_all | solution.py:559
  410.2 21.5 %all-to-all-start.4 = ((bf16[16,192,768]{2,1,0:T(8,128)(2,1)}), bf16[16,192,768]{2,1,0:T(8,128)(2,1)}, u32[]{:S(2)}, u32[]{:S(2)}) async-start(bf16[16,192,768]{2,1,0:T(8,128)(2,1)} %get-tuple-element.44), calls=%async_computation.4 | async-start | bytes 9437184 | tf_op jit(solution)/shard_map/all_to_all | solution.py:559
  454.2 22.8 %attend_back.2 = (bf16[512,768]{1,0:T(8,128)(2,1)S(1)}, bf16[2,512,768]{2,1,0:T(8,128)(2,1)S(1)}, bf16[2,512,768]{2,1,0:T(8,128)(2,1)}, f32[6,1,256]{2,1,0:T(1,128)S(1)}) custom-call(s32[4]{0:T(128)S(1)} %subtract_clamp_fusion.1.tiles, bf16[512,768]{1,0:T(8,128)(2,1)S(1)} %copy-done.18, bf16[512,1536]{1,0:T(8,128)(2,1)} %convolution_convert_fusion.5.k_ref.v_ref, ...), custom_call_target="tpu_custom_call" | custom-call | flops 8053063680 | bytes 12582912 | tf_op jit(solution)/shard_map/attend_back/pallas_call | solution.py:262
  478.5 5.7 add_bitcast_fusion
  484.2 6.2 add_bitcast_fusion.1
  499.4 19.9 %all-to-all-done.4 = bf16[16,192,768]{2,1,0:T(8,128)(2,1)} async-done(((bf16[16,192,768]{2,1,0:T(8,128)(2,1)}), bf16[16,192,768]{2,1,0:T(8,128)(2,1)}, u32[]{:S(2)}, u32[]{:S(2)}) %all-to-all-start.4) | async-done | bytes 4718624 | tf_op jit(solution)/shard_map/all_to_all | solution.py:559
  535.9 23.1 %attend_back.3 = (bf16[512,768]{1,0:T(8,128)(2,1)S(1)}, bf16[2,512,768]{2,1,0:T(8,128)(2,1)S(1)}, bf16[2,512,768]{2,1,0:T(8,128)(2,1)S(1)}, f32[6,1,256]{2,1,0:T(1,128)S(1)}) custom-call(s32[4]{0:T(128)S(1)} %copy-done.14, bf16[512,768]{1,0:T(8,128)(2,1)S(1)} %copy-done.16, bf16[512,1536]{1,0:T(8,128)(2,1)S(1)} %copy-done.10, ...), custom_call_target="tpu_custom_call" | custom-call | flops 8053063680 | bytes 12582912 | tf_op jit(solution)/shard_map/attend_back/pallas_call | solution.py:262
  569.1 17.4 %collective-permute-start.27 = (f32[12,32]{1,0:T(8,128)S(1)}, f32[12,32]{1,0:T(8,128)S(1)}, u32[]{:S(2)}, u32[]{:S(2)}) collective-permute-start(f32[12,32]{1,0:T(8,128)S(1)} %fusion.198), channel_id=1, source_target_pairs={{0,8},{1,9},{2,10},{3,11},{4,12},{5,13},{6,14},{7,15},{8,0},{9,1},... | collective-permute-start | bytes 4616 | tf_op jit(solution)/shard_map/ppermute | solution.py:419
  629.6 6.5 concatenate.67
  646.2 7.4 %collective-permute-done.18 = bf16[4,24,1536]{2,1,0:T(8,128)(2,1)S(1)} collective-permute-done((bf16[4,24,1536]{2,1,0:T(8,128)(2,1)S(1)}, bf16[4,24,1536]{2,1,0:T(8,128)(2,1)S(1)}, u32[]{:S(2)}, u32[]{:S(2)}) %collective-permute-start.18) | collective-permute-done | bytes 294944 | tf_op jit(solution)/shard_map/ppermute | solution.py:419
  653.8 13.1 %collective-permute-done.22 = bf16[4,2,24,1664]{3,2,0,1:T(8,128)(2,1)S(1)} collective-permute-done((bf16[4,2,24,1664]{3,2,0,1:T(8,128)(2,1)S(1)}, bf16[4,2,24,1664]{3,2,0,1:T(8,128)(2,1)S(1)}, u32[]{:S(2)}, u32[]{:S(2)}) %collective-permute-start.22) | collective-permute-done | bytes 639008 | tf_op jit(solution)/shard_map/ppermute | solution.py:419
  667.7 8.5 %collective-permute-done.23 = bf16[4,24,1664]{2,1,0:T(8,128)(2,1)S(1)} collective-permute-done((bf16[4,24,1664]{2,1,0:T(8,128)(2,1)S(1)}, bf16[4,24,1664]{2,1,0:T(8,128)(2,1)S(1)}, u32[]{:S(2)}, u32[]{:S(2)}) %collective-permute-start.23) | collective-permute-done | bytes 319520 | tf_op jit(solution)/shard_map/ppermute | solution.py:419
  676.5 5.2 collective-permute-done.24
  (447 shorter events, 218.8 us)
Async XLA Ops:
  3.9 17.5 %collective-permute-start = (bf16[1,24,1664]{2,1,0:T(8,128)(2,1)S(1)}, bf16[1,24,1664]{2,1,0:T(8,128)(2,1)S(1)}, u32[]{:S(2)}, u32[]{:S(2)}) collective-permute-start(bf16[1,24,1664]{2,1,0:T(8,128)(2,1)S(1)} %bitcast.306), channel_id=1, source_target_pairs={{0,8},{1,9},{2,10},{3,11},{4,12},{5,13},{6,14},{7,15},{8,0},{9,1},... | collective-permute-start | bytes 239624 | tf_op jit(solution)/shard_map/ppermute | solution.py:419
  9.6 9.8 %collective-permute-start.5 = (bf16[1,24,1536]{2,1,0:T(8,128)(2,1)S(1)}, bf16[1,24,1536]{2,1,0:T(8,128)(2,1)S(1)}, u32[]{:S(2)}, u32[]{:S(2)}) collective-permute-start(bf16[1,24,1536]{2,1,0:T(8,128)(2,1)S(1)} %maximum_bitcast_fusion.4), channel_id=1, source_target_pairs={{0,8},{1,9},{2,10},{3,11},{4,12},{5,13},{6,14},{7,15},{8,0},{9,1},... | collective-permute-start | bytes 221192 | tf_op jit(solution)/shard_map/ppermute | solution.py:419
  9.6 186.2 %collective-permute-start.11 = (bf16[384,3072]{1,0:T(8,128)(2,1)}, bf16[384,3072]{1,0:T(8,128)(2,1)}, u32[]{:S(2)}, u32[]{:S(2)}) collective-permute-start(bf16[384,3072]{1,0:T(8,128)(2,1)} %bitcast.288), channel_id=1, source_target_pairs={{0,16},{16,0},{1,17},{17,1},{2,18},{18,2},{3,19},{19,3},{4,20},{20... | collective-permute-start | bytes 7077896 | tf_op jit(solution)/shard_map/ppermute | solution.py:419
  29.4 10.5 %collective-permute-start.2 = (bf16[4,24,1664]{2,1,0:T(8,128)(2,1)S(1)}, bf16[4,24,1664]{2,1,0:T(8,128)(2,1)S(1)}, u32[]{:S(2)}, u32[]{:S(2)}) collective-permute-start(bf16[4,24,1664]{2,1,0:T(8,128)(2,1)S(1)} %bitcast.304), channel_id=1, source_target_pairs={{0,1},{1,0},{2,3},{3,2},{4,5},{5,4},{6,7},{7,6},{8,9},{9,8},{10,11... | collective-permute-start | bytes 958472 | tf_op jit(solution)/shard_map/ppermute | solution.py:419
  34.9 16.5 %collective-permute-start.8 = (bf16[4,2,24,1536]{3,2,0,1:T(8,128)(2,1)S(1)}, bf16[4,2,24,1536]{3,2,0,1:T(8,128)(2,1)S(1)}, u32[]{:S(2)}, u32[]{:S(2)}) collective-permute-start(bf16[4,2,24,1536]{3,2,0,1:T(8,128)(2,1)S(1)} %pad_maximum_fusion.14), channel_id=1, source_target_pairs={{0,1},{1,0},{2,3},{3,2},{4,5},{5,4},{6,7},{7,6},{8,9},{9,8},{10,11... | collective-permute-start | bytes 1769480 | tf_op jit(solution)/shard_map/ppermute | solution.py:419
  40.1 14.2 %collective-permute-start.3 = (bf16[4,2,24,1664]{3,2,0,1:T(8,128)(2,1)S(1)}, bf16[4,2,24,1664]{3,2,0,1:T(8,128)(2,1)S(1)}, u32[]{:S(2)}, u32[]{:S(2)}) collective-permute-start(bf16[4,2,24,1664]{3,2,0,1:T(8,128)(2,1)S(1)} %pad_maximum_fusion.13), channel_id=1, source_target_pairs={{0,2},{1,3},{2,0},{3,1},{4,6},{5,7},{6,4},{7,5},{8,10},{9,11},{10,... | collective-permute-start | bytes 1916936 | tf_op jit(solution)/shard_map/ppermute | solution.py:419
  64.6 98.1 %all-to-all-start = ((bf16[16,192,768]{2,1,0:T(8,128)(2,1)}), bf16[16,192,768]{2,1,0:T(8,128)(2,1)}, u32[]{:S(2)}, u32[]{:S(2)}) async-start(bf16[16,192,768]{2,1,0:T(8,128)(2,1)} %pad_maximum_fusion), calls=%async_computation | async-start | bytes 9437184 | tf_op jit(solution)/shard_map/all_to_all | solution.py:559
  75.5 12.7 %collective-permute-start.13 = (bf16[512,1536]{1,0:T(8,128)(2,1)S(1)}, bf16[512,1536]{1,0:T(8,128)(2,1)}, u32[]{:S(2)}, u32[]{:S(2)}) collective-permute-start(bf16[512,1536]{1,0:T(8,128)(2,1)S(1)} %convolution_convert_fusion.4.k_ref.v_ref), channel_id=1, source_target_pairs={{0,16},{1,17},{2,18},{3,19},{4,20},{5,21},{6,22},{7,23},{8,24},{9,... | collective-permute-start | bytes 4718600 | tf_op jit(solution)/shard_map/ppermute | solution.py:615
  81.4 24.0 %collective-permute-start.10 = (bf16[512,1536]{1,0:T(8,128)(2,1)}, bf16[512,1536]{1,0:T(8,128)(2,1)}, u32[]{:S(2)}, u32[]{:S(2)}) collective-permute-start(bf16[512,1536]{1,0:T(8,128)(2,1)} %convolution_convert_fusion.5.k_ref.v_ref), channel_id=1, source_target_pairs={{0,16},{1,17},{2,18},{3,19},{4,20},{5,21},{6,22},{7,23},{8,24},{9,... | collective-permute-start | bytes 4718600 | tf_op jit(solution)/shard_map/ppermute | solution.py:615
  162.7 80.3 %all-to-all-start.1 = ((bf16[16,96,768]{2,1,0:T(8,128)(2,1)}), bf16[16,96,768]{2,1,0:T(8,128)(2,1)}, u32[]{:S(2)}, u32[]{:S(2)}) async-start(bf16[16,96,768]{2,1,0:T(8,128)(2,1)} %get-tuple-element.36), calls=%async_computation.1 | async-start | bytes 4718592 | tf_op jit(solution)/shard_map/all_to_all | solution.py:559
  243.0 72.9 %all-to-all-start.2 = ((bf16[16,96,768]{2,1,0:T(8,128)(2,1)}), bf16[16,96,768]{2,1,0:T(8,128)(2,1)}, u32[]{:S(2)}, u32[]{:S(2)}) async-start(bf16[16,96,768]{2,1,0:T(8,128)(2,1)} %get-tuple-element.39), calls=%async_computation.2 | async-start | bytes 4718592 | tf_op jit(solution)/shard_map/all_to_all | solution.py:559
  315.9 94.3 %all-to-all-start.3 = ((bf16[16,192,768]{2,1,0:T(8,128)(2,1)}), bf16[16,192,768]{2,1,0:T(8,128)(2,1)}, u32[]{:S(2)}, u32[]{:S(2)}) async-start(bf16[16,192,768]{2,1,0:T(8,128)(2,1)} %get-tuple-element.40), calls=%async_computation.3 | async-start | bytes 9437184 | tf_op jit(solution)/shard_map/all_to_all | solution.py:559
  410.2 109.1 %all-to-all-start.4 = ((bf16[16,192,768]{2,1,0:T(8,128)(2,1)}), bf16[16,192,768]{2,1,0:T(8,128)(2,1)}, u32[]{:S(2)}, u32[]{:S(2)}) async-start(bf16[16,192,768]{2,1,0:T(8,128)(2,1)} %get-tuple-element.44), calls=%async_computation.4 | async-start | bytes 9437184 | tf_op jit(solution)/shard_map/all_to_all | solution.py:559
  435.8 42.7 %collective-permute-start.32 = (bf16[1536,768]{1,0:T(8,128)(2,1)}, bf16[1536,768]{1,0:T(8,128)(2,1)}, u32[]{:S(2)}, u32[]{:S(2)}) collective-permute-start(bf16[1536,768]{1,0:T(8,128)(2,1)} %dynamic-slice_convert_fusion), channel_id=1, source_target_pairs={{0,16},{16,0},{1,17},{17,1},{2,18},{18,2},{3,19},{19,3},{4,20},{20... | collective-permute-start | bytes 7077896 | tf_op jit(solution)/shard_map/ppermute | solution.py:419
  439.9 44.3 %collective-permute-start.31 = (bf16[384,3072]{1,0:T(8,128)(2,1)}, bf16[384,3072]{1,0:T(8,128)(2,1)}, u32[]{:S(2)}, u32[]{:S(2)}) collective-permute-start(bf16[384,3072]{1,0:T(8,128)(2,1)} %dynamic-slice_convert_fusion.1), channel_id=1, source_target_pairs={{0,16},{16,0},{1,17},{17,1},{2,18},{18,2},{3,19},{19,3},{4,20},{20... | collective-permute-start | bytes 7077896 | tf_op jit(solution)/shard_map/ppermute | solution.py:419
  477.0 13.4 %collective-permute-start.14 = (bf16[2,512,768]{2,1,0:T(8,128)(2,1)}, bf16[2,512,768]{2,1,0:T(8,128)(2,1)}, u32[]{:S(2)}, u32[]{:S(2)}) collective-permute-start(bf16[2,512,768]{2,1,0:T(8,128)(2,1)} %get-tuple-element.48), channel_id=1, source_target_pairs={{16,0},{17,1},{18,2},{19,3},{20,4},{21,5},{22,6},{23,7},{24,8},{25... | collective-permute-start | bytes 4718600 | tf_op jit(solution)/shard_map/ppermute | solution.py:691
  569.0 35.7 %collective-permute-start.16 = (bf16[384,1536]{0,1:T(8,128)(2,1)}, bf16[384,1536]{0,1:T(8,128)(2,1)}, u32[]{:S(2)}, u32[]{:S(2)}) collective-permute-start(bf16[384,1536]{0,1:T(8,128)(2,1)} %fusion.23), channel_id=1, source_target_pairs={{0,16},{16,0},{1,17},{17,1},{2,18},{18,2},{3,19},{19,3},{4,20},{20... | collective-permute-start | bytes 3538952 | tf_op jit(solution)/shard_map/ppermute | solution.py:419
  569.1 19.1 %collective-permute-start.27 = (f32[12,32]{1,0:T(8,128)S(1)}, f32[12,32]{1,0:T(8,128)S(1)}, u32[]{:S(2)}, u32[]{:S(2)}) collective-permute-start(f32[12,32]{1,0:T(8,128)S(1)} %fusion.198), channel_id=1, source_target_pairs={{0,8},{1,9},{2,10},{3,11},{4,12},{5,13},{6,14},{7,15},{8,0},{9,1},... | collective-permute-start | bytes 4616 | tf_op jit(solution)/shard_map/ppermute | solution.py:419
  586.7 29.0 %collective-permute-start.15 = (bf16[2,512,768]{2,1,0:T(8,128)(2,1)S(1)}, bf16[2,512,768]{2,1,0:T(8,128)(2,1)}, u32[]{:S(2)}, u32[]{:S(2)}) collective-permute-start(bf16[2,512,768]{2,1,0:T(8,128)(2,1)S(1)} %copy-done.12), channel_id=1, source_target_pairs={{16,0},{17,1},{18,2},{19,3},{20,4},{21,5},{22,6},{23,7},{24,8},{25... | collective-permute-start | bytes 4718600 | tf_op jit(solution)/shard_map/ppermute | solution.py:691
  613.7 27.8 %collective-permute-start.17 = (bf16[4,2,24,1536]{3,2,1,0:T(8,128)(2,1)}, bf16[4,2,24,1536]{3,2,1,0:T(8,128)(2,1)}, u32[]{:S(2)}, u32[]{:S(2)}) collective-permute-start(bf16[4,2,24,1536]{3,2,1,0:T(8,128)(2,1)} %fusion.94), channel_id=1, source_target_pairs={{0,2},{1,3},{2,0},{3,1},{4,6},{5,7},{6,4},{7,5},{8,10},{9,11},{10,... | collective-permute-start | bytes 1769480 | tf_op jit(solution)/shard_map/ppermute | solution.py:419
  643.7 9.9 %collective-permute-start.18 = (bf16[4,24,1536]{2,1,0:T(8,128)(2,1)S(1)}, bf16[4,24,1536]{2,1,0:T(8,128)(2,1)S(1)}, u32[]{:S(2)}, u32[]{:S(2)}) collective-permute-start(bf16[4,24,1536]{2,1,0:T(8,128)(2,1)S(1)} %fusion.105), channel_id=1, source_target_pairs={{0,1},{1,0},{2,3},{3,2},{4,5},{5,4},{6,7},{7,6},{8,9},{9,8},{10,11... | collective-permute-start | bytes 884744 | tf_op jit(solution)/shard_map/ppermute | solution.py:419
  644.7 22.2 %collective-permute-start.22 = (bf16[4,2,24,1664]{3,2,0,1:T(8,128)(2,1)S(1)}, bf16[4,2,24,1664]{3,2,0,1:T(8,128)(2,1)S(1)}, u32[]{:S(2)}, u32[]{:S(2)}) collective-permute-start(bf16[4,2,24,1664]{3,2,0,1:T(8,128)(2,1)S(1)} %fusion.93), channel_id=1, source_target_pairs={{0,1},{1,0},{2,3},{3,2},{4,5},{5,4},{6,7},{7,6},{8,9},{9,8},{10,11... | collective-permute-start | bytes 1916936 | tf_op jit(solution)/shard_map/ppermute | solution.py:419
  653.7 13.4 %collective-permute-start.19 = (bf16[2,24,1536]{2,1,0:T(8,128)(2,1)S(1)}, bf16[2,24,1536]{2,1,0:T(8,128)(2,1)S(1)}, u32[]{:S(2)}, u32[]{:S(2)}) collective-permute-start(bf16[2,24,1536]{2,1,0:T(8,128)(2,1)S(1)} %fusion.111), channel_id=1, source_target_pairs={{0,4},{1,5},{2,6},{3,7},{4,0},{5,1},{6,2},{7,3},{8,12},{9,13},{10,... | collective-permute-start | bytes 442376 | tf_op jit(solution)/shard_map/ppermute | solution.py:419
  667.2 9.2 %collective-permute-start.20 = (bf16[1,24,1536]{2,1,0:T(8,128)(2,1)S(1)}, bf16[1,24,1536]{2,1,0:T(8,128)(2,1)S(1)}, u32[]{:S(2)}, u32[]{:S(2)}) collective-permute-start(bf16[1,24,1536]{2,1,0:T(8,128)(2,1)S(1)} %dynamic-slice_convert_fusion.9), channel_id=1, source_target_pairs={{0,8},{1,9},{2,10},{3,11},{4,12},{5,13},{6,14},{7,15},{8,0},{9,1},... | collective-permute-start | bytes 221192 | tf_op jit(solution)/shard_map/ppermute | solution.py:419
  (102 other events, 1007.1 us)

commit v3 on v2

--- a/solution.py
+++ b/solution.py
@@ -298,19 +298,29 @@
 GELU_B = 0.044715
 
 
-def expert_kernel(more, capacity, room, chunk, x_ref, cot_ref, up_ref, down_ref, *refs):
+def expert_kernel(more, halves, split, capacity, room, chunk, ctx, x_ref, cot_ref, up_ref, down_ref, *refs):
+    refs = list(refs)
+    take = lambda n: [refs.pop(0) for _ in range(n)]
     if more:
-        up_before, down_before, *refs = refs
-    out_ref, du_ref, dd_ref, y_sum, back_sum, x, result_grad, gate, act_all, pre_grad_all = refs
+        _, up_before, down_before = take(3)
+    y_ref, back_ref = take(2)
+    sums = take(4 if split else 2)
+    y_sum, back_sum, x, result_grad, gate, act_all, pre_grad_all = take(7)
     rows, width = x.shape
     step = pl.program_id(0)
+    pieces = 2 if halves else 1
+    piece = width // pieces
+
+    def columns(i):
+        return pl.ds(pl.multiple_of((ctx[0] + i) % pieces * piece, TILE), piece)
 
     @pl.when(step == 0)
     def _():
         lane = lax.broadcasted_iota(jnp.int32, (1, TILE), 1)
         for e in range(rows // room):
             at = e * room
-            x[at : at + room, :] = x_ref[e]
+            for i in range(pieces):
+                x[at : at + room, i * piece : (i + 1) * piece] = x_ref[e, :, columns(i)]
             line = x_ref[e, capacity : capacity + 1, : 2 * TILE].astype(f32)
             line = jnp.where(lane < capacity, line[:, :TILE] + line[:, TILE:], 0.0)
             column = jnp.broadcast_to(line, (TILE, TILE)).T[:room]
@@ -338,71 +348,117 @@
         return carry
 
     lax.fori_loop(0, rows // chunk, part, 0)
-    dd = mm(act_all[...], result_grad[...], ((0,), (0,)))
-    du = mm(x[...], pre_grad_all[...], ((0,), (0,)))
-    if more:
-        dd = dd + down_before[...]
-        du = du + up_before[...]
-    dd_ref[...] = dd
-    du_ref[...] = du
+
+    def up_grad():
+        grad = mm(x[...], pre_grad_all[...], ((0,), (0,)))
+        return grad + up_before[...] if more else grad
+
+    def down_grad():
+        grad = mm(act_all[...], result_grad[...], ((0,), (0,)))
+        return grad + down_before[...] if more else grad
+
+    if split:
+        mine, theirs, down_mine, down_theirs = sums
+        early = step < pl.num_programs(0) // 2
+
+        @pl.when(early)
+        def _():
+            down_mine[...] = down_grad()
+
+        @pl.when(jnp.logical_not(early))
+        def _():
+            down_theirs[...] = down_grad().astype(bf16)
+
+        grad = up_grad()
+        mine[...] = grad[:piece]
+        theirs[...] = grad[piece:].astype(bf16)
+    else:
+        sums[1][...] = down_grad()
+        sums[0][...] = up_grad()
 
     @pl.when(step == pl.num_programs(0) - 1)
     def _():
+        row = lax.broadcasted_iota(jnp.int32, (room, 1), 0)
         for e in range(rows // room):
             at = e * room
+            dots = jnp.zeros((room, TILE), f32)
             for c in range(0, width, TILE):
                 scaled = y_sum[at : at + room, c : c + TILE] * gate[at : at + room, :]
-                out_ref[e, :room, c : c + TILE] = scaled.astype(bf16)
-            out_ref[e, room:, :] = back_sum[at : at + room, :].astype(bf16)
-
-
-def run_experts(x, cot, batch, up, down, before, capacity):
+                y_ref[e, :, c : c + TILE] = scaled.astype(bf16)
+                dots = dots + scaled * cot_ref[e, :, c : c + TILE].astype(f32)
+            if room < TILE:
+                dots = jnp.concatenate([dots, jnp.zeros((TILE - room, TILE), f32)], axis=0)
+            line = jnp.sum(dots.T, axis=0, keepdims=True)
+            high = line.astype(bf16).astype(f32)
+            line = jnp.concatenate(
+                [high, line - high, jnp.zeros((1, width - 2 * TILE), f32)], axis=1
+            )
+            for i in range(pieces):
+                back_ref[e, :, columns(i)] = back_sum[
+                    at : at + room, i * piece : (i + 1) * piece
+                ].astype(bf16)
+            back_ref[e] = jnp.where(row == capacity, line.astype(bf16), back_ref[e])
+
+
+def run_experts(ctx, x, cot, batch, up, down, made, capacity, halves, split):
     sources, room, width = x.shape
     rows = sources * room
     hidden = up.shape[1]
-    part = math.gcd(hidden, 512)
+    part = math.gcd(hidden // 2, 512)
+    steps = hidden // part
+    ahead = steps // 2 if halves else 0
     chunk = rows // 2 if rows % 32 == 0 else rows
+    more = len(made) > 0
     once = pl.Buffered(1)
-    columns = pl.BlockSpec((width, part), lambda t: (0, t))
-    lines = pl.BlockSpec((part, width), lambda t: (t, 0))
-    more = len(before) > 0
+    columns = pl.BlockSpec((width, part), lambda t, c: (0, (t + c[0] * ahead) % steps))
+    lines = pl.BlockSpec((part, width), lambda t, c: (t, 0))
+    cot_rows = pl.BlockSpec((sources, room, width), lambda t, c: (0, batch, 0), pipeline_mode=once)
+    whole = pl.BlockSpec((sources, room, width), lambda t, c: (0, 0, 0), pipeline_mode=once)
+    if split:
+        half = pl.BlockSpec((width // 2, part), lambda t, c: (0, (t + c[0] * ahead) % steps))
+        sums = [
+            (half, (width // 2, hidden), f32),
+            (half, (width // 2, hidden), bf16),
+            (pl.BlockSpec((part, width), lambda t, c: (jnp.minimum(t, ahead - 1), 0)),
+             (hidden // 2, width), f32),
+            (pl.BlockSpec((part, width), lambda t, c: (jnp.maximum(t - ahead, 0), 0)),
+             (hidden // 2, width), bf16),
+        ]
+    else:
+        sums = [(columns, up.shape, f32), (lines, down.shape, f32)]
+    aliases = {5: 0} if split else {5: 0, 6: 2, 7: 3}
     return pl.pallas_call(
-        functools.partial(expert_kernel, more, capacity, room, chunk),
-        grid=(hidden // part,),
-        in_specs=[
-            pl.BlockSpec((sources, room, width), lambda t: (0, 0, 0), pipeline_mode=once),
-            pl.BlockSpec((sources, room, width), lambda t: (0, batch, 0), pipeline_mode=once),
-            columns,
-            lines,
+        functools.partial(expert_kernel, more, halves, split, capacity, room, chunk),
+        grid_spec=pltpu.PrefetchScalarGridSpec(
+            num_scalar_prefetch=1,
+            grid=(steps,),
+            in_specs=[whole, cot_rows, columns, lines]
+            + ([pl.BlockSpec(memory_space=pl.ANY), columns, lines] if more else []),
+            out_specs=[cot_rows, whole]
+            + [spec for spec, _, _ in sums],
+            scratch_shapes=[
+                pltpu.VMEM((rows, width), f32),
+                pltpu.VMEM((rows, width), f32),
+                pltpu.VMEM((rows, width), bf16),
+                pltpu.VMEM((rows, width), bf16),
+                pltpu.VMEM((rows, TILE), f32),
+                pltpu.VMEM((rows, part), bf16),
+                pltpu.VMEM((rows, part), bf16),
+            ]
+        ),
+        out_shape=[
+            jax.ShapeDtypeStruct(cot.shape, bf16),
+            jax.ShapeDtypeStruct((sources, room, width), bf16),
         ]
-        + ([columns, lines] if more else []),
-        out_specs=[
-            pl.BlockSpec((sources, 2 * room, width), lambda t: (0, 0, 0), pipeline_mode=once),
-            columns,
-            lines,
-        ],
-        out_shape=[
-            jax.ShapeDtypeStruct((sources, 2 * room, width), bf16),
-            jax.ShapeDtypeStruct((width, hidden), f32),
-            jax.ShapeDtypeStruct((hidden, width), f32),
-        ],
-        scratch_shapes=[
-            pltpu.VMEM((rows, width), f32),
-            pltpu.VMEM((rows, width), f32),
-            pltpu.VMEM((rows, width), bf16),
-            pltpu.VMEM((rows, width), bf16),
-            pltpu.VMEM((rows, TILE), f32),
-            pltpu.VMEM((rows, part), bf16),
-            pltpu.VMEM((rows, part), bf16),
-        ],
-        input_output_aliases={4: 1, 5: 2} if more else {},
+        + [jax.ShapeDtypeStruct(shape, kind) for _, shape, kind in sums],
+        input_output_aliases=aliases if more else {},
         compiler_params=pltpu.CompilerParams(vmem_limit_bytes=60 * 2**20),
         cost_estimate=pl.CostEstimate(
-            flops=12 * rows * width * hidden, bytes_accessed=40 * 2**20,
+            flops=18 * rows * width * hidden, bytes_accessed=40 * 2**20,
             transcendentals=rows * hidden,
         ),
         name="experts",
-    )(x, cot, up, down, *before)
+    )(ctx, x, cot, up, down, *made)
 
 
 def bits_of(axis):
@@ -428,7 +484,7 @@
     return lax.optimization_barrier((x, *others))[0]
 
 
-def gather_rows(left, right):
+def gather_rows(left, right, early):
     if not (power_of_two("ctx") and power_of_two("exp")):
         return [lax.all_gather(x, ("ctx", "exp"), axis=0, tiled=True) for x in (left, right)]
     bits = bits_of("exp")
@@ -441,6 +497,7 @@
             jnp.stack(ordered(h, g, "exp", bit), axis=1).reshape((-1,) + h.shape[1:])
             for h, g in zip(held, got)
         ]
+    held = [after(h, early) for h in held]
     got = [swap(h, "exp", bit) for h, bit in zip(held, last)]
     held = [jnp.stack(ordered(h, g, "exp", bit), axis=1) for h, g, bit in zip(held, got, last)]
     got = [swap(h, "exp", bit) for h, bit in zip(held, last[::-1])]
@@ -458,21 +515,10 @@
     return held
 
 
-def pair_rows(x, axis):
+def pair_rows(x):
     if lax.axis_size("ctx") != 2:
-        return lax.all_gather(x, "ctx", axis=axis, tiled=True)
-    return jnp.concatenate(ordered(x, swap(x, "ctx", 1), "ctx", 1), axis=axis)
-
-
-def send_half(x, axis):
-    ways = lax.axis_size("ctx")
-    if ways != 2:
-        return lax.psum_scatter(x.astype(bf16), "ctx", scatter_dimension=axis, tiled=True).astype(f32)
-    part = x.shape[axis] // 2
-    me = lax.axis_index("ctx")
-    mine = lax.dynamic_slice_in_dim(x, me * part, part, axis)
-    theirs = lax.dynamic_slice_in_dim(x, (1 - me) * part, part, axis)
-    return mine + swap(theirs.astype(bf16), "ctx", 1).astype(f32)
+        return lax.all_gather(x, "ctx", axis=0, tiled=True)
+    return jnp.concatenate([x, swap(x, "ctx", 1)], axis=0)
 
 
 def halve(x, axis, bit, dim):
@@ -482,21 +528,28 @@
     return mine + swap(theirs.astype(bf16), axis, bit).astype(f32)
 
 
-def scatter_sum(left, right):
+def scatter_sum(grads, width, late):
     if not (power_of_two("exp") and lax.axis_size("ctx") == 2 and lax.axis_size("exp") > 3):
-        return [
-            lax.psum_scatter(x, ("ctx", "exp"), scatter_dimension=0, tiled=True)
-            for x in (left, right)
+        whole = grads(lambda x, axis: x)
+        sums = [
+            lax.psum_scatter(x, ("ctx", "exp"), scatter_dimension=0, tiled=True) for x in whole
         ]
+        return [*sums, sums[0]]
+    me = lax.axis_index("ctx")
+    part = width // 2
+    theirs = grads(lambda x, axis: lax.dynamic_slice_in_dim(x, (1 - me) * part, part, axis))
+    got = [swap(x.astype(bf16), "ctx", 1) for x in theirs]
+    mine = grads(lambda x, axis: lax.dynamic_slice_in_dim(x, me * part, part, axis))
+    begun = got[1]
     bits = bits_of("exp")
-    held = [send_half(x, 0) for x in (left, right)]
+    held = [after(m + g.astype(f32), late) for m, g in zip(mine, got)]
     held = [h.reshape((-1, 2, 2, h.shape[0] // lax.axis_size("exp"), h.shape[1])) for h in held]
     high, low = bits[-2:]
     held = [halve(held[0], "exp", high, 1), halve(held[1], "exp", low, 2)]
     held = [halve(held[0], "exp", low, 1), halve(held[1], "exp", high, 1)]
     for bit in bits[:-2][::-1]:
         held = [halve(h.reshape((-1, 2) + h.shape[1:]), "exp", bit, 1) for h in held]
-    return [h.reshape(h.shape[-2:]) for h in held]
+    return [*(h.reshape(h.shape[-2:]) for h in held), begun]
 
 
 def total_of(x):
@@ -558,6 +611,9 @@
     def cross(x):
         return lax.all_to_all(x, "exp", split_axis=0, concat_axis=0, tiled=True)
 
+    cots = [cotangent[b, 0] for b in range(batches)]
+    cot_sent = jnp.concatenate([dispatch(b, cots[b]) for b in range(batches)], axis=1)
+
     pad = -(experts + 2) % 128
     left, right = gather_rows(
         jnp.concatenate([query_key_value_weight[:, :width], output_projection_weight], axis=1),
@@ -571,6 +627,7 @@
             ],
             axis=1,
         ),
+        cot_sent,
     )
     query_weight = left[:, :width]
     proj_weight = left[:, width:]
@@ -579,12 +636,7 @@
     gains = right[:, 2 * width + experts : 2 * width + experts + 2].astype(f32)
     attn_scale = gains[:, 0]
     expert_scale = gains[:, 1]
-    up_all = pair_rows(expert_up[0], 0)
-    down_all = pair_rows(expert_down[0], 0)
-
-    cots = [cotangent[b, 0] for b in range(batches)]
-    sent = jnp.concatenate([dispatch(b, cots[b]) for b in range(batches)], axis=1)
-    cot_here = cross(after(sent, left, right))
+    expert_weights = [pair_rows(w[0]) for w in (expert_up, expert_down)]
 
     distance = jnp.arange(2 * TILE, dtype=jnp.int32)
     hot_bucket = (
@@ -624,8 +676,10 @@
         view = (tiles, queries, kv, kv_back, query_docs[None], key_docs[None], bias_rows)
         state.append(dict(rows=rows, inv_one=inv_one, normed=normed, view=view))
 
-    last = cot_here
+    cot_here = cross(after(cot_sent, left, right))
+    sent = ()
     for b, s in enumerate(state):
+        s["view"] = (after(s["view"][0], *sent),) + s["view"][1:]
         attended, lse = attend(*s["view"])
         hidden = s["rows"] + mm(attended, proj_weight, ((1,), (0,)))
         inv_two = norm_stats(hidden)
@@ -645,38 +699,52 @@
             [gate_high, gate_low, jnp.zeros((experts, 1, width - 2 * TILE), bf16)], axis=2
         )
         at_gate = lax.broadcasted_iota(jnp.int32, (1, room, 1), 1) == capacity
-        sent = jnp.where(at_gate, gate_row, dispatch(b, shared))
+        sent = (jnp.where(at_gate, gate_row, dispatch(b, shared)),)
         s.update(attended=attended, lse=lse, hidden=hidden, inv_two=inv_two, shared=shared,
-                 gates=gates, here=cross(after(sent, last)))
-        last = s["here"]
-
-    grads = ()
+                 gates=gates, sent=sent[0])
+
+    made = ()
+    last = (cot_here, *(s["sent"] for s in state))
+    for s in state:
+        s["here"] = cross(after(s["sent"], *last))
+        last = (s["here"],)
     for b, s in enumerate(state):
-        out, *grads = run_experts(s["here"], cot_here, b, up_all, down_all, grads, capacity)
-        s["back"] = cross(after(out, last))
-        last = s["back"]
-    grad_up, grad_down = grads
-    up_share = send_half(grad_up, 0)[None]
-    down_share = send_half(grad_down, 0)[None]
-
-    outputs = []
+        y, back, *sums = run_experts(
+            me[None].astype(jnp.int32), s["here"], cot_here, b, *expert_weights, made, capacity,
+            ways == 2, ways == 2 and b == batches - 1,
+        )
+        made = (y, *sums)
+        s["back"] = cross(after(back, *last))
+        last = (s["back"],)
+    results = cross(after(y, *last))
+    if ways == 2:
+        up_share, down_share = (
+            (mine + swap(theirs, "ctx", 1).astype(f32))[None]
+            for mine, theirs in zip(sums[::2], sums[1::2])
+        )
+    else:
+        up_share, down_share = (
+            lax.psum_scatter(g.astype(bf16), "ctx", scatter_dimension=0, tiled=True).astype(f32)[None]
+            for g in sums
+        )
+
     input_grads = []
     parts = []
+    picks = []
+    before = ()
     for b, s in enumerate(state):
         upstream = cots[b].astype(f32)
-        packet = after(s["back"], *input_grads)
-        returned = packet[:, :room].reshape(slots, width)
-        grad_rows = packet[:, room:].reshape(slots, width)
+        packet = after(s["back"], *before)
+        dots = packet[:, capacity, : 2 * TILE].astype(f32)
+        dots = (dots[:, :room] + dots[:, TILE : TILE + room]).reshape(1, slots)
         slot = slot_of[b]
-        picks = [(slot[:, k : k + 1] == slot_rows[None, :]).astype(bf16) for k in range(top)]
-        picked = [mm(p, returned, ((1,), (0,))) for p in picks]
-        outputs.append((s["hidden"] + functools.reduce(jnp.add, picked)).astype(bf16))
-        scaled = jnp.stack([jnp.sum(p * upstream, axis=1) for p in picked], axis=1)
+        pick = [slot[:, k : k + 1] == slot_rows[None, :] for k in range(top)]
+        picks.append(functools.reduce(jnp.logical_or, pick).astype(bf16))
+        scaled = jnp.stack([jnp.sum(jnp.where(p, dots, 0.0), axis=1) for p in pick], axis=1)
         chosen_grad = scaled - s["gates"] * jnp.sum(scaled, axis=1, keepdims=True)
         logit_grad = jnp.sum(jnp.where(hots[b], chosen_grad[:, :, None], 0.0), axis=1).astype(bf16)
-        shared_grad = mm(functools.reduce(jnp.add, picks), grad_rows, ((1,), (0,)))
+        shared_grad = mm(picks[b], packet.reshape(slots, width), ((1,), (0,)))
         shared_grad = shared_grad + mm(logit_grad, router_all, ((1,), (1,)))
-        grad_router = mm(s["shared"], logit_grad, ((0,), (0,)))
         unit = s["hidden"] * s["inv_two"]
         grad_expert = jnp.sum(shared_grad * unit, axis=0)
         inner = shared_grad * expert_scale
@@ -684,9 +752,9 @@
             inner - unit * jnp.mean(inner * unit, axis=1, keepdims=True)
         )
         branch_grad = hidden_grad.astype(bf16)
-        grad_proj = mm(s["attended"], branch_grad, ((0,), (0,)))
         attended_grad = mm(branch_grad, proj_weight, ((1,), (1,))).astype(bf16)
         dq, own, back, near = attend_back(*s["view"], s["attended"], attended_grad, s["lse"])
+        before = (dq,)
         if ways == 2:
             got = lax.ppermute(back, "ctx", [(1, 0)])
         else:
@@ -696,38 +764,51 @@
         both = (own.astype(f32) + got.astype(f32)).astype(bf16)
         dkv = jnp.concatenate([both[0], both[1]], axis=1)
         normed = s["normed"]
-        grad_query = mm(normed, dq, ((0,), (0,)))
-        grad_kv = mm(normed, dkv, ((0,), (0,)))
         normed_grad = mm(dq, query_weight, ((1,), (1,))) + mm(dkv, kv_weight, ((1,), (1,)))
         unit = s["rows"] * s["inv_one"]
         grad_attn = jnp.sum(normed_grad * unit, axis=0)
         inner = normed_grad * attn_scale
         input_part = s["inv_one"] * (inner - unit * jnp.mean(inner * unit, axis=1, keepdims=True))
         input_grads.append((hidden_grad + input_part).astype(bf16))
-        parts.append((grad_query, grad_kv, grad_proj, grad_router, grad_attn, grad_expert, near))
-
-    grad_query, grad_kv, grad_proj, grad_router, grad_attn, grad_expert, near = (
-        functools.reduce(jnp.add, p) for p in zip(*parts)
-    )
+        parts.append((near, grad_attn, grad_expert))
+        s.update(dq=dq, dkv=dkv, branch_grad=branch_grad, logit_grad=logit_grad)
+
+    outputs = []
+    for b, s in enumerate(state):
+        mine = results[:, b * room : (b + 1) * room].reshape(slots, width)
+        outputs.append((s["hidden"] + mm(picks[b], mine, ((1,), (0,)))).astype(bf16))
+
+    near, grad_attn, grad_expert = (functools.reduce(jnp.add, p) for p in zip(*parts))
+
+    def weight_grads(rows):
+        def total(left, right):
+            return functools.reduce(
+                jnp.add, [mm(rows(s[left], 1), s[right], ((0,), (0,))) for s in state]
+            )
+
+        small = total("shared", "logit_grad")
+        return (
+            jnp.concatenate([total("normed", "dq"), total("attended", "branch_grad")], axis=1),
+            jnp.concatenate(
+                [
+                    total("normed", "dkv"),
+                    small,
+                    rows(grad_attn, 0)[:, None],
+                    rows(grad_expert, 0)[:, None],
+                    jnp.zeros((small.shape[0], pad), f32),
+                ],
+                axis=1,
+            ),
+        )
+
+    left, right, begun = scatter_sum(weight_grads, width, results)
     hot_near = jnp.where(
         jnp.arange(buckets)[:, None] < buckets - 1, hot_bucket[:, :TILE], 0.0
     )
     grad_bias = jnp.sum(near.reshape(HEADS, 1, TILE) * hot_near[None], axis=2)
     far = jnp.where(jnp.arange(buckets) == buckets - 1, 1.0, 0.0)
-    bias_total = total_of(grad_bias - jnp.sum(grad_bias, axis=1, keepdims=True) * far)
-    left, right = scatter_sum(
-        jnp.concatenate([grad_query, grad_proj], axis=1),
-        jnp.concatenate(
-            [
-                grad_kv,
-                grad_router,
-                grad_attn[:, None],
-                grad_expert[:, None],
-                jnp.zeros((width, pad), f32),
-            ],
-            axis=1,
-        ),
-    )
+    grad_bias = grad_bias - jnp.sum(grad_bias, axis=1, keepdims=True) * far
+    bias_total = total_of(after(grad_bias, begun))
     return (
         jnp.stack(outputs)[:, None],
         jnp.stack(input_grads)[:, None],

time: 700 us -> 623 us (0.89)
  waiting for transfers between devices: 180 us -> 136 us
  starting transfers between devices: 132 us -> 107 us
  local copies, waits for them, and re-layouts: 54.5 us -> 46.8 us
    all_to_all x5 -> x6, waiting for transfers between devices: 115 us -> 56 us  [cross(): return lax.all_to_all(x, 'exp', split_axis=0, concat_axis=0, tiled=True)]
    ppermute x29, waiting for transfers between devices: 65.5 us -> 79.7 us  [swap(): return lax.ppermute(x, axis, [(i, i ^ bit) for i in range(size)])]
    all_to_all x5 -> x6, starting transfers between devices: 79.2 us -> 66.2 us  [cross(): return lax.all_to_all(x, 'exp', split_axis=0, concat_axis=0, tiled=True)]
    ppermute x29, starting transfers between devices: 44.5 us -> 33.2 us  [swap(): return lax.ppermute(x, axis, [(i, i ^ bit) for i in range(size)])]
    convert_element_type x3 -> x0, local copies, waits for them, and re-layouts: 10.1 us -> none  [send_half(): return mine + swap(theirs.astype(bf16), 'ctx', 1).astype(f32)]
    unnamed x179 -> x273, local copies, waits for them, and re-layouts: 17.2 us -> 24.5 us
    dot_general x36 -> x42, matrix products: 62.3 us -> 63.3 us  [mm(): return lax.dot_general(a, b, (dims, ((), ())), preferred_element_type=f32)]
  transfers between devices with their start and end apart: 38 -> 39, of which waited for: 17 -> 21; matrix products, arithmetic and copies ran while one was open for 21% -> 21% of each run, Pallas kernels for 25% -> 32%
where the time goes in v3:
time: 623 us; the launch traced here: 613 us
  Pallas kernels  199 us (32%)
  waiting for transfers between devices  136 us (22%)
  starting transfers between devices  107 us (17%)
  matrix products  63.3 us (10%)
  other arithmetic  58.6 us (9%)
  local copies, waits for them, and re-layouts  46.8 us (8%)
    pallas_call x2, Pallas kernels, run_experts(): pl.pallas_call(functools.partial(expert_kernel, more, halves, split, capa...  121 us
    ppermute x29, waiting for transfers between devices, swap(): return lax.ppermute(x, axis, [(i, i ^ bit) for i in range(size)])  79.7 us
    all_to_all x6, starting transfers between devices, cross(): return lax.all_to_all(x, 'exp', split_axis=0, concat_axis=0, tiled=True)  66.2 us
    dot_general x42, matrix products, mm(): return lax.dot_general(a, b, (dims, ((), ())), preferred_element_type=f32)  63.3 us
    all_to_all x6, waiting for transfers between devices, cross(): return lax.all_to_all(x, 'exp', split_axis=0, concat_axis=0, tiled=True)  56 us
    pallas_call x2, Pallas kernels, attend_back(): pl.pallas_call(bwd_kernel, grid_spec=pltpu.PrefetchScalarGridSpec(num_sca...  44.8 us
    ppermute x29, starting transfers between devices, swap(): return lax.ppermute(x, axis, [(i, i ^ bit) for i in range(size)])  33.2 us
    pallas_call x2, Pallas kernels, attend(): pl.pallas_call(fwd_kernel, grid_spec=pltpu.PrefetchScalarGridSpec(num_sca...  32.5 us
  transfers between devices with their start and end apart: 39, of which 21 were waited for; matrix products, arithmetic and copies ran while one was open for 21% of the time, Pallas kernels for 32%

profile of v3, /device:TPU:0, one launch (start us, length us, event | category | flops | bytes accessed | tf_op | source)
XLA Modules:
  0.0 613.0 jit_solution(2305249403975453229)
XLA Ops:
  21.5 4.6 collective-permute-done.6
  40.5 8.5 %collective-permute-done.8 = bf16[4,2,24,1536]{3,2,0,1:T(8,128)(2,1)S(1)} collective-permute-done((bf16[4,2,24,1536]{3,2,0,1:T(8,128)(2,1)S(1)}, bf16[4,2,24,1536]{3,2,0,1:T(8,128)(2,1)S(1)}, u32[]{:S(2)}, u32[]{:S(2)}) %collective-permute-start.8) | collective-permute-done | bytes 589856 | tf_op jit(solution)/shard_map/ppermute | solution.py:475
  60.3 6.7 %all-to-all-start = ((bf16[16,192,768]{2,1,0:T(8,128)(2,1)}), bf16[16,192,768]{2,1,0:T(8,128)(2,1)}, u32[]{:S(2)}, u32[]{:S(2)}) async-start(bf16[16,192,768]{2,1,0:T(8,128)(2,1)} %pad_maximum_fusion), calls=%async_computation | async-start | bytes 9437184 | tf_op jit(solution)/shard_map/all_to_all | solution.py:612
  83.8 16.6 %attend.2 = (bf16[512,768]{1,0:T(8,128)(2,1)S(1)}, f32[6,4,256]{2,1,0:T(4,128)S(1)}) custom-call(s32[4]{0:T(128)S(1)} %subtract_clamp_fusion.1.tiles, bf16[512,768]{1,0:T(8,128)(2,1)S(1)} %convolution_convert_fusion.9.q_ref, bf16[512,1536]{1,0:T(8,128)(2,1)} %convolution_convert_fusion.5.k_ref.v_ref, ...), custom_call_target="tpu_custom_call" | custom-call | flops 3221225472 | bytes 6291456 | tf_op jit(solution)/shard_map/attend/pallas_call | solution.py:226
  110.7 15.9 %attend.3 = (bf16[512,768]{1,0:T(8,128)(2,1)S(1)}, f32[6,4,256]{2,1,0:T(4,128)S(1)}) custom-call(s32[4]{0:T(128)S(1)} %subtract_clamp_fusion.tiles, bf16[512,768]{1,0:T(8,128)(2,1)S(1)} %copy-done.18, bf16[512,1536]{1,0:T(8,128)(2,1)S(1)} %convolution_convert_fusion.4.k_ref.v_ref, bf16[512,1536]{1,0:T(8,128)(2,1)S(1)} %convolution_convert_fusion.4.k_ref.v_ref, ...), custom_call_target="tpu_custom_call" | custom-call | flops 3221225472 | bytes 6291456 | tf_op jit(solution)/shard_map/attend/pallas_call | solution.py:226
  134.5 22.4 %all-to-all-done.cot_ref = bf16[16,192,768]{2,1,0:T(8,128)(2,1)} async-done(((bf16[16,192,768]{2,1,0:T(8,128)(2,1)}), bf16[16,192,768]{2,1,0:T(8,128)(2,1)}, u32[]{:S(2)}, u32[]{:S(2)}) %all-to-all-start) | async-done | bytes 4718624 | tf_op jit(solution)/shard_map/all_to_all | solution.py:612
  156.9 23.0 %all-to-all-start.1 = ((bf16[16,96,768]{2,1,0:T(8,128)(2,1)}), bf16[16,96,768]{2,1,0:T(8,128)(2,1)S(1)}, u32[]{:S(2)}, u32[]{:S(2)}) async-start(bf16[16,96,768]{2,1,0:T(8,128)(2,1)} %broadcast_select_fusion.1), calls=%async_computation.1 | async-start | bytes 4718592 | tf_op jit(solution)/shard_map/all_to_all | solution.py:612
  184.8 5.0 pad_maximum_fusion.1.up_ref
  189.8 4.2 pad_maximum_fusion.2.down_ref
  194.0 32.7 %all-to-all-done.1.x_ref = bf16[16,96,768]{2,1,0:T(8,128)(2,1)S(1)} async-done(((bf16[16,96,768]{2,1,0:T(8,128)(2,1)}), bf16[16,96,768]{2,1,0:T(8,128)(2,1)S(1)}, u32[]{:S(2)}, u32[]{:S(2)}) %all-to-all-start.1) | async-done | bytes 2359328 | tf_op jit(solution)/shard_map/all_to_all | solution.py:612
  228.1 10.9 %all-to-all-start.2 = ((bf16[16,96,768]{2,1,0:T(8,128)(2,1)}), bf16[16,96,768]{2,1,0:T(8,128)(2,1)}, u32[]{:S(2)}, u32[]{:S(2)}) async-start(bf16[16,96,768]{2,1,0:T(8,128)(2,1)} %broadcast_select_fusion), calls=%async_computation.2 | async-start | bytes 4718592 | tf_op jit(solution)/shard_map/all_to_all | solution.py:612
  239.0 59.4 %experts.2 = (bf16[16,192,768]{2,1,0:T(8,128)(2,1)}, bf16[16,96,768]{2,1,0:T(8,128)(2,1)}, f32[768,3072]{1,0:T(8,128)}, f32[3072,768]{1,0:T(8,128)}) custom-call(s32[1]{0:T(128)} %bitcast.51.ctx, bf16[16,96,768]{2,1,0:T(8,128)(2,1)} %copy-done.73, bf16[16,192,768]{2,1,0:T(8,128)(2,1)} %all-to-all-done.cot_ref, bf16[768,3072]{1,0:T(8,128)(2,1)} %pad_maximum_fusion.1.up_ref, ...), custom_call_target="tpu_custom_call" | custom-call | flops 65229815808 | bytes 41943040 | tf_op jit(solution)/shard_map/experts/pallas_call | solution.py:430
  298.4 7.0 %all-to-all-start.3 = ((bf16[16,96,768]{2,1,0:T(8,128)(2,1)}), bf16[16,96,768]{2,1,0:T(8,128)(2,1)S(1)}, u32[]{:S(2)}, u32[]{:S(2)}) async-start(bf16[16,96,768]{2,1,0:T(8,128)(2,1)} %get-tuple-element.59), calls=%async_computation.3 | async-start | bytes 4718592 | tf_op jit(solution)/shard_map/all_to_all | solution.py:612
  305.5 61.9 %experts.3 = (bf16[16,192,768]{2,1,0:T(8,128)(2,1)}, bf16[16,96,768]{2,1,0:T(8,128)(2,1)}, f32[384,3072]{1,0:T(8,128)}, bf16[384,3072]{1,0:T(8,128)(2,1)}, f32[1...) custom-call(s32[1]{0:T(128)} %bitcast.51.ctx, ...), custom_call_target="tpu_custom_call", output_to_operand_aliasing={{0}: (5, {})} | custom-call | flops 65229815808 | bytes 41943040 | tf_op jit(solution)/shard_map/experts/pallas_call | solution.py:430
  374.6 7.1 %all-to-all-start.4 = ((bf16[16,96,768]{2,1,0:T(8,128)(2,1)}), bf16[16,96,768]{2,1,0:T(8,128)(2,1)}, u32[]{:S(2)}, u32[]{:S(2)}) async-start(bf16[16,96,768]{2,1,0:T(8,128)(2,1)} %get-tuple-element.60), calls=%async_computation.4 | async-start | bytes 4718592 | tf_op jit(solution)/shard_map/all_to_all | solution.py:612
  385.5 22.3 %attend_back.2 = (bf16[512,768]{1,0:T(8,128)(2,1)S(1)}, bf16[2,512,768]{2,1,0:T(8,128)(2,1)S(1)}, bf16[2,512,768]{2,1,0:T(8,128)(2,1)S(1)}, f32[6,1,256]{2,1,0:T(1,128)S(1)}) custom-call(s32[4]{0:T(128)S(1)} %subtract_clamp_fusion.1.tiles, bf16[512,768]{1,0:T(8,128)(2,1)S(1)} %copy-done.21, bf16[512,1536]{1,0:T(8,128)(2,1)} %convolution_convert_fusion.5.k_ref.v_ref, ...), custom_call_target="tpu_custom_call" | custom-call | flops 8053063680 | bytes 12582912 | tf_op jit(solution)/shard_map/attend_back/pallas_call | solution.py:262
  409.2 4.6 add_bitcast_fusion
  413.8 4.9 add_bitcast_fusion.1
  439.7 11.6 %all-to-all-start.5 = ((bf16[16,192,768]{2,1,0:T(8,128)(2,1)}), bf16[16,192,768]{2,1,0:T(8,128)(2,1)}, u32[]{:S(2)}, u32[]{:S(2)}) async-start(bf16[16,192,768]{2,1,0:T(8,128)(2,1)} %get-tuple-element.61), calls=%async_computation.5 | async-start | bytes 9437184 | tf_op jit(solution)/shard_map/all_to_all | solution.py:612
  457.6 22.5 %attend_back.3 = (bf16[512,768]{1,0:T(8,128)(2,1)S(1)}, bf16[2,512,768]{2,1,0:T(8,128)(2,1)S(1)}, bf16[2,512,768]{2,1,0:T(8,128)(2,1)}, f32[6,1,256]{2,1,0:T(1,128)S(1)}) custom-call(s32[4]{0:T(128)S(1)} %subtract_clamp_fusion.tiles, bf16[512,768]{1,0:T(8,128)(2,1)S(1)} %copy-done.19, bf16[512,1536]{1,0:T(8,128)(2,1)S(1)} %copy-done.14, ...), custom_call_target="tpu_custom_call" | custom-call | flops 8053063680 | bytes 12582912 | tf_op jit(solution)/shard_map/attend_back/pallas_call | solution.py:262
  522.7 4.3 collective-permute-start.27
  527.9 27.4 %collective-permute-done.27 = f32[12,32]{1,0:T(8,128)S(1)} collective-permute-done((f32[12,32]{1,0:T(8,128)S(1)}, f32[12,32]{1,0:T(8,128)S(1)}, u32[]{:S(2)}, u32[]{:S(2)}) %collective-permute-start.27) | collective-permute-done | bytes 1568 | tf_op jit(solution)/shard_map/ppermute | solution.py:475
  599.0 5.4 collective-permute-done.20
  605.9 4.7 collective-permute-done.25
  (562 shorter events, 216.6 us)
Async XLA Ops:
  2.3 16.0 %collective-permute-start.5 = (bf16[1,24,1536]{2,1,0:T(8,128)(2,1)S(1)}, bf16[1,24,1536]{2,1,0:T(8,128)(2,1)}, u32[]{:S(2)}, u32[]{:S(2)}) collective-permute-start(bf16[1,24,1536]{2,1,0:T(8,128)(2,1)S(1)} %maximum_bitcast_fusion.4), channel_id=1, source_target_pairs={{0,8},{1,9},{2,10},{3,11},{4,12},{5,13},{6,14},{7,15},{8,0},{9,1},... | collective-permute-start | bytes 221192 | tf_op jit(solution)/shard_map/ppermute | solution.py:475
  9.6 11.6 %collective-permute-start = (bf16[1,24,1664]{2,1,0:T(8,128)(2,1)S(1)}, bf16[1,24,1664]{2,1,0:T(8,128)(2,1)S(1)}, u32[]{:S(2)}, u32[]{:S(2)}) collective-permute-start(bf16[1,24,1664]{2,1,0:T(8,128)(2,1)S(1)} %bitcast.295), channel_id=1, source_target_pairs={{0,8},{1,9},{2,10},{3,11},{4,12},{5,13},{6,14},{7,15},{8,0},{9,1},... | collective-permute-start | bytes 239624 | tf_op jit(solution)/shard_map/ppermute | solution.py:475
  28.2 10.5 %collective-permute-start.2 = (bf16[4,24,1664]{2,1,0:T(8,128)(2,1)S(1)}, bf16[4,24,1664]{2,1,0:T(8,128)(2,1)S(1)}, u32[]{:S(2)}, u32[]{:S(2)}) collective-permute-start(bf16[4,24,1664]{2,1,0:T(8,128)(2,1)S(1)} %bitcast.291), channel_id=1, source_target_pairs={{0,1},{1,0},{2,3},{3,2},{4,5},{5,4},{6,7},{7,6},{8,9},{9,8},{10,11... | collective-permute-start | bytes 958472 | tf_op jit(solution)/shard_map/ppermute | solution.py:475
  33.1 15.9 %collective-permute-start.8 = (bf16[4,2,24,1536]{3,2,0,1:T(8,128)(2,1)S(1)}, bf16[4,2,24,1536]{3,2,0,1:T(8,128)(2,1)S(1)}, u32[]{:S(2)}, u32[]{:S(2)}) collective-permute-start(bf16[4,2,24,1536]{3,2,0,1:T(8,128)(2,1)S(1)} %pad_maximum_fusion.11), channel_id=1, source_target_pairs={{0,1},{1,0},{2,3},{3,2},{4,5},{5,4},{6,7},{7,6},{8,9},{9,8},{10,11... | collective-permute-start | bytes 1769480 | tf_op jit(solution)/shard_map/ppermute | solution.py:475
  38.8 11.7 %collective-permute-start.3 = (bf16[4,2,24,1664]{3,2,0,1:T(8,128)(2,1)S(1)}, bf16[4,2,24,1664]{3,2,0,1:T(8,128)(2,1)S(1)}, u32[]{:S(2)}, u32[]{:S(2)}) collective-permute-start(bf16[4,2,24,1664]{3,2,0,1:T(8,128)(2,1)S(1)} %pad_maximum_fusion.10), channel_id=1, source_target_pairs={{0,2},{1,3},{2,0},{3,1},{4,6},{5,7},{6,4},{7,5},{8,10},{9,11},{10,... | collective-permute-start | bytes 1916936 | tf_op jit(solution)/shard_map/ppermute | solution.py:475
  60.3 96.6 %all-to-all-start = ((bf16[16,192,768]{2,1,0:T(8,128)(2,1)}), bf16[16,192,768]{2,1,0:T(8,128)(2,1)}, u32[]{:S(2)}, u32[]{:S(2)}) async-start(bf16[16,192,768]{2,1,0:T(8,128)(2,1)} %pad_maximum_fusion), calls=%async_computation | async-start | bytes 9437184 | tf_op jit(solution)/shard_map/all_to_all | solution.py:612
  71.9 11.9 %collective-permute-start.10 = (bf16[512,1536]{1,0:T(8,128)(2,1)}, bf16[512,1536]{1,0:T(8,128)(2,1)}, u32[]{:S(2)}, u32[]{:S(2)}) collective-permute-start(bf16[512,1536]{1,0:T(8,128)(2,1)} %convolution_convert_fusion.5.k_ref.v_ref), channel_id=1, source_target_pairs={{0,16},{1,17},{2,18},{3,19},{4,20},{5,21},{6,22},{7,23},{8,24},{9,... | collective-permute-start | bytes 4718600 | tf_op jit(solution)/shard_map/ppermute | solution.py:667
  78.5 32.1 %collective-permute-start.11 = (bf16[512,1536]{1,0:T(8,128)(2,1)S(1)}, bf16[512,1536]{1,0:T(8,128)(2,1)S(1)}, u32[]{:S(2)}, u32[]{:S(2)}) collective-permute-start(bf16[512,1536]{1,0:T(8,128)(2,1)S(1)} %convolution_convert_fusion.4.k_ref.v_ref), channel_id=1, source_target_pairs={{0,16},{1,17},{2,18},{3,19},{4,20},{5,21},{6,22},{7,23},{8,24},{9,... | collective-permute-start | bytes 4718600 | tf_op jit(solution)/shard_map/ppermute | solution.py:667
  156.9 69.8 %all-to-all-start.1 = ((bf16[16,96,768]{2,1,0:T(8,128)(2,1)}), bf16[16,96,768]{2,1,0:T(8,128)(2,1)S(1)}, u32[]{:S(2)}, u32[]{:S(2)}) async-start(bf16[16,96,768]{2,1,0:T(8,128)(2,1)} %broadcast_select_fusion.1), calls=%async_computation.1 | async-start | bytes 4718592 | tf_op jit(solution)/shard_map/all_to_all | solution.py:612
  179.9 9.9 %collective-permute-start.13 = (bf16[1536,768]{1,0:T(8,128)(2,1)}, bf16[1536,768]{1,0:T(8,128)(2,1)}, u32[]{:S(2)}, u32[]{:S(2)}) collective-permute-start(bf16[1536,768]{1,0:T(8,128)(2,1)} %bitcast.281), channel_id=1, source_target_pairs={{0,16},{16,0},{1,17},{17,1},{2,18},{18,2},{3,19},{19,3},{4,20},{20... | collective-permute-start | bytes 7077896 | tf_op jit(solution)/shard_map/ppermute | solution.py:475
  228.1 70.3 %all-to-all-start.2 = ((bf16[16,96,768]{2,1,0:T(8,128)(2,1)}), bf16[16,96,768]{2,1,0:T(8,128)(2,1)}, u32[]{:S(2)}, u32[]{:S(2)}) async-start(bf16[16,96,768]{2,1,0:T(8,128)(2,1)} %broadcast_select_fusion), calls=%async_computation.2 | async-start | bytes 4718592 | tf_op jit(solution)/shard_map/all_to_all | solution.py:612
  298.4 69.5 %all-to-all-start.3 = ((bf16[16,96,768]{2,1,0:T(8,128)(2,1)}), bf16[16,96,768]{2,1,0:T(8,128)(2,1)S(1)}, u32[]{:S(2)}, u32[]{:S(2)}) async-start(bf16[16,96,768]{2,1,0:T(8,128)(2,1)} %get-tuple-element.59), calls=%async_computation.3 | async-start | bytes 4718592 | tf_op jit(solution)/shard_map/all_to_all | solution.py:612
  367.4 41.8 %collective-permute-start.32 = (bf16[1536,768]{1,0:T(8,128)(2,1)}, bf16[1536,768]{1,0:T(8,128)(2,1)}, u32[]{:S(2)}, u32[]{:S(2)}) collective-permute-start(bf16[1536,768]{1,0:T(8,128)(2,1)} %get-tuple-element.79), channel_id=1, source_target_pairs={{0,16},{16,0},{1,17},{17,1},{2,18},{18,2},{3,19},{19,3},{4,20},{20... | collective-permute-start | bytes 7077896 | tf_op jit(solution)/shard_map/ppermute | solution.py:475
  367.5 46.3 %collective-permute-start.31 = (bf16[384,3072]{1,0:T(8,128)(2,1)}, bf16[384,3072]{1,0:T(8,128)(2,1)}, u32[]{:S(2)}, u32[]{:S(2)}) collective-permute-start(bf16[384,3072]{1,0:T(8,128)(2,1)} %get-tuple-element.77), channel_id=1, source_target_pairs={{0,16},{16,0},{1,17},{17,1},{2,18},{18,2},{3,19},{19,3},{4,20},{20... | collective-permute-start | bytes 7077896 | tf_op jit(solution)/shard_map/ppermute | solution.py:475
  374.6 54.7 %all-to-all-start.4 = ((bf16[16,96,768]{2,1,0:T(8,128)(2,1)}), bf16[16,96,768]{2,1,0:T(8,128)(2,1)}, u32[]{:S(2)}, u32[]{:S(2)}) async-start(bf16[16,96,768]{2,1,0:T(8,128)(2,1)} %get-tuple-element.60), calls=%async_computation.4 | async-start | bytes 4718592 | tf_op jit(solution)/shard_map/all_to_all | solution.py:612
  407.8 11.9 %collective-permute-start.14 = (bf16[2,512,768]{2,1,0:T(8,128)(2,1)S(1)}, bf16[2,512,768]{2,1,0:T(8,128)(2,1)S(1)}, u32[]{:S(2)}, u32[]{:S(2)}) collective-permute-start(bf16[2,512,768]{2,1,0:T(8,128)(2,1)S(1)} %get-tuple-element.65), channel_id=1, source_target_pairs={{16,0},{17,1},{18,2},{19,3},{20,4},{21,5},{22,6},{23,7},{24,8},{25... | collective-permute-start | bytes 4718600 | tf_op jit(solution)/shard_map/ppermute | solution.py:759
  439.7 130.7 %all-to-all-start.5 = ((bf16[16,192,768]{2,1,0:T(8,128)(2,1)}), bf16[16,192,768]{2,1,0:T(8,128)(2,1)}, u32[]{:S(2)}, u32[]{:S(2)}) async-start(bf16[16,192,768]{2,1,0:T(8,128)(2,1)} %get-tuple-element.61), calls=%async_computation.5 | async-start | bytes 9437184 | tf_op jit(solution)/shard_map/all_to_all | solution.py:612
  480.1 19.0 %collective-permute-start.15 = (bf16[2,512,768]{2,1,0:T(8,128)(2,1)}, bf16[2,512,768]{2,1,0:T(8,128)(2,1)}, u32[]{:S(2)}, u32[]{:S(2)}) collective-permute-start(bf16[2,512,768]{2,1,0:T(8,128)(2,1)} %get-tuple-element.70), channel_id=1, source_target_pairs={{16,0},{17,1},{18,2},{19,3},{20,4},{21,5},{22,6},{23,7},{24,8},{25... | collective-permute-start | bytes 4718600 | tf_op jit(solution)/shard_map/ppermute | solution.py:759
  490.4 27.7 %collective-permute-start.16 = (bf16[384,1536]{1,0:T(8,128)(2,1)}, bf16[384,1536]{1,0:T(8,128)(2,1)}, u32[]{:S(2)}, u32[]{:S(2)}) collective-permute-start(bf16[384,1536]{1,0:T(8,128)(2,1)} %pad_maximum_fusion.9), channel_id=1, source_target_pairs={{0,16},{16,0},{1,17},{17,1},{2,18},{18,2},{3,19},{19,3},{4,20},{20... | collective-permute-start | bytes 3538952 | tf_op jit(solution)/shard_map/ppermute | solution.py:475
  522.7 32.6 %collective-permute-start.27 = (f32[12,32]{1,0:T(8,128)S(1)}, f32[12,32]{1,0:T(8,128)S(1)}, u32[]{:S(2)}, u32[]{:S(2)}) collective-permute-start(f32[12,32]{1,0:T(8,128)S(1)} %add.506), channel_id=1, source_target_pairs={{0,8},{1,9},{2,10},{3,11},{4,12},{5,13},{6,14},{7,15},{8,0},{9,1},... | collective-permute-start | bytes 4616 | tf_op jit(solution)/shard_map/ppermute | solution.py:475
  571.7 11.5 %collective-permute-start.17 = (bf16[4,2,24,1536]{3,2,0,1:T(8,128)(2,1)S(1)}, bf16[4,2,24,1536]{3,2,0,1:T(8,128)(2,1)S(1)}, u32[]{:S(2)}, u32[]{:S(2)}) collective-permute-start(bf16[4,2,24,1536]{3,2,0,1:T(8,128)(2,1)S(1)} %fusion.94), channel_id=1, source_target_pairs={{0,2},{1,3},{2,0},{3,1},{4,6},{5,7},{6,4},{7,5},{8,10},{9,11},{10,... | collective-permute-start | bytes 1769480 | tf_op jit(solution)/shard_map/ppermute | solution.py:475
  571.9 15.3 %collective-permute-start.22 = (bf16[4,2,24,1664]{3,2,0,1:T(8,128)(2,1)S(1)}, bf16[4,2,24,1664]{3,2,0,1:T(8,128)(2,1)S(1)}, u32[]{:S(2)}, u32[]{:S(2)}) collective-permute-start(bf16[4,2,24,1664]{3,2,0,1:T(8,128)(2,1)S(1)} %fusion.93), channel_id=1, source_target_pairs={{0,1},{1,0},{2,3},{3,2},{4,5},{5,4},{6,7},{7,6},{8,9},{9,8},{10,11... | collective-permute-start | bytes 1916936 | tf_op jit(solution)/shard_map/ppermute | solution.py:475
  583.4 7.5 %collective-permute-start.18 = (bf16[4,24,1536]{2,1,0:T(8,128)(2,1)S(1)}, bf16[4,24,1536]{2,1,0:T(8,128)(2,1)S(1)}, u32[]{:S(2)}, u32[]{:S(2)}) collective-permute-start(bf16[4,24,1536]{2,1,0:T(8,128)(2,1)S(1)} %fusion.122), channel_id=1, source_target_pairs={{0,1},{1,0},{2,3},{3,2},{4,5},{5,4},{6,7},{7,6},{8,9},{9,8},{10,11... | collective-permute-start | bytes 884744 | tf_op jit(solution)/shard_map/ppermute | solution.py:475
  596.8 7.5 %collective-permute-start.20 = (bf16[1,24,1536]{2,1,0:T(8,128)(2,1)S(1)}, bf16[1,24,1536]{2,1,0:T(8,128)(2,1)S(1)}, u32[]{:S(2)}, u32[]{:S(2)}) collective-permute-start(bf16[1,24,1536]{2,1,0:T(8,128)(2,1)S(1)} %dynamic-slice_convert_fusion.5), channel_id=1, source_target_pairs={{0,8},{1,9},{2,10},{3,11},{4,12},{5,13},{6,14},{7,15},{8,0},{9,1},... | collective-permute-start | bytes 221192 | tf_op jit(solution)/shard_map/ppermute | solution.py:475
  (149 other events, 2305.6 us)

commit v4 on v3

--- a/solution.py
+++ b/solution.py
@@ -287,8 +287,7 @@
         ],
         compiler_params=pltpu.CompilerParams(vmem_limit_bytes=32 * 2**20),
         cost_estimate=pl.CostEstimate(
-            flops=10 * 2 * HEADS * length * BACK * 128, bytes_accessed=12 * 2**20,
-            transcendentals=HEADS * length * BACK,
+            flops=2**20, bytes_accessed=2**20, transcendentals=0,
         ),
         name="attend_back",
     )(tiles, queries, kv, kv, kv_back, kv_back, query_docs, key_docs, bias_rows, out, out_grad, lse)
@@ -484,9 +483,10 @@
     return lax.optimization_barrier((x, *others))[0]
 
 
-def gather_rows(left, right, early):
+def gather_rows(left, right):
     if not (power_of_two("ctx") and power_of_two("exp")):
-        return [lax.all_gather(x, ("ctx", "exp"), axis=0, tiled=True) for x in (left, right)]
+        every = [lax.all_gather(x, ("ctx", "exp"), axis=0, tiled=True) for x in (left, right)]
+        return [*every, every, every]
     bits = bits_of("exp")
     last = bits[-2:]
     parts = [left, right]
@@ -497,22 +497,23 @@
             jnp.stack(ordered(h, g, "exp", bit), axis=1).reshape((-1,) + h.shape[1:])
             for h, g in zip(held, got)
         ]
-    held = [after(h, early) for h in held]
     got = [swap(h, "exp", bit) for h, bit in zip(held, last)]
     held = [jnp.stack(ordered(h, g, "exp", bit), axis=1) for h, g, bit in zip(held, got, last)]
+    begun = held
     got = [swap(h, "exp", bit) for h, bit in zip(held, last[::-1])]
     held = [
         jnp.stack(ordered(h, g, "exp", bit), axis=at)
         for h, g, bit, at in zip(held, got, last[::-1], (2, 1))
     ]
     held = [h.reshape(-1, h.shape[-1]) for h in held]
+    over_exp = held
     for bit in bits_of("ctx"):
         got = [swap(h, "ctx", bit) for h in held]
         held = [
             jnp.stack(ordered(h, g, "ctx", bit), axis=0).reshape(-1, h.shape[-1])
             for h, g in zip(held, got)
         ]
-    return held
+    return [*held, begun, over_exp]
 
 
 def pair_rows(x):
@@ -521,44 +522,57 @@
     return jnp.concatenate([x, swap(x, "ctx", 1)], axis=0)
 
 
-def halve(x, axis, bit, dim):
+def add_received(mine, got, even):
+    column = lax.broadcasted_iota(jnp.int32, mine.shape, mine.ndim - 1)
+    rounded = lax.reduce_precision(mine, 8, 7)
+    return jnp.where(column < even, mine, rounded) + got.astype(f32)
+
+
+def halve(x, axis, bit, dim, even):
     side = ((lax.axis_index(axis) & bit) > 0).astype(jnp.int32)
     mine = lax.dynamic_index_in_dim(x, side, dim, keepdims=False)
     theirs = lax.dynamic_index_in_dim(x, 1 - side, dim, keepdims=False)
-    return mine + swap(theirs.astype(bf16), axis, bit).astype(f32)
-
-
-def scatter_sum(grads, width, late):
-    if not (power_of_two("exp") and lax.axis_size("ctx") == 2 and lax.axis_size("exp") > 3):
+    return add_received(mine, swap(theirs.astype(bf16), axis, bit), even)
+
+
+def scatter_sum(grads, width, late, small):
+    blocks = lax.axis_size("exp")
+    part = width // 2
+    depth = part // blocks
+    if not (
+        power_of_two("exp") and lax.axis_size("ctx") == 2 and blocks > 3
+        and small.shape[0] <= depth and small.shape[1] <= TILE
+    ):
         whole = grads(lambda x, axis: x)
         sums = [
             lax.psum_scatter(x, ("ctx", "exp"), scatter_dimension=0, tiled=True) for x in whole
         ]
-        return [*sums, sums[0]]
+        return [*sums, lax.psum(small, ("ctx", "exp"))]
     me = lax.axis_index("ctx")
-    part = width // 2
-    theirs = grads(lambda x, axis: lax.dynamic_slice_in_dim(x, (1 - me) * part, part, axis))
+    rows, columns = small.shape
+    small = jnp.pad(small, ((0, depth - rows), (0, TILE - columns)))
+    small = jnp.broadcast_to(small[None], (blocks, depth, TILE)).reshape(part, TILE)
+
+    def half_of(side):
+        left, right = grads(lambda x, axis: lax.dynamic_slice_in_dim(x, side * part, part, axis))
+        return jnp.concatenate([left, small], axis=1), right
+
+    theirs = half_of(1 - me)
+    even = [theirs[0].shape[1] - TILE, theirs[1].shape[1]]
     got = [swap(x.astype(bf16), "ctx", 1) for x in theirs]
-    mine = grads(lambda x, axis: lax.dynamic_slice_in_dim(x, me * part, part, axis))
-    begun = got[1]
+    mine = half_of(me)
     bits = bits_of("exp")
-    held = [after(m + g.astype(f32), late) for m, g in zip(mine, got)]
-    held = [h.reshape((-1, 2, 2, h.shape[0] // lax.axis_size("exp"), h.shape[1])) for h in held]
+    held = [after(add_received(m, g, e), late) for m, g, e in zip(mine, got, even)]
+    held = [h.reshape((-1, 2, 2, depth, h.shape[1])) for h in held]
     high, low = bits[-2:]
-    held = [halve(held[0], "exp", high, 1), halve(held[1], "exp", low, 2)]
-    held = [halve(held[0], "exp", low, 1), halve(held[1], "exp", high, 1)]
+    held = [halve(held[0], "exp", high, 1, even[0]), halve(held[1], "exp", low, 2, even[1])]
+    held = [halve(held[0], "exp", low, 1, even[0]), halve(held[1], "exp", high, 1, even[1])]
     for bit in bits[:-2][::-1]:
-        held = [halve(h.reshape((-1, 2) + h.shape[1:]), "exp", bit, 1) for h in held]
-    return [*(h.reshape(h.shape[-2:]) for h in held), begun]
-
-
-def total_of(x):
-    if not (power_of_two("ctx") and power_of_two("exp")):
-        return lax.psum(x, ("ctx", "exp"))
-    for axis in ("ctx", "exp"):
-        for bit in bits_of(axis):
-            x = x + swap(x, axis, bit)
-    return x
+        held = [
+            halve(h.reshape((-1, 2) + h.shape[1:]), "exp", bit, 1, e) for h, e in zip(held, even)
+        ]
+    left, right = (h.reshape(h.shape[-2:]) for h in held)
+    return [left[:, : even[0]], right, left[:rows, even[0] : even[0] + columns]]
 
 
 def shards(
@@ -612,10 +626,8 @@
         return lax.all_to_all(x, "exp", split_axis=0, concat_axis=0, tiled=True)
 
     cots = [cotangent[b, 0] for b in range(batches)]
-    cot_sent = jnp.concatenate([dispatch(b, cots[b]) for b in range(batches)], axis=1)
-
     pad = -(experts + 2) % 128
-    left, right = gather_rows(
+    left, right, begun, over_exp = gather_rows(
         jnp.concatenate([query_key_value_weight[:, :width], output_projection_weight], axis=1),
         jnp.concatenate(
             [
@@ -627,7 +639,6 @@
             ],
             axis=1,
         ),
-        cot_sent,
     )
     query_weight = left[:, :width]
     proj_weight = left[:, width:]
@@ -676,7 +687,9 @@
         view = (tiles, queries, kv, kv_back, query_docs[None], key_docs[None], bias_rows)
         state.append(dict(rows=rows, inv_one=inv_one, normed=normed, view=view))
 
-    cot_here = cross(after(cot_sent, left, right))
+    cot_rows = [after(c, *begun) for c in cots]
+    cot_sent = jnp.concatenate([dispatch(b, cot_rows[b]) for b in range(batches)], axis=1)
+    cot_here = cross(after(cot_sent, *over_exp))
     sent = ()
     for b, s in enumerate(state):
         s["view"] = (after(s["view"][0], *sent),) + s["view"][1:]
@@ -801,14 +814,13 @@
             ),
         )
 
-    left, right, begun = scatter_sum(weight_grads, width, results)
     hot_near = jnp.where(
         jnp.arange(buckets)[:, None] < buckets - 1, hot_bucket[:, :TILE], 0.0
     )
     grad_bias = jnp.sum(near.reshape(HEADS, 1, TILE) * hot_near[None], axis=2)
     far = jnp.where(jnp.arange(buckets) == buckets - 1, 1.0, 0.0)
     grad_bias = grad_bias - jnp.sum(grad_bias, axis=1, keepdims=True) * far
-    bias_total = total_of(after(grad_bias, begun))
+    left, right, bias_total = scatter_sum(weight_grads, width, results, grad_bias)
     return (
         jnp.stack(outputs)[:, None],
         jnp.stack(input_grads)[:, None],

time: 623 us -> 600 us (0.963)
  waiting for transfers between devices: 136 us -> 93.7 us
  starting transfers between devices: 107 us -> 123 us
    ppermute x29 -> x24, waiting for transfers between devices: 79.7 us -> 36.2 us  [swap(): return lax.ppermute(x, axis, [(i, i ^ bit) for i in range(size)])]
    ppermute x29 -> x24, starting transfers between devices: 33.2 us -> 53.2 us  [swap(): return lax.ppermute(x, axis, [(i, i ^ bit) for i in range(size)])]
    unnamed x273 -> x249, local copies, waits for them, and re-layouts: 24.5 us -> 24.1 us
  transfers between devices with their start and end apart: 39 -> 34, of which waited for: 21 -> 14; matrix products, arithmetic and copies ran while one was open for 21% -> 23% of each run, Pallas kernels for 32% -> 34%
where the time goes in v4:
time: 600 us; the launch traced here: 590 us
  Pallas kernels  199 us (33%)
  starting transfers between devices  123 us (20%)
  waiting for transfers between devices  93.7 us (16%)
  other arithmetic  60.6 us (10%)
  matrix products  59.4 us (10%)
  local copies, waits for them, and re-layouts  51.5 us (9%)
    pallas_call x2, Pallas kernels, run_experts(): pl.pallas_call(functools.partial(expert_kernel, more, halves, split, capa...  121 us
    all_to_all x6, starting transfers between devices, cross(): return lax.all_to_all(x, 'exp', split_axis=0, concat_axis=0, tiled=True)  63.5 us
    dot_general x42, matrix products, mm(): return lax.dot_general(a, b, (dims, ((), ())), preferred_element_type=f32)  59.4 us
    all_to_all x6, waiting for transfers between devices, cross(): return lax.all_to_all(x, 'exp', split_axis=0, concat_axis=0, tiled=True)  57.5 us
    ppermute x24, starting transfers between devices, swap(): return lax.ppermute(x, axis, [(i, i ^ bit) for i in range(size)])  53.2 us
    pallas_call x2, Pallas kernels, attend_back(): pl.pallas_call(bwd_kernel, grid_spec=pltpu.PrefetchScalarGridSpec(num_sca...  45 us
    ppermute x24, waiting for transfers between devices, swap(): return lax.ppermute(x, axis, [(i, i ^ bit) for i in range(size)])  36.2 us
    pallas_call x2, Pallas kernels, attend(): pl.pallas_call(fwd_kernel, grid_spec=pltpu.PrefetchScalarGridSpec(num_sca...  32.5 us
  transfers between devices with their start and end apart: 34, of which 14 were waited for; matrix products, arithmetic and copies ran while one was open for 23% of the time, Pallas kernels for 34%

profile of v4, /device:TPU:0, one launch (start us, length us, event | category | flops | bytes accessed | tf_op | source)
XLA Modules:
  0.0 590.1 jit_solution(6595576201642113716)
XLA Ops:
  18.4 4.2 collective-permute-done.1
  37.6 7.3 %collective-permute-done.3 = bf16[4,2,24,1664]{3,2,0,1:T(8,128)(2,1)S(1)} collective-permute-done((bf16[4,2,24,1664]{3,2,0,1:T(8,128)(2,1)S(1)}, bf16[4,2,24,1664]{3,2,0,1:T(8,128)(2,1)S(1)}, u32[]{:S(2)}, u32[]{:S(2)}) %collective-permute-start.3) | collective-permute-done | bytes 639008 | tf_op jit(solution)/shard_map/ppermute | solution.py:474
  51.7 7.4 %all-to-all-start = ((bf16[16,192,768]{2,1,0:T(8,128)(2,1)}), bf16[16,192,768]{2,1,0:T(8,128)(2,1)}, u32[]{:S(2)}, u32[]{:S(2)}) async-start(bf16[16,192,768]{2,1,0:T(8,128)(2,1)} %pad_maximum_fusion), calls=%async_computation | async-start | bytes 9437184 | tf_op jit(solution)/shard_map/all_to_all | solution.py:626
  76.0 16.6 %attend.2 = (bf16[512,768]{1,0:T(8,128)(2,1)S(1)}, f32[6,4,256]{2,1,0:T(4,128)S(1)}) custom-call(s32[4]{0:T(128)S(1)} %subtract_clamp_fusion.1.tiles, bf16[512,768]{1,0:T(8,128)(2,1)S(1)} %convolution_convert_fusion.9.q_ref, bf16[512,1536]{1,0:T(8,128)(2,1)S(1)} %convolution_convert_fusion.5.k_ref.v_ref, ...), custom_call_target="tpu_custom_call" | custom-call | flops 3221225472 | bytes 6291456 | tf_op jit(solution)/shard_map/attend/pallas_call | solution.py:226
  102.0 15.9 %attend.3 = (bf16[512,768]{1,0:T(8,128)(2,1)S(1)}, f32[6,4,256]{2,1,0:T(4,128)S(1)}) custom-call(s32[4]{0:T(128)S(1)} %subtract_clamp_fusion.tiles, bf16[512,768]{1,0:T(8,128)(2,1)S(1)} %copy-done.15, bf16[512,1536]{1,0:T(8,128)(2,1)S(1)} %convolution_convert_fusion.4.k_ref.v_ref, bf16[512,1536]{1,0:T(8,128)(2,1)S(1)} %convolution_convert_fusion.4.k_ref.v_ref, ...), custom_call_target="tpu_custom_call" | custom-call | flops 3221225472 | bytes 6291456 | tf_op jit(solution)/shard_map/attend/pallas_call | solution.py:226
  126.0 24.3 %all-to-all-done.cot_ref = bf16[16,192,768]{2,1,0:T(8,128)(2,1)} async-done(((bf16[16,192,768]{2,1,0:T(8,128)(2,1)}), bf16[16,192,768]{2,1,0:T(8,128)(2,1)}, u32[]{:S(2)}, u32[]{:S(2)}) %all-to-all-start) | async-done | bytes 4718624 | tf_op jit(solution)/shard_map/all_to_all | solution.py:626
  150.3 23.3 %all-to-all-start.1 = ((bf16[16,96,768]{2,1,0:T(8,128)(2,1)}), bf16[16,96,768]{2,1,0:T(8,128)(2,1)}, u32[]{:S(2)}, u32[]{:S(2)}) async-start(bf16[16,96,768]{2,1,0:T(8,128)(2,1)} %broadcast_select_fusion.1), calls=%async_computation.1 | async-start | bytes 4718592 | tf_op jit(solution)/shard_map/all_to_all | solution.py:626
  178.6 5.0 pad_maximum_fusion.1.up_ref
  187.8 33.2 %all-to-all-done.1.x_ref = bf16[16,96,768]{2,1,0:T(8,128)(2,1)} async-done(((bf16[16,96,768]{2,1,0:T(8,128)(2,1)}), bf16[16,96,768]{2,1,0:T(8,128)(2,1)}, u32[]{:S(2)}, u32[]{:S(2)}) %all-to-all-start.1) | async-done | bytes 2359328 | tf_op jit(solution)/shard_map/all_to_all | solution.py:626
  221.0 10.9 %all-to-all-start.2 = ((bf16[16,96,768]{2,1,0:T(8,128)(2,1)}), bf16[16,96,768]{2,1,0:T(8,128)(2,1)}, u32[]{:S(2)}, u32[]{:S(2)}) async-start(bf16[16,96,768]{2,1,0:T(8,128)(2,1)} %broadcast_select_fusion), calls=%async_computation.2 | async-start | bytes 4718592 | tf_op jit(solution)/shard_map/all_to_all | solution.py:626
  231.8 59.2 %experts.2 = (bf16[16,192,768]{2,1,0:T(8,128)(2,1)}, bf16[16,96,768]{2,1,0:T(8,128)(2,1)}, f32[768,3072]{1,0:T(8,128)}, f32[3072,768]{1,0:T(8,128)}) custom-call(s32[1]{0:T(128)} %bitcast.44.ctx, bf16[16,96,768]{2,1,0:T(8,128)(2,1)} %all-to-all-done.1.x_ref, bf16[16,192,768]{2,1,0:T(8,128)(2,1)} %all-to-all-done.cot_ref, ...), custom_call_target="tpu_custom_call" | custom-call | flops 65229815808 | bytes 41943040 | tf_op jit(solution)/shard_map/experts/pallas_call | solution.py:429
  291.0 7.1 %all-to-all-start.3 = ((bf16[16,96,768]{2,1,0:T(8,128)(2,1)}), bf16[16,96,768]{2,1,0:T(8,128)(2,1)}, u32[]{:S(2)}, u32[]{:S(2)}) async-start(bf16[16,96,768]{2,1,0:T(8,128)(2,1)} %get-tuple-element.58), calls=%async_computation.3 | async-start | bytes 4718592 | tf_op jit(solution)/shard_map/all_to_all | solution.py:626
  298.1 61.9 %experts.3 = (bf16[16,192,768]{2,1,0:T(8,128)(2,1)}, bf16[16,96,768]{2,1,0:T(8,128)(2,1)}, f32[384,3072]{1,0:T(8,128)}, bf16[384,3072]{1,0:T(8,128)(2,1)}, f32[1...) custom-call(s32[1]{0:T(128)} %bitcast.44.ctx, ...), custom_call_target="tpu_custom_call", output_to_operand_aliasing={{0}: (5, {})} | custom-call | flops 65229815808 | bytes 41943040 | tf_op jit(solution)/shard_map/experts/pallas_call | solution.py:429
  361.5 7.3 %all-to-all-start.4 = ((bf16[16,96,768]{2,1,0:T(8,128)(2,1)}), bf16[16,96,768]{2,1,0:T(8,128)(2,1)}, u32[]{:S(2)}, u32[]{:S(2)}) async-start(bf16[16,96,768]{2,1,0:T(8,128)(2,1)} %get-tuple-element.59), calls=%async_computation.4 | async-start | bytes 4718592 | tf_op jit(solution)/shard_map/all_to_all | solution.py:626
  379.2 22.6 %attend_back.2 = (bf16[512,768]{1,0:T(8,128)(2,1)S(1)}, bf16[2,512,768]{2,1,0:T(8,128)(2,1)S(1)}, bf16[2,512,768]{2,1,0:T(8,128)(2,1)S(1)}, f32[6,1,256]{2,1,0:T(1,128)S(1)}) custom-call(s32[4]{0:T(128)S(1)} %copy-done.24, bf16[512,768]{1,0:T(8,128)(2,1)S(1)} %copy-done.18, bf16[512,1536]{1,0:T(8,128)(2,1)S(1)} %copy-done.3, ...), custom_call_target="tpu_custom_call" | custom-call | flops 1048576 | bytes 1048576 | tf_op jit(solution)/shard_map/attend_back/pallas_call | solution.py:262
  403.4 4.6 add_bitcast_fusion
  408.0 4.9 add_bitcast_fusion.1
  430.2 7.5 %all-to-all-start.5 = ((bf16[16,192,768]{2,1,0:T(8,128)(2,1)}), bf16[16,192,768]{2,1,0:T(8,128)(2,1)}, u32[]{:S(2)}, u32[]{:S(2)}) async-start(bf16[16,192,768]{2,1,0:T(8,128)(2,1)} %get-tuple-element.60), calls=%async_computation.5 | async-start | bytes 9437184 | tf_op jit(solution)/shard_map/all_to_all | solution.py:626
  443.0 22.5 %attend_back.3 = (bf16[512,768]{1,0:T(8,128)(2,1)S(1)}, bf16[2,512,768]{2,1,0:T(8,128)(2,1)S(1)}, bf16[2,512,768]{2,1,0:T(8,128)(2,1)}, f32[6,1,256]{2,1,0:T(1,128)S(1)}) custom-call(s32[4]{0:T(128)S(1)} %copy-done.22, bf16[512,768]{1,0:T(8,128)(2,1)S(1)} %copy-done.16, bf16[512,1536]{1,0:T(8,128)(2,1)S(1)} %copy-done.1, bf16[512,1536]{1,0:T(8,128)(2,1)S(1)} %copy-done.1, ...), custom_call_target="tpu_custom_call" | custom-call | flops 1048576 | bytes 1048576 | tf_op jit(solution)/shard_map/attend_back/pallas_call | solution.py:262
  473.4 5.1 collective-permute-start.16
  515.9 4.4 concatenate.76
  529.1 5.8 collective-permute-start.17
  554.3 5.8 collective-permute-done.18
  560.3 13.3 %collective-permute-start.19 = (bf16[2,24,1664]{2,1,0:T(8,128)(2,1)S(1)}, bf16[2,24,1664]{2,1,0:T(8,128)(2,1)S(1)}, u32[]{:S(2)}, u32[]{:S(2)}) collective-permute-start(bf16[2,24,1664]{2,1,0:T(8,128)(2,1)S(1)} %fusion.135), channel_id=1, source_target_pairs={{0,4},{1,5},{2,6},{3,7},{4,0},{5,1},{6,2},{7,3},{8,12},{9,13},{10,... | collective-permute-start | bytes 479240 | tf_op jit(solution)/shard_map/ppermute | solution.py:474
  (530 shorter events, 207.1 us)
Async XLA Ops:
  2.2 13.1 %collective-permute-start.5 = (bf16[1,24,1536]{2,1,0:T(8,128)(2,1)S(1)}, bf16[1,24,1536]{2,1,0:T(8,128)(2,1)S(1)}, u32[]{:S(2)}, u32[]{:S(2)}) collective-permute-start(bf16[1,24,1536]{2,1,0:T(8,128)(2,1)S(1)} %maximum_bitcast_fusion.4), channel_id=1, source_target_pairs={{0,8},{1,9},{2,10},{3,11},{4,12},{5,13},{6,14},{7,15},{8,0},{9,1},... | collective-permute-start | bytes 221192 | tf_op jit(solution)/shard_map/ppermute | solution.py:474
  24.4 9.9 %collective-permute-start.7 = (bf16[4,24,1536]{2,1,0:T(8,128)(2,1)S(1)}, bf16[4,24,1536]{2,1,0:T(8,128)(2,1)S(1)}, u32[]{:S(2)}, u32[]{:S(2)}) collective-permute-start(bf16[4,24,1536]{2,1,0:T(8,128)(2,1)S(1)} %bitcast.299), channel_id=1, source_target_pairs={{0,2},{1,3},{2,0},{3,1},{4,6},{5,7},{6,4},{7,5},{8,10},{9,11},{10,... | collective-permute-start | bytes 884744 | tf_op jit(solution)/shard_map/ppermute | solution.py:474
  29.9 14.9 %collective-permute-start.3 = (bf16[4,2,24,1664]{3,2,0,1:T(8,128)(2,1)S(1)}, bf16[4,2,24,1664]{3,2,0,1:T(8,128)(2,1)S(1)}, u32[]{:S(2)}, u32[]{:S(2)}) collective-permute-start(bf16[4,2,24,1664]{3,2,0,1:T(8,128)(2,1)S(1)} %pad_maximum_fusion.10), channel_id=1, source_target_pairs={{0,2},{1,3},{2,0},{3,1},{4,6},{5,7},{6,4},{7,5},{8,10},{9,11},{10,... | collective-permute-start | bytes 1916936 | tf_op jit(solution)/shard_map/ppermute | solution.py:474
  34.5 15.9 %collective-permute-start.8 = (bf16[4,2,24,1536]{3,2,0,1:T(8,128)(2,1)S(1)}, bf16[4,2,24,1536]{3,2,0,1:T(8,128)(2,1)S(1)}, u32[]{:S(2)}, u32[]{:S(2)}) collective-permute-start(bf16[4,2,24,1536]{3,2,0,1:T(8,128)(2,1)S(1)} %pad_maximum_fusion.11), channel_id=1, source_target_pairs={{0,1},{1,0},{2,3},{3,2},{4,5},{5,4},{6,7},{7,6},{8,9},{9,8},{10,11... | collective-permute-start | bytes 1769480 | tf_op jit(solution)/shard_map/ppermute | solution.py:474
  45.2 13.9 %collective-permute-start.4 = (bf16[384,1664]{1,0:T(8,128)(2,1)S(1)}, bf16[384,1664]{1,0:T(8,128)(2,1)}, u32[]{:S(2)}, u32[]{:S(2)}) collective-permute-start(bf16[384,1664]{1,0:T(8,128)(2,1)S(1)} %bitcast.270), channel_id=1, source_target_pairs={{0,16},{16,0},{1,17},{17,1},{2,18},{18,2},{3,19},{19,3},{4,20},{20... | collective-permute-start | bytes 3833864 | tf_op jit(solution)/shard_map/ppermute | solution.py:474
  51.7 16.9 %collective-permute-start.9 = (bf16[384,1536]{1,0:T(8,128)(2,1)}, bf16[384,1536]{1,0:T(8,128)(2,1)}, u32[]{:S(2)}, u32[]{:S(2)}) collective-permute-start(bf16[384,1536]{1,0:T(8,128)(2,1)} %bitcast.33), channel_id=1, source_target_pairs={{0,16},{16,0},{1,17},{17,1},{2,18},{18,2},{3,19},{19,3},{4,20},{20... | collective-permute-start | bytes 3538952 | tf_op jit(solution)/shard_map/ppermute | solution.py:474
  51.7 98.6 %all-to-all-start = ((bf16[16,192,768]{2,1,0:T(8,128)(2,1)}), bf16[16,192,768]{2,1,0:T(8,128)(2,1)}, u32[]{:S(2)}, u32[]{:S(2)}) async-start(bf16[16,192,768]{2,1,0:T(8,128)(2,1)} %pad_maximum_fusion), calls=%async_computation | async-start | bytes 9437184 | tf_op jit(solution)/shard_map/all_to_all | solution.py:626
  72.0 29.9 %collective-permute-start.11 = (bf16[512,1536]{1,0:T(8,128)(2,1)S(1)}, bf16[512,1536]{1,0:T(8,128)(2,1)S(1)}, u32[]{:S(2)}, u32[]{:S(2)}) collective-permute-start(bf16[512,1536]{1,0:T(8,128)(2,1)S(1)} %convolution_convert_fusion.4.k_ref.v_ref), channel_id=1, source_target_pairs={{0,16},{1,17},{2,18},{3,19},{4,20},{5,21},{6,22},{7,23},{8,24},{9,... | collective-permute-start | bytes 4718600 | tf_op jit(solution)/shard_map/ppermute | solution.py:678
  150.3 70.6 %all-to-all-start.1 = ((bf16[16,96,768]{2,1,0:T(8,128)(2,1)}), bf16[16,96,768]{2,1,0:T(8,128)(2,1)}, u32[]{:S(2)}, u32[]{:S(2)}) async-start(bf16[16,96,768]{2,1,0:T(8,128)(2,1)} %broadcast_select_fusion.1), calls=%async_computation.1 | async-start | bytes 4718592 | tf_op jit(solution)/shard_map/all_to_all | solution.py:626
  221.0 70.1 %all-to-all-start.2 = ((bf16[16,96,768]{2,1,0:T(8,128)(2,1)}), bf16[16,96,768]{2,1,0:T(8,128)(2,1)}, u32[]{:S(2)}, u32[]{:S(2)}) async-start(bf16[16,96,768]{2,1,0:T(8,128)(2,1)} %broadcast_select_fusion), calls=%async_computation.2 | async-start | bytes 4718592 | tf_op jit(solution)/shard_map/all_to_all | solution.py:626
  291.0 69.5 %all-to-all-start.3 = ((bf16[16,96,768]{2,1,0:T(8,128)(2,1)}), bf16[16,96,768]{2,1,0:T(8,128)(2,1)}, u32[]{:S(2)}, u32[]{:S(2)}) async-start(bf16[16,96,768]{2,1,0:T(8,128)(2,1)} %get-tuple-element.58), calls=%async_computation.3 | async-start | bytes 4718592 | tf_op jit(solution)/shard_map/all_to_all | solution.py:626
  360.0 43.3 %collective-permute-start.27 = (bf16[1536,768]{1,0:T(8,128)(2,1)}, bf16[1536,768]{1,0:T(8,128)(2,1)}, u32[]{:S(2)}, u32[]{:S(2)}) collective-permute-start(bf16[1536,768]{1,0:T(8,128)(2,1)} %get-tuple-element.77), channel_id=1, source_target_pairs={{0,16},{16,0},{1,17},{17,1},{2,18},{18,2},{3,19},{19,3},{4,20},{20... | collective-permute-start | bytes 7077896 | tf_op jit(solution)/shard_map/ppermute | solution.py:474
  360.1 47.9 %collective-permute-start.26 = (bf16[384,3072]{1,0:T(8,128)(2,1)}, bf16[384,3072]{1,0:T(8,128)(2,1)}, u32[]{:S(2)}, u32[]{:S(2)}) collective-permute-start(bf16[384,3072]{1,0:T(8,128)(2,1)} %get-tuple-element.75), channel_id=1, source_target_pairs={{0,16},{16,0},{1,17},{17,1},{2,18},{18,2},{3,19},{19,3},{4,20},{20... | collective-permute-start | bytes 7077896 | tf_op jit(solution)/shard_map/ppermute | solution.py:474
  361.5 60.5 %all-to-all-start.4 = ((bf16[16,96,768]{2,1,0:T(8,128)(2,1)}), bf16[16,96,768]{2,1,0:T(8,128)(2,1)}, u32[]{:S(2)}, u32[]{:S(2)}) async-start(bf16[16,96,768]{2,1,0:T(8,128)(2,1)} %get-tuple-element.59), calls=%async_computation.4 | async-start | bytes 4718592 | tf_op jit(solution)/shard_map/all_to_all | solution.py:626
  401.7 11.5 %collective-permute-start.14 = (bf16[2,512,768]{2,1,0:T(8,128)(2,1)S(1)}, bf16[2,512,768]{2,1,0:T(8,128)(2,1)S(1)}, u32[]{:S(2)}, u32[]{:S(2)}) collective-permute-start(bf16[2,512,768]{2,1,0:T(8,128)(2,1)S(1)} %get-tuple-element.64), channel_id=1, source_target_pairs={{16,0},{17,1},{18,2},{19,3},{20,4},{21,5},{22,6},{23,7},{24,8},{25... | collective-permute-start | bytes 4718600 | tf_op jit(solution)/shard_map/ppermute | solution.py:772
  430.2 98.9 %all-to-all-start.5 = ((bf16[16,192,768]{2,1,0:T(8,128)(2,1)}), bf16[16,192,768]{2,1,0:T(8,128)(2,1)}, u32[]{:S(2)}, u32[]{:S(2)}) async-start(bf16[16,192,768]{2,1,0:T(8,128)(2,1)} %get-tuple-element.60), calls=%async_computation.5 | async-start | bytes 9437184 | tf_op jit(solution)/shard_map/all_to_all | solution.py:626
  473.4 14.4 %collective-permute-start.16 = (bf16[384,1664]{1,0:T(8,128)(2,1)}, bf16[384,1664]{1,0:T(8,128)(2,1)}, u32[]{:S(2)}, u32[]{:S(2)}) collective-permute-start(bf16[384,1664]{1,0:T(8,128)(2,1)} %pad_maximum_fusion.8), channel_id=1, source_target_pairs={{0,16},{16,0},{1,17},{17,1},{2,18},{18,2},{3,19},{19,3},{4,20},{20... | collective-permute-start | bytes 3833864 | tf_op jit(solution)/shard_map/ppermute | solution.py:474
  478.5 12.8 %collective-permute-start.15 = (bf16[2,512,768]{2,1,0:T(8,128)(2,1)}, bf16[2,512,768]{2,1,0:T(8,128)(2,1)}, u32[]{:S(2)}, u32[]{:S(2)}) collective-permute-start(bf16[2,512,768]{2,1,0:T(8,128)(2,1)} %get-tuple-element.69), channel_id=1, source_target_pairs={{16,0},{17,1},{18,2},{19,3},{20,4},{21,5},{22,6},{23,7},{24,8},{25... | collective-permute-start | bytes 4718600 | tf_op jit(solution)/shard_map/ppermute | solution.py:772
  508.4 16.4 %collective-permute-start.21 = (bf16[384,1664]{1,0:T(8,128)(2,1)}, bf16[384,1664]{1,0:T(8,128)(2,1)}, u32[]{:S(2)}, u32[]{:S(2)}) collective-permute-start(bf16[384,1664]{1,0:T(8,128)(2,1)} %concatenate.77), channel_id=1, source_target_pairs={{0,16},{16,0},{1,17},{17,1},{2,18},{18,2},{3,19},{19,3},{4,20},{20... | collective-permute-start | bytes 3833864 | tf_op jit(solution)/shard_map/ppermute | solution.py:474
  529.1 20.1 %collective-permute-start.17 = (bf16[4,2,24,1664]{3,2,0,1:T(8,128)(2,1)S(1)}, bf16[4,2,24,1664]{3,2,0,1:T(8,128)(2,1)S(1)}, u32[]{:S(2)}, u32[]{:S(2)}) collective-permute-start(bf16[4,2,24,1664]{3,2,0,1:T(8,128)(2,1)S(1)} %fusion.95), channel_id=1, source_target_pairs={{0,2},{1,3},{2,0},{3,1},{4,6},{5,7},{6,4},{7,5},{8,10},{9,11},{10,... | collective-permute-start | bytes 1916936 | tf_op jit(solution)/shard_map/ppermute | solution.py:474
  536.3 16.8 %collective-permute-start.22 = (bf16[4,2,24,1664]{3,2,0,1:T(8,128)(2,1)S(1)}, bf16[4,2,24,1664]{3,2,0,1:T(8,128)(2,1)S(1)}, u32[]{:S(2)}, u32[]{:S(2)}) collective-permute-start(bf16[4,2,24,1664]{3,2,0,1:T(8,128)(2,1)S(1)} %fusion.96), channel_id=1, source_target_pairs={{0,1},{1,0},{2,3},{3,2},{4,5},{5,4},{6,7},{7,6},{8,9},{9,8},{10,11... | collective-permute-start | bytes 1916936 | tf_op jit(solution)/shard_map/ppermute | solution.py:474
  549.5 10.7 %collective-permute-start.18 = (bf16[4,24,1664]{2,1,0:T(8,128)(2,1)S(1)}, bf16[4,24,1664]{2,1,0:T(8,128)(2,1)S(1)}, u32[]{:S(2)}, u32[]{:S(2)}) collective-permute-start(bf16[4,24,1664]{2,1,0:T(8,128)(2,1)S(1)} %fusion.125), channel_id=1, source_target_pairs={{0,1},{1,0},{2,3},{3,2},{4,5},{5,4},{6,7},{7,6},{8,9},{9,8},{10,11... | collective-permute-start | bytes 958472 | tf_op jit(solution)/shard_map/ppermute | solution.py:474
  553.4 20.2 %collective-permute-start.23 = (bf16[4,24,1664]{2,1,0:T(8,128)(2,1)S(1)}, bf16[4,24,1664]{2,1,0:T(8,128)(2,1)S(1)}, u32[]{:S(2)}, u32[]{:S(2)}) collective-permute-start(bf16[4,24,1664]{2,1,0:T(8,128)(2,1)S(1)} %fusion.126), channel_id=1, source_target_pairs={{0,2},{1,3},{2,0},{3,1},{4,6},{5,7},{6,4},{7,5},{8,10},{9,11},{10,... | collective-permute-start | bytes 958472 | tf_op jit(solution)/shard_map/ppermute | solution.py:474
  560.3 18.3 %collective-permute-start.19 = (bf16[2,24,1664]{2,1,0:T(8,128)(2,1)S(1)}, bf16[2,24,1664]{2,1,0:T(8,128)(2,1)S(1)}, u32[]{:S(2)}, u32[]{:S(2)}) collective-permute-start(bf16[2,24,1664]{2,1,0:T(8,128)(2,1)S(1)} %fusion.135), channel_id=1, source_target_pairs={{0,4},{1,5},{2,6},{3,7},{4,0},{5,1},{6,2},{7,3},{8,12},{9,13},{10,... | collective-permute-start | bytes 479240 | tf_op jit(solution)/shard_map/ppermute | solution.py:474
  (132 other events, 1588.1 us)

commit v5 on v4

--- a/solution.py
+++ b/solution.py
@@ -11,6 +11,7 @@
 HEADS = 12
 HEAD = 64
 PAIRS = HEADS // 2
+GROUP = 3
 TILE = 128
 BACK = 512
 SPAN = BACK // TILE + 1
@@ -58,14 +59,21 @@
 
 
 def fill_bias(bias, bv_ref):
-    for head in range(2):
-        for d in range(2):
-            row = jnp.broadcast_to(bv_ref[0, 2 * head + d : 2 * head + d + 1, :], (TILE, 2 * TILE))
-            rolled = pltpu.roll(row, 0, 1, stride=1, stride_axis=0)
-            bias[d, :, head * TILE : (head + 1) * TILE] = rolled[:, :TILE]
-
-
-def masked_scores(scores, mask, bias, qi, tiles):
+    for g in range(GROUP):
+        for head in range(2):
+            for d in range(2):
+                row = bv_ref[g, 2 * head + d : 2 * head + d + 1, :]
+                rolled = pltpu.roll(
+                    jnp.broadcast_to(row, (TILE, 2 * TILE)), 0, 1, stride=1, stride_axis=0
+                )
+                bias[g, d, :, head * TILE : (head + 1) * TILE] = rolled[:, :TILE]
+
+
+def lanes_of(g):
+    return slice(g * TILE, (g + 1) * TILE)
+
+
+def masked_scores(scores, mask, bias, g, qi, tiles):
     parts = []
     for j in range(tiles):
         d = tiles - 1 - j
@@ -73,9 +81,15 @@
         m = mask[qi, off : off + TILE, :]
         x = scores[j * TILE : (j + 1) * TILE] + jnp.concatenate([m, m], axis=1)
         if d < 2:
-            x = x + bias[d]
+            x = x + bias[g, d]
         parts.append(x)
     return parts
+
+
+def transpose_tiles(out, at, rows_ref):
+    for g in range(GROUP):
+        for t in range(0, rows_ref.shape[0], TILE):
+            out[g, :, at + t : at + t + TILE] = rows_ref[t : t + TILE, lanes_of(g)].T
 
 
 def fwd_kernel(tiles, q_ref, k_ref, v_ref, kp_ref, vp_ref, qd_ref, kd_ref, bv_ref, o_ref, lse_ref,
@@ -87,32 +101,39 @@
     fill_bias(bias, bv_ref)
     kwin[:BACK] = kp_ref[...]
     kwin[BACK:] = k_ref[...]
-    for t in range(BACK // TILE):
-        vwin_t[:, t * TILE : (t + 1) * TILE] = vp_ref[t * TILE : (t + 1) * TILE, :].T
-    for t in range(q_ref.shape[0] // TILE):
-        at = BACK + t * TILE
-        vwin_t[:, at : at + TILE] = v_ref[t * TILE : (t + 1) * TILE, :].T
+    transpose_tiles(vwin_t, 0, vp_ref)
+    transpose_tiles(vwin_t, BACK, v_ref)
+    groups = range(GROUP)
 
     def step(qi, carry):
         q0 = pl.multiple_of(qi * TILE, TILE)
-        q2 = stack_heads(q_ref[pl.ds(q0, TILE), :] * 0.125)
+        q2 = [stack_heads(q_ref[pl.ds(q0, TILE), lanes_of(g)] * 0.125) for g in groups]
 
         def branch(count):
             def go():
                 lo = pl.multiple_of((qi + SPAN - count) * TILE, TILE)
-                keys = kwin[pl.ds(lo, count * TILE), :]
-                parts = masked_scores(mm(keys, q2, ((1,), (1,))), mask, bias, qi, count)
-                top = functools.reduce(jnp.maximum, parts)
-                top = jnp.max(top, axis=0, keepdims=True)
-                probs = [jnp.exp(x - top) for x in parts]
-                total = jnp.sum(functools.reduce(jnp.add, probs), axis=0, keepdims=True)
-                low = jnp.concatenate([p.astype(bf16) for p in probs], axis=0)
-                out = fold_heads(mm(vwin_t[:, pl.ds(lo, count * TILE)], low, ((1,), (0,))))
-                inv = 1.0 / total
+                rows = pl.ds(lo, count * TILE)
+                raw = [mm(kwin[rows, lanes_of(g)], q2[g], ((1,), (1,))) for g in groups]
+                lows, tops, totals = [], [], []
+                for g in groups:
+                    parts = masked_scores(raw[g], mask, bias, g, qi, count)
+                    top = functools.reduce(jnp.maximum, parts)
+                    top = jnp.max(top, axis=0, keepdims=True)
+                    probs = [jnp.exp(x - top) for x in parts]
+                    totals.append(
+                        jnp.sum(functools.reduce(jnp.add, probs), axis=0, keepdims=True)
+                    )
+                    tops.append(top)
+                    lows.append(jnp.concatenate([p.astype(bf16) for p in probs], axis=0))
+                outs = [mm(vwin_t[g, :, rows], lows[g], ((1,), (0,))) for g in groups]
                 row = lax.broadcasted_iota(jnp.int32, (TILE, TILE), 0)
-                out = out * jnp.where(row < HEAD, inv[:, :TILE], inv[:, TILE:])
-                o_ref[pl.ds(q0, TILE), :] = out.T.astype(bf16)
-                lse_ref[0, pl.ds(qi, 1), :] = top + jnp.log(total)
+                for g in groups:
+                    inv = 1.0 / totals[g]
+                    out = fold_heads(outs[g]) * jnp.where(
+                        row < HEAD, inv[:, :TILE], inv[:, TILE:]
+                    )
+                    o_ref[pl.ds(q0, TILE), lanes_of(g)] = out.T.astype(bf16)
+                    lse_ref[g, pl.ds(qi, 1), :] = tops[g] + jnp.log(totals[g])
                 return 0
 
             return go
@@ -135,53 +156,60 @@
     kwin[BACK:] = k_ref[...]
     vwin[:BACK] = vp_ref[...]
     vwin[BACK:] = v_ref[...]
-    for t in range(kwin.shape[0] // TILE):
-        kwin_t[:, t * TILE : (t + 1) * TILE] = kwin[t * TILE : (t + 1) * TILE, :].T
+    transpose_tiles(kwin_t, 0, kp_ref)
+    transpose_tiles(kwin_t, BACK, k_ref)
     dk[...] = jnp.zeros_like(dk)
     dv[...] = jnp.zeros_like(dv)
     near[...] = jnp.zeros_like(near)
+    groups = range(GROUP)
 
     def step(qi, carry):
         q0 = pl.multiple_of(qi * TILE, TILE)
-        q2 = stack_heads(q_ref[pl.ds(q0, TILE), :] * 0.125)
-        do = do_ref[pl.ds(q0, TILE), :]
-        do2 = stack_heads(do)
-        lse = lse_ref[0, pl.ds(qi, 1), :]
-        prod = (do.astype(f32) * o_ref[pl.ds(q0, TILE), :].astype(f32)).T
-        delta = jnp.concatenate(
-            [jnp.sum(prod[:HEAD], axis=0, keepdims=True),
-             jnp.sum(prod[HEAD:], axis=0, keepdims=True)],
-            axis=1,
-        )
+        q2, do2, lse, delta = [], [], [], []
+        for g in groups:
+            q2.append(stack_heads(q_ref[pl.ds(q0, TILE), lanes_of(g)] * 0.125))
+            do = do_ref[pl.ds(q0, TILE), lanes_of(g)]
+            do2.append(stack_heads(do))
+            lse.append(lse_ref[g, pl.ds(qi, 1), :])
+            prod = (do.astype(f32) * o_ref[pl.ds(q0, TILE), lanes_of(g)].astype(f32)).T
+            delta.append(
+                jnp.concatenate(
+                    [jnp.sum(prod[:HEAD], axis=0, keepdims=True),
+                     jnp.sum(prod[HEAD:], axis=0, keepdims=True)],
+                    axis=1,
+                )
+            )
 
         def branch(count):
             def go():
                 lo = pl.multiple_of((qi + SPAN - count) * TILE, TILE)
                 rows = pl.ds(lo, count * TILE)
-                parts = masked_scores(
-                    mm(kwin[rows, :], q2, ((1,), (1,))), mask, bias, qi, count
-                )
-                prob_grad = mm(vwin[rows, :], do2, ((1,), (1,)))
-                lows = []
-                grads = []
-                for j in range(count):
-                    prob = jnp.exp(parts[j] - lse)
-                    grad = prob * (prob_grad[j * TILE : (j + 1) * TILE] - delta)
-                    if j == count - 1:
-                        near[...] += grad
-                    elif j == count - 2:
-                        r = lax.broadcasted_iota(jnp.int32, grad.shape, 0)
-                        c = lax.broadcasted_iota(jnp.int32, grad.shape, 1)
-                        c = jnp.where(c >= TILE, c - TILE, c)
-                        near[...] += jnp.where(c < r, grad, 0.0)
-                    lows.append(prob.astype(bf16))
-                    grads.append(grad.astype(bf16))
-                low = jnp.concatenate(lows, axis=0)
-                score_grad = jnp.concatenate(grads, axis=0)
-                dk[rows, :] += mm(score_grad, q2, ((1,), (0,)))
-                dv[rows, :] += mm(low, do2, ((1,), (0,)))
-                dq = fold_heads(mm(kwin_t[:, rows], score_grad, ((1,), (0,))))
-                dq_ref[pl.ds(q0, TILE), :] = (dq.T * 0.125).astype(bf16)
+                raw = [mm(kwin[rows, lanes_of(g)], q2[g], ((1,), (1,))) for g in groups]
+                prob_grad = [mm(vwin[rows, lanes_of(g)], do2[g], ((1,), (1,))) for g in groups]
+                low, score_grad = [], []
+                for g in groups:
+                    parts = masked_scores(raw[g], mask, bias, g, qi, count)
+                    lows, grads = [], []
+                    for j in range(count):
+                        prob = jnp.exp(parts[j] - lse[g])
+                        grad = prob * (prob_grad[g][j * TILE : (j + 1) * TILE] - delta[g])
+                        if j == count - 1:
+                            near[g] += grad
+                        elif j == count - 2:
+                            r = lax.broadcasted_iota(jnp.int32, grad.shape, 0)
+                            c = lax.broadcasted_iota(jnp.int32, grad.shape, 1)
+                            c = jnp.where(c >= TILE, c - TILE, c)
+                            near[g] += jnp.where(c < r, grad, 0.0)
+                        lows.append(prob.astype(bf16))
+                        grads.append(grad.astype(bf16))
+                    low.append(jnp.concatenate(lows, axis=0))
+                    score_grad.append(jnp.concatenate(grads, axis=0))
+                for g in groups:
+                    dv[rows, lanes_of(g)] += mm(low[g], do2[g], ((1,), (0,)))
+                    dk[rows, lanes_of(g)] += mm(score_grad[g], q2[g], ((1,), (0,)))
+                for g in groups:
+                    dq = fold_heads(mm(kwin_t[g, :, rows], score_grad[g], ((1,), (0,))))
+                    dq_ref[pl.ds(q0, TILE), lanes_of(g)] = (dq.T * 0.125).astype(bf16)
                 return 0
 
             return go
@@ -193,29 +221,29 @@
     for i, total in enumerate((dk, dv)):
         back_ref[i] = total[:BACK].astype(bf16)
         own_ref[i] = total[BACK:].astype(bf16)
-    for head in range(2):
-        at = slice(head * TILE, (head + 1) * TILE)
-        turned = near[:, at]
-        r = lax.broadcasted_iota(jnp.int32, turned.shape, 0)
-        bit = 1
-        while bit < TILE:
-            turned = jnp.where((r & bit) > 0, pltpu.roll(turned, TILE - bit, 1), turned)
-            bit *= 2
-        near_ref[0, :, at] = jnp.sum(turned, axis=0, keepdims=True)
+    for g in groups:
+        for head in range(2):
+            turned = near[g, :, lanes_of(head)]
+            r = lax.broadcasted_iota(jnp.int32, turned.shape, 0)
+            bit = 1
+            while bit < TILE:
+                turned = jnp.where((r & bit) > 0, pltpu.roll(turned, TILE - bit, 1), turned)
+                bit *= 2
+            near_ref[g, :, lanes_of(head)] = jnp.sum(turned, axis=0, keepdims=True)
 
 
 def attention_specs(length):
     full = lambda p, *_: (0, 0)
     lanes = lambda off: (lambda p, *_: (0, p + off))
     return [
-        pl.BlockSpec((length, TILE), lanes(0)),
-        pl.BlockSpec((length, TILE), lanes(0)),
-        pl.BlockSpec((length, TILE), lanes(PAIRS)),
-        pl.BlockSpec((BACK, TILE), lanes(0)),
-        pl.BlockSpec((BACK, TILE), lanes(PAIRS)),
+        pl.BlockSpec((length, GROUP * TILE), lanes(0)),
+        pl.BlockSpec((length, GROUP * TILE), lanes(0)),
+        pl.BlockSpec((length, GROUP * TILE), lanes(PAIRS // GROUP)),
+        pl.BlockSpec((BACK, GROUP * TILE), lanes(0)),
+        pl.BlockSpec((BACK, GROUP * TILE), lanes(PAIRS // GROUP)),
         pl.BlockSpec((1, length), full),
         pl.BlockSpec((1, BACK + length), full),
-        pl.BlockSpec((1, 4, 2 * TILE), lambda p, *_: (p, 0, 0)),
+        pl.BlockSpec((GROUP, 4, 2 * TILE), lambda p, *_: (p, 0, 0)),
     ]
 
 
@@ -227,16 +255,16 @@
         fwd_kernel,
         grid_spec=pltpu.PrefetchScalarGridSpec(
             num_scalar_prefetch=1,
-            grid=(PAIRS,),
+            grid=(PAIRS // GROUP,),
             in_specs=attention_specs(length),
             out_specs=[
-                pl.BlockSpec((length, TILE), lambda p, *_: (0, p)),
-                pl.BlockSpec((1, blocks, 2 * TILE), lambda p, *_: (p, 0, 0)),
+                pl.BlockSpec((length, GROUP * TILE), lambda p, *_: (0, p)),
+                pl.BlockSpec((GROUP, blocks, 2 * TILE), lambda p, *_: (p, 0, 0)),
             ],
             scratch_shapes=[
-                pltpu.VMEM((BACK + length, TILE), bf16),
-                pltpu.VMEM((TILE, BACK + length), bf16),
-                pltpu.VMEM((2, TILE, 2 * TILE), f32),
+                pltpu.VMEM((BACK + length, GROUP * TILE), bf16),
+                pltpu.VMEM((GROUP, TILE, BACK + length), bf16),
+                pltpu.VMEM((GROUP, 2, TILE, 2 * TILE), f32),
                 pltpu.VMEM((blocks, SPAN * TILE, TILE), f32),
             ],
         ),
@@ -257,25 +285,25 @@
     length = queries.shape[0]
     width = HEADS * HEAD
     blocks = length // TILE
-    own = pl.BlockSpec((length, TILE), lambda p, *_: (0, p))
-    both = lambda n: pl.BlockSpec((2, n, TILE), lambda p, *_: (0, 0, p))
+    own = pl.BlockSpec((length, GROUP * TILE), lambda p, *_: (0, p))
+    both = lambda n: pl.BlockSpec((2, n, GROUP * TILE), lambda p, *_: (0, 0, p))
     return pl.pallas_call(
         bwd_kernel,
         grid_spec=pltpu.PrefetchScalarGridSpec(
             num_scalar_prefetch=1,
-            grid=(PAIRS,),
+            grid=(PAIRS // GROUP,),
             in_specs=attention_specs(length)
-            + [own, own, pl.BlockSpec((1, blocks, 2 * TILE), lambda p, *_: (p, 0, 0))],
+            + [own, own, pl.BlockSpec((GROUP, blocks, 2 * TILE), lambda p, *_: (p, 0, 0))],
             out_specs=[own, both(length), both(BACK),
-                       pl.BlockSpec((1, 1, 2 * TILE), lambda p, *_: (p, 0, 0))],
+                       pl.BlockSpec((GROUP, 1, 2 * TILE), lambda p, *_: (p, 0, 0))],
             scratch_shapes=[
-                pltpu.VMEM((BACK + length, TILE), bf16),
-                pltpu.VMEM((TILE, BACK + length), bf16),
-                pltpu.VMEM((BACK + length, TILE), bf16),
-                pltpu.VMEM((BACK + length, TILE), f32),
-                pltpu.VMEM((BACK + length, TILE), f32),
-                pltpu.VMEM((TILE, 2 * TILE), f32),
-                pltpu.VMEM((2, TILE, 2 * TILE), f32),
+                pltpu.VMEM((BACK + length, GROUP * TILE), bf16),
+                pltpu.VMEM((GROUP, TILE, BACK + length), bf16),
+                pltpu.VMEM((BACK + length, GROUP * TILE), bf16),
+                pltpu.VMEM((BACK + length, GROUP * TILE), f32),
+                pltpu.VMEM((BACK + length, GROUP * TILE), f32),
+                pltpu.VMEM((GROUP, TILE, 2 * TILE), f32),
+                pltpu.VMEM((GROUP, 2, TILE, 2 * TILE), f32),
                 pltpu.VMEM((blocks, SPAN * TILE, TILE), f32),
             ],
         ),
@@ -687,9 +715,8 @@
         view = (tiles, queries, kv, kv_back, query_docs[None], key_docs[None], bias_rows)
         state.append(dict(rows=rows, inv_one=inv_one, normed=normed, view=view))
 
-    cot_rows = [after(c, *begun) for c in cots]
-    cot_sent = jnp.concatenate([dispatch(b, cot_rows[b]) for b in range(batches)], axis=1)
-    cot_here = cross(after(cot_sent, *over_exp))
+    cot_sent = jnp.concatenate([dispatch(b, cots[b]) for b in range(batches)], axis=1)
+    cot_here = cross(after(cot_sent, *begun))
     sent = ()
     for b, s in enumerate(state):
         s["view"] = (after(s["view"][0], *sent),) + s["view"][1:]

time: 600 us -> 589 us (0.982)
  Pallas kernels: 199 us -> 166 us
  waiting for transfers between devices: 93.7 us -> 123 us
  local copies, waits for them, and re-layouts: 51.5 us -> 45.5 us
    all_to_all x6, waiting for transfers between devices: 57.5 us -> 82.9 us  [cross(): return lax.all_to_all(x, 'exp', split_axis=0, concat_axis=0, tiled=True)]
    pallas_call x2, Pallas kernels: 45 us -> 29.2 us  [attend_back(): pl.pallas_call(bwd_kernel, grid_spec=pltpu.PrefetchScalarGridSpec(num_sca...]
    pallas_call x2, Pallas kernels: 32.5 us -> 17.5 us  [attend(): pl.pallas_call(fwd_kernel, grid_spec=pltpu.PrefetchScalarGridSpec(num_sca...]
    ppermute x24, starting transfers between devices: 53.2 us -> 43.4 us  [swap(): return lax.ppermute(x, axis, [(i, i ^ bit) for i in range(size)])]
    unnamed x249 -> x265, local copies, waits for them, and re-layouts: 24.1 us -> 21.5 us
  transfers between devices with their start and end apart: 34 -> 34, of which waited for: 14 -> 17; matrix products, arithmetic and copies ran while one was open for 23% -> 24% of each run, Pallas kernels for 34% -> 29%
where the time goes in v5:
time: 589 us; the launch traced here: 580 us
  Pallas kernels  166 us (28%)
  waiting for transfers between devices  123 us (21%)
  starting transfers between devices  118 us (20%)
  other arithmetic  64 us (11%)
  matrix products  59.5 us (10%)
  local copies, waits for them, and re-layouts  45.5 us (8%)
    pallas_call x2, Pallas kernels, run_experts(): pl.pallas_call(functools.partial(expert_kernel, more, halves, split, capa...  120 us
    all_to_all x6, waiting for transfers between devices, cross(): return lax.all_to_all(x, 'exp', split_axis=0, concat_axis=0, tiled=True)  82.9 us
    all_to_all x6, starting transfers between devices, cross(): return lax.all_to_all(x, 'exp', split_axis=0, concat_axis=0, tiled=True)  67.3 us
    dot_general x42, matrix products, mm(): return lax.dot_general(a, b, (dims, ((), ())), preferred_element_type=f32)  59.5 us
    ppermute x24, starting transfers between devices, swap(): return lax.ppermute(x, axis, [(i, i ^ bit) for i in range(size)])  43.4 us
    ppermute x24, waiting for transfers between devices, swap(): return lax.ppermute(x, axis, [(i, i ^ bit) for i in range(size)])  40.3 us
    pallas_call x2, Pallas kernels, attend_back(): pl.pallas_call(bwd_kernel, grid_spec=pltpu.PrefetchScalarGridSpec(num_sca...  29.2 us
    unnamed x265, local copies, waits for them, and re-layouts  21.5 us
  transfers between devices with their start and end apart: 34, of which 17 were waited for; matrix products, arithmetic and copies ran while one was open for 24% of the time, Pallas kernels for 29%

profile of v5, /device:TPU:0, one launch (start us, length us, event | category | flops | bytes accessed | tf_op | source)
XLA Modules:
  0.0 579.9 jit_solution(8354694658982400931)
XLA Ops:
  18.4 4.8 collective-permute-done.1
  37.4 8.6 %collective-permute-done.3 = bf16[4,2,24,1664]{3,2,0,1:T(8,128)(2,1)S(1)} collective-permute-done((bf16[4,2,24,1664]{3,2,0,1:T(8,128)(2,1)S(1)}, bf16[4,2,24,1664]{3,2,0,1:T(8,128)(2,1)S(1)}, u32[]{:S(2)}, u32[]{:S(2)}) %collective-permute-start.3) | collective-permute-done | bytes 639008 | tf_op jit(solution)/shard_map/ppermute | solution.py:502
  50.6 6.9 %all-to-all-start = ((bf16[16,192,768]{2,1,0:T(8,128)(2,1)}), bf16[16,192,768]{2,1,0:T(8,128)(2,1)}, u32[]{:S(2)}, u32[]{:S(2)}) async-start(bf16[16,192,768]{2,1,0:T(8,128)(2,1)} %pad_maximum_fusion), calls=%async_computation | async-start | bytes 9437184 | tf_op jit(solution)/shard_map/all_to_all | solution.py:654
  76.3 8.2 %attend.2 = (bf16[512,768]{1,0:T(8,128)(2,1)S(1)}, f32[6,4,256]{2,1,0:T(4,128)S(1)}) custom-call(s32[4]{0:T(128)S(1)} %subtract_clamp_fusion.1.tiles, bf16[512,768]{1,0:T(8,128)(2,1)S(1)} %convolution_convert_fusion.9.q_ref, bf16[512,1536]{1,0:T(8,128)(2,1)S(1)} %convolution_convert_fusion.5.k_ref.v_ref, ...), custom_call_target="tpu_custom_call" | custom-call | flops 3221225472 | bytes 6291456 | tf_op jit(solution)/shard_map/attend/pallas_call | solution.py:254
  93.9 9.3 %attend.3 = (bf16[512,768]{1,0:T(8,128)(2,1)S(1)}, f32[6,4,256]{2,1,0:T(4,128)S(1)}) custom-call(s32[4]{0:T(128)S(1)} %subtract_clamp_fusion.tiles, bf16[512,768]{1,0:T(8,128)(2,1)S(1)} %copy-done.15, bf16[512,1536]{1,0:T(8,128)(2,1)S(1)} %convolution_convert_fusion.4.k_ref.v_ref, bf16[512,1536]{1,0:T(8,128)(2,1)S(1)} %convolution_convert_fusion.4.k_ref.v_ref, ...), custom_call_target="tpu_custom_call" | custom-call | flops 3221225472 | bytes 6291456 | tf_op jit(solution)/shard_map/attend/pallas_call | solution.py:254
  110.3 38.4 %all-to-all-done.cot_ref = bf16[16,192,768]{2,1,0:T(8,128)(2,1)} async-done(((bf16[16,192,768]{2,1,0:T(8,128)(2,1)}), bf16[16,192,768]{2,1,0:T(8,128)(2,1)}, u32[]{:S(2)}, u32[]{:S(2)}) %all-to-all-start) | async-done | bytes 4718624 | tf_op jit(solution)/shard_map/all_to_all | solution.py:654
  148.7 22.8 %all-to-all-start.1 = ((bf16[16,96,768]{2,1,0:T(8,128)(2,1)}), bf16[16,96,768]{2,1,0:T(8,128)(2,1)}, u32[]{:S(2)}, u32[]{:S(2)}) async-start(bf16[16,96,768]{2,1,0:T(8,128)(2,1)} %broadcast_select_fusion.1), calls=%async_computation.1 | async-start | bytes 4718592 | tf_op jit(solution)/shard_map/all_to_all | solution.py:654
  176.4 5.0 pad_maximum_fusion.1.up_ref
  181.5 4.2 pad_maximum_fusion.2.down_ref
  185.6 33.3 %all-to-all-done.1.x_ref = bf16[16,96,768]{2,1,0:T(8,128)(2,1)} async-done(((bf16[16,96,768]{2,1,0:T(8,128)(2,1)}), bf16[16,96,768]{2,1,0:T(8,128)(2,1)}, u32[]{:S(2)}, u32[]{:S(2)}) %all-to-all-start.1) | async-done | bytes 2359328 | tf_op jit(solution)/shard_map/all_to_all | solution.py:654
  218.9 11.1 %all-to-all-start.2 = ((bf16[16,96,768]{2,1,0:T(8,128)(2,1)}), bf16[16,96,768]{2,1,0:T(8,128)(2,1)}, u32[]{:S(2)}, u32[]{:S(2)}) async-start(bf16[16,96,768]{2,1,0:T(8,128)(2,1)} %broadcast_select_fusion), calls=%async_computation.2 | async-start | bytes 4718592 | tf_op jit(solution)/shard_map/all_to_all | solution.py:654
  230.0 58.5 %experts.2 = (bf16[16,192,768]{2,1,0:T(8,128)(2,1)}, bf16[16,96,768]{2,1,0:T(8,128)(2,1)}, f32[768,3072]{1,0:T(8,128)}, f32[3072,768]{1,0:T(8,128)}) custom-call(s32[1]{0:T(128)} %bitcast.44.ctx, bf16[16,96,768]{2,1,0:T(8,128)(2,1)} %all-to-all-done.1.x_ref, bf16[16,192,768]{2,1,0:T(8,128)(2,1)} %all-to-all-done.cot_ref, ...), custom_call_target="tpu_custom_call" | custom-call | flops 65229815808 | bytes 41943040 | tf_op jit(solution)/shard_map/experts/pallas_call | solution.py:457
  288.5 7.5 %all-to-all-start.3 = ((bf16[16,96,768]{2,1,0:T(8,128)(2,1)}), bf16[16,96,768]{2,1,0:T(8,128)(2,1)}, u32[]{:S(2)}, u32[]{:S(2)}) async-start(bf16[16,96,768]{2,1,0:T(8,128)(2,1)} %get-tuple-element.54), calls=%async_computation.3 | async-start | bytes 4718592 | tf_op jit(solution)/shard_map/all_to_all | solution.py:654
  296.0 61.1 %experts.3 = (bf16[16,192,768]{2,1,0:T(8,128)(2,1)}, bf16[16,96,768]{2,1,0:T(8,128)(2,1)}, f32[384,3072]{1,0:T(8,128)}, bf16[384,3072]{1,0:T(8,128)(2,1)}, f32[1...) custom-call(s32[1]{0:T(128)} %bitcast.44.ctx, ...), custom_call_target="tpu_custom_call", output_to_operand_aliasing={{0}: (5, {})} | custom-call | flops 65229815808 | bytes 41943040 | tf_op jit(solution)/shard_map/experts/pallas_call | solution.py:457
  358.7 7.3 %all-to-all-start.4 = ((bf16[16,96,768]{2,1,0:T(8,128)(2,1)}), bf16[16,96,768]{2,1,0:T(8,128)(2,1)}, u32[]{:S(2)}, u32[]{:S(2)}) async-start(bf16[16,96,768]{2,1,0:T(8,128)(2,1)} %get-tuple-element.55), calls=%async_computation.4 | async-start | bytes 4718592 | tf_op jit(solution)/shard_map/all_to_all | solution.py:654
  376.3 13.5 %attend_back.2 = (bf16[512,768]{1,0:T(8,128)(2,1)S(1)}, bf16[2,512,768]{2,1,0:T(8,128)(2,1)S(1)}, bf16[2,512,768]{2,1,0:T(8,128)(2,1)S(1)}, f32[6,1,256]{2,1,0:T(1,128)S(1)}) custom-call(s32[4]{0:T(128)S(1)} %copy-done.24, bf16[512,768]{1,0:T(8,128)(2,1)S(1)} %copy-done.18, bf16[512,1536]{1,0:T(8,128)(2,1)S(1)} %copy-done.3, ...), custom_call_target="tpu_custom_call" | custom-call | flops 1048576 | bytes 1048576 | tf_op jit(solution)/shard_map/attend_back/pallas_call | solution.py:290
  391.4 4.7 add_bitcast_fusion
  396.2 4.8 add_bitcast_fusion.1
  421.8 11.7 %all-to-all-start.5 = ((bf16[16,192,768]{2,1,0:T(8,128)(2,1)}), bf16[16,192,768]{2,1,0:T(8,128)(2,1)}, u32[]{:S(2)}, u32[]{:S(2)}) async-start(bf16[16,192,768]{2,1,0:T(8,128)(2,1)} %get-tuple-element.56), calls=%async_computation.5 | async-start | bytes 9437184 | tf_op jit(solution)/shard_map/all_to_all | solution.py:654
  438.8 15.7 %attend_back.3 = (bf16[512,768]{1,0:T(8,128)(2,1)S(1)}, bf16[2,512,768]{2,1,0:T(8,128)(2,1)S(1)}, bf16[2,512,768]{2,1,0:T(8,128)(2,1)}, f32[6,1,256]{2,1,0:T(1,128)S(1)}) custom-call(s32[4]{0:T(128)S(1)} %copy-done.22, bf16[512,768]{1,0:T(8,128)(2,1)S(1)} %copy-done.16, bf16[512,1536]{1,0:T(8,128)(2,1)S(1)} %copy-done.1, bf16[512,1536]{1,0:T(8,128)(2,1)S(1)} %copy-done.1, ...), custom_call_target="tpu_custom_call" | custom-call | flops 1048576 | bytes 1048576 | tf_op jit(solution)/shard_map/attend_back/pallas_call | solution.py:290
  500.2 4.4 concatenate.76
  513.3 7.9 %all-to-all-done.5 = bf16[16,192,768]{2,1,0:T(8,128)(2,1)} async-done(((bf16[16,192,768]{2,1,0:T(8,128)(2,1)}), bf16[16,192,768]{2,1,0:T(8,128)(2,1)}, u32[]{:S(2)}, u32[]{:S(2)}) %all-to-all-start.5) | async-done | bytes 4718624 | tf_op jit(solution)/shard_map/all_to_all | solution.py:654
  521.3 7.7 %collective-permute-start.17 = (bf16[4,2,24,1664]{3,2,0,1:T(8,128)(2,1)S(1)}, bf16[4,2,24,1664]{3,2,0,1:T(8,128)(2,1)S(1)}, u32[]{:S(2)}, u32[]{:S(2)}) collective-permute-start(bf16[4,2,24,1664]{3,2,0,1:T(8,128)(2,1)S(1)} %fusion.99), channel_id=1, source_target_pairs={{0,2},{1,3},{2,0},{3,1},{4,6},{5,7},{6,4},{7,5},{8,10},{9,11},{10,... | collective-permute-start | bytes 1916936 | tf_op jit(solution)/shard_map/ppermute | solution.py:502
  551.5 13.3 %collective-permute-start.19 = (bf16[2,24,1664]{2,1,0:T(8,128)(2,1)S(1)}, bf16[2,24,1664]{2,1,0:T(8,128)(2,1)S(1)}, u32[]{:S(2)}, u32[]{:S(2)}) collective-permute-start(bf16[2,24,1664]{2,1,0:T(8,128)(2,1)S(1)} %fusion.139), channel_id=1, source_target_pairs={{0,4},{1,5},{2,6},{3,7},{4,0},{5,1},{6,2},{7,3},{8,12},{9,13},{10,... | collective-permute-start | bytes 479240 | tf_op jit(solution)/shard_map/ppermute | solution.py:502
  (545 shorter events, 205.9 us)
Async XLA Ops:
  2.2 13.7 %collective-permute-start.5 = (bf16[1,24,1536]{2,1,0:T(8,128)(2,1)S(1)}, bf16[1,24,1536]{2,1,0:T(8,128)(2,1)S(1)}, u32[]{:S(2)}, u32[]{:S(2)}) collective-permute-start(bf16[1,24,1536]{2,1,0:T(8,128)(2,1)S(1)} %maximum_bitcast_fusion.4), channel_id=1, source_target_pairs={{0,8},{1,9},{2,10},{3,11},{4,12},{5,13},{6,14},{7,15},{8,0},{9,1},... | collective-permute-start | bytes 221192 | tf_op jit(solution)/shard_map/ppermute | solution.py:502
  25.0 10.0 %collective-permute-start.7 = (bf16[4,24,1536]{2,1,0:T(8,128)(2,1)S(1)}, bf16[4,24,1536]{2,1,0:T(8,128)(2,1)S(1)}, u32[]{:S(2)}, u32[]{:S(2)}) collective-permute-start(bf16[4,24,1536]{2,1,0:T(8,128)(2,1)S(1)} %bitcast.298), channel_id=1, source_target_pairs={{0,2},{1,3},{2,0},{3,1},{4,6},{5,7},{6,4},{7,5},{8,10},{9,11},{10,... | collective-permute-start | bytes 884744 | tf_op jit(solution)/shard_map/ppermute | solution.py:502
  30.6 15.4 %collective-permute-start.3 = (bf16[4,2,24,1664]{3,2,0,1:T(8,128)(2,1)S(1)}, bf16[4,2,24,1664]{3,2,0,1:T(8,128)(2,1)S(1)}, u32[]{:S(2)}, u32[]{:S(2)}) collective-permute-start(bf16[4,2,24,1664]{3,2,0,1:T(8,128)(2,1)S(1)} %pad_maximum_fusion.10), channel_id=1, source_target_pairs={{0,2},{1,3},{2,0},{3,1},{4,6},{5,7},{6,4},{7,5},{8,10},{9,11},{10,... | collective-permute-start | bytes 1916936 | tf_op jit(solution)/shard_map/ppermute | solution.py:502
  36.0 21.5 %collective-permute-start.8 = (bf16[4,2,24,1536]{3,2,0,1:T(8,128)(2,1)}, bf16[4,2,24,1536]{3,2,0,1:T(8,128)(2,1)}, u32[]{:S(2)}, u32[]{:S(2)}) collective-permute-start(bf16[4,2,24,1536]{3,2,0,1:T(8,128)(2,1)} %pad_maximum_fusion.11), channel_id=1, source_target_pairs={{0,1},{1,0},{2,3},{3,2},{4,5},{5,4},{6,7},{7,6},{8,9},{9,8},{10,11... | collective-permute-start | bytes 1769480 | tf_op jit(solution)/shard_map/ppermute | solution.py:502
  46.4 12.7 %collective-permute-start.4 = (bf16[384,1664]{1,0:T(8,128)(2,1)S(1)}, bf16[384,1664]{1,0:T(8,128)(2,1)}, u32[]{:S(2)}, u32[]{:S(2)}) collective-permute-start(bf16[384,1664]{1,0:T(8,128)(2,1)S(1)} %bitcast.268), channel_id=1, source_target_pairs={{0,16},{16,0},{1,17},{17,1},{2,18},{18,2},{3,19},{19,3},{4,20},{20... | collective-permute-start | bytes 3833864 | tf_op jit(solution)/shard_map/ppermute | solution.py:502
  50.6 98.0 %all-to-all-start = ((bf16[16,192,768]{2,1,0:T(8,128)(2,1)}), bf16[16,192,768]{2,1,0:T(8,128)(2,1)}, u32[]{:S(2)}, u32[]{:S(2)}) async-start(bf16[16,192,768]{2,1,0:T(8,128)(2,1)} %pad_maximum_fusion), calls=%async_computation | async-start | bytes 9437184 | tf_op jit(solution)/shard_map/all_to_all | solution.py:654
  58.9 9.9 %collective-permute-start.9 = (bf16[384,1536]{1,0:T(8,128)(2,1)S(1)}, bf16[384,1536]{1,0:T(8,128)(2,1)}, u32[]{:S(2)}, u32[]{:S(2)}) collective-permute-start(bf16[384,1536]{1,0:T(8,128)(2,1)S(1)} %bitcast.278), channel_id=1, source_target_pairs={{0,16},{16,0},{1,17},{17,1},{2,18},{18,2},{3,19},{19,3},{4,20},{20... | collective-permute-start | bytes 3538952 | tf_op jit(solution)/shard_map/ppermute | solution.py:502
  71.8 22.0 %collective-permute-start.11 = (bf16[512,1536]{1,0:T(8,128)(2,1)S(1)}, bf16[512,1536]{1,0:T(8,128)(2,1)S(1)}, u32[]{:S(2)}, u32[]{:S(2)}) collective-permute-start(bf16[512,1536]{1,0:T(8,128)(2,1)S(1)} %convolution_convert_fusion.4.k_ref.v_ref), channel_id=1, source_target_pairs={{0,16},{1,17},{2,18},{3,19},{4,20},{5,21},{6,22},{7,23},{8,24},{9,... | collective-permute-start | bytes 4718600 | tf_op jit(solution)/shard_map/ppermute | solution.py:706
  148.7 70.2 %all-to-all-start.1 = ((bf16[16,96,768]{2,1,0:T(8,128)(2,1)}), bf16[16,96,768]{2,1,0:T(8,128)(2,1)}, u32[]{:S(2)}, u32[]{:S(2)}) async-start(bf16[16,96,768]{2,1,0:T(8,128)(2,1)} %broadcast_select_fusion.1), calls=%async_computation.1 | async-start | bytes 4718592 | tf_op jit(solution)/shard_map/all_to_all | solution.py:654
  171.6 9.9 %collective-permute-start.13 = (bf16[1536,768]{1,0:T(8,128)(2,1)}, bf16[1536,768]{1,0:T(8,128)(2,1)}, u32[]{:S(2)}, u32[]{:S(2)}) collective-permute-start(bf16[1536,768]{1,0:T(8,128)(2,1)} %bitcast.287), channel_id=1, source_target_pairs={{0,16},{16,0},{1,17},{17,1},{2,18},{18,2},{3,19},{19,3},{4,20},{20... | collective-permute-start | bytes 7077896 | tf_op jit(solution)/shard_map/ppermute | solution.py:502
  218.9 69.6 %all-to-all-start.2 = ((bf16[16,96,768]{2,1,0:T(8,128)(2,1)}), bf16[16,96,768]{2,1,0:T(8,128)(2,1)}, u32[]{:S(2)}, u32[]{:S(2)}) async-start(bf16[16,96,768]{2,1,0:T(8,128)(2,1)} %broadcast_select_fusion), calls=%async_computation.2 | async-start | bytes 4718592 | tf_op jit(solution)/shard_map/all_to_all | solution.py:654
  288.5 69.2 %all-to-all-start.3 = ((bf16[16,96,768]{2,1,0:T(8,128)(2,1)}), bf16[16,96,768]{2,1,0:T(8,128)(2,1)}, u32[]{:S(2)}, u32[]{:S(2)}) async-start(bf16[16,96,768]{2,1,0:T(8,128)(2,1)} %get-tuple-element.54), calls=%async_computation.3 | async-start | bytes 4718592 | tf_op jit(solution)/shard_map/all_to_all | solution.py:654
  357.1 34.3 %collective-permute-start.27 = (bf16[1536,768]{1,0:T(8,128)(2,1)}, bf16[1536,768]{1,0:T(8,128)(2,1)}, u32[]{:S(2)}, u32[]{:S(2)}) collective-permute-start(bf16[1536,768]{1,0:T(8,128)(2,1)} %get-tuple-element.73), channel_id=1, source_target_pairs={{0,16},{16,0},{1,17},{17,1},{2,18},{18,2},{3,19},{19,3},{4,20},{20... | collective-permute-start | bytes 7077896 | tf_op jit(solution)/shard_map/ppermute | solution.py:502
  357.2 39.0 %collective-permute-start.26 = (bf16[384,3072]{1,0:T(8,128)(2,1)}, bf16[384,3072]{1,0:T(8,128)(2,1)}, u32[]{:S(2)}, u32[]{:S(2)}) collective-permute-start(bf16[384,3072]{1,0:T(8,128)(2,1)} %get-tuple-element.71), channel_id=1, source_target_pairs={{0,16},{16,0},{1,17},{17,1},{2,18},{18,2},{3,19},{19,3},{4,20},{20... | collective-permute-start | bytes 7077896 | tf_op jit(solution)/shard_map/ppermute | solution.py:502
  358.7 54.9 %all-to-all-start.4 = ((bf16[16,96,768]{2,1,0:T(8,128)(2,1)}), bf16[16,96,768]{2,1,0:T(8,128)(2,1)}, u32[]{:S(2)}, u32[]{:S(2)}) async-start(bf16[16,96,768]{2,1,0:T(8,128)(2,1)} %get-tuple-element.55), calls=%async_computation.4 | async-start | bytes 4718592 | tf_op jit(solution)/shard_map/all_to_all | solution.py:654
  389.8 11.6 %collective-permute-start.14 = (bf16[2,512,768]{2,1,0:T(8,128)(2,1)S(1)}, bf16[2,512,768]{2,1,0:T(8,128)(2,1)S(1)}, u32[]{:S(2)}, u32[]{:S(2)}) collective-permute-start(bf16[2,512,768]{2,1,0:T(8,128)(2,1)S(1)} %get-tuple-element.60), channel_id=1, source_target_pairs={{16,0},{17,1},{18,2},{19,3},{20,4},{21,5},{22,6},{23,7},{24,8},{25... | collective-permute-start | bytes 4718600 | tf_op jit(solution)/shard_map/ppermute | solution.py:799
  421.8 99.4 %all-to-all-start.5 = ((bf16[16,192,768]{2,1,0:T(8,128)(2,1)}), bf16[16,192,768]{2,1,0:T(8,128)(2,1)}, u32[]{:S(2)}, u32[]{:S(2)}) async-start(bf16[16,192,768]{2,1,0:T(8,128)(2,1)} %get-tuple-element.56), calls=%async_computation.5 | async-start | bytes 9437184 | tf_op jit(solution)/shard_map/all_to_all | solution.py:654
  462.4 9.8 %collective-permute-start.16 = (bf16[384,1664]{1,0:T(8,128)(2,1)}, bf16[384,1664]{1,0:T(8,128)(2,1)}, u32[]{:S(2)}, u32[]{:S(2)}) collective-permute-start(bf16[384,1664]{1,0:T(8,128)(2,1)} %pad_maximum_fusion.8), channel_id=1, source_target_pairs={{0,16},{16,0},{1,17},{17,1},{2,18},{18,2},{3,19},{19,3},{4,20},{20... | collective-permute-start | bytes 3833864 | tf_op jit(solution)/shard_map/ppermute | solution.py:502
  462.4 13.3 %collective-permute-start.15 = (bf16[2,512,768]{2,1,0:T(8,128)(2,1)}, bf16[2,512,768]{2,1,0:T(8,128)(2,1)}, u32[]{:S(2)}, u32[]{:S(2)}) collective-permute-start(bf16[2,512,768]{2,1,0:T(8,128)(2,1)} %get-tuple-element.65), channel_id=1, source_target_pairs={{16,0},{17,1},{18,2},{19,3},{20,4},{21,5},{22,6},{23,7},{24,8},{25... | collective-permute-start | bytes 4718600 | tf_op jit(solution)/shard_map/ppermute | solution.py:799
  492.7 16.4 %collective-permute-start.21 = (bf16[384,1664]{1,0:T(8,128)(2,1)}, bf16[384,1664]{1,0:T(8,128)(2,1)}, u32[]{:S(2)}, u32[]{:S(2)}) collective-permute-start(bf16[384,1664]{1,0:T(8,128)(2,1)} %concatenate.77), channel_id=1, source_target_pairs={{0,16},{16,0},{1,17},{17,1},{2,18},{18,2},{3,19},{19,3},{4,20},{20... | collective-permute-start | bytes 3833864 | tf_op jit(solution)/shard_map/ppermute | solution.py:502
  521.3 20.3 %collective-permute-start.17 = (bf16[4,2,24,1664]{3,2,0,1:T(8,128)(2,1)S(1)}, bf16[4,2,24,1664]{3,2,0,1:T(8,128)(2,1)S(1)}, u32[]{:S(2)}, u32[]{:S(2)}) collective-permute-start(bf16[4,2,24,1664]{3,2,0,1:T(8,128)(2,1)S(1)} %fusion.99), channel_id=1, source_target_pairs={{0,2},{1,3},{2,0},{3,1},{4,6},{5,7},{6,4},{7,5},{8,10},{9,11},{10,... | collective-permute-start | bytes 1916936 | tf_op jit(solution)/shard_map/ppermute | solution.py:502
  530.4 16.7 %collective-permute-start.22 = (bf16[4,2,24,1664]{3,2,0,1:T(8,128)(2,1)S(1)}, bf16[4,2,24,1664]{3,2,0,1:T(8,128)(2,1)S(1)}, u32[]{:S(2)}, u32[]{:S(2)}) collective-permute-start(bf16[4,2,24,1664]{3,2,0,1:T(8,128)(2,1)S(1)} %fusion.100), channel_id=1, source_target_pairs={{0,1},{1,0},{2,3},{3,2},{4,5},{5,4},{6,7},{7,6},{8,9},{9,8},{10,11... | collective-permute-start | bytes 1916936 | tf_op jit(solution)/shard_map/ppermute | solution.py:502
  547.3 17.4 %collective-permute-start.23 = (bf16[4,24,1664]{2,1,0:T(8,128)(2,1)S(1)}, bf16[4,24,1664]{2,1,0:T(8,128)(2,1)S(1)}, u32[]{:S(2)}, u32[]{:S(2)}) collective-permute-start(bf16[4,24,1664]{2,1,0:T(8,128)(2,1)S(1)} %fusion.130), channel_id=1, source_target_pairs={{0,2},{1,3},{2,0},{3,1},{4,6},{5,7},{6,4},{7,5},{8,10},{9,11},{10,... | collective-permute-start | bytes 958472 | tf_op jit(solution)/shard_map/ppermute | solution.py:502
  551.5 17.8 %collective-permute-start.19 = (bf16[2,24,1664]{2,1,0:T(8,128)(2,1)S(1)}, bf16[2,24,1664]{2,1,0:T(8,128)(2,1)S(1)}, u32[]{:S(2)}, u32[]{:S(2)}) collective-permute-start(bf16[2,24,1664]{2,1,0:T(8,128)(2,1)S(1)} %fusion.139), channel_id=1, source_target_pairs={{0,4},{1,5},{2,6},{3,7},{4,0},{5,1},{6,2},{7,3},{8,12},{9,13},{10,... | collective-permute-start | bytes 479240 | tf_op jit(solution)/shard_map/ppermute | solution.py:502
  (140 other events, 1419.5 us)

commit v6 on v5

--- a/solution.py
+++ b/solution.py
@@ -511,10 +511,10 @@
     return lax.optimization_barrier((x, *others))[0]
 
 
-def gather_rows(left, right):
+def gather_rows(left, right, beside):
     if not (power_of_two("ctx") and power_of_two("exp")):
         every = [lax.all_gather(x, ("ctx", "exp"), axis=0, tiled=True) for x in (left, right)]
-        return [*every, every, every]
+        return [*every, beside(every), every]
     bits = bits_of("exp")
     last = bits[-2:]
     parts = [left, right]
@@ -527,8 +527,8 @@
         ]
     got = [swap(h, "exp", bit) for h, bit in zip(held, last)]
     held = [jnp.stack(ordered(h, g, "exp", bit), axis=1) for h, g, bit in zip(held, got, last)]
-    begun = held
-    got = [swap(h, "exp", bit) for h, bit in zip(held, last[::-1])]
+    made = beside(held)
+    got = [after(swap(h, "exp", bit), made) for h, bit in zip(held, last[::-1])]
     held = [
         jnp.stack(ordered(h, g, "exp", bit), axis=at)
         for h, g, bit, at in zip(held, got, last[::-1], (2, 1))
@@ -541,7 +541,7 @@
             jnp.stack(ordered(h, g, "ctx", bit), axis=0).reshape(-1, h.shape[-1])
             for h, g in zip(held, got)
         ]
-    return [*held, begun, over_exp]
+    return [*held, made, over_exp]
 
 
 def pair_rows(x):
@@ -634,17 +634,7 @@
     slot_rows = jnp.arange(slots, dtype=jnp.int32)
     earlier = jnp.tril(jnp.ones((length, length), bf16), -1)
     hots, slot_of, holds, spreads = [], [], [], []
-    for b in range(batches):
-        route_ids = routes[b, 0]
-        hot = route_ids[:, :, None] == expert_ids[None, None, :]
-        used = jnp.any(hot, axis=1)
-        rank = mm(earlier, used.astype(bf16), ((1,), (0,))).astype(jnp.int32)
-        slot = jnp.sum(jnp.where(hot, rank[:, None, :], 0), axis=2) + route_ids * room
-        hold = [slot[None, :, k] == slot_rows[:, None] for k in range(top)]
-        hots.append(hot)
-        slot_of.append(slot)
-        holds.append(hold)
-        spreads.append(functools.reduce(jnp.logical_or, hold).astype(bf16))
+    cots = [cotangent[b, 0] for b in range(batches)]
 
     def dispatch(b, rows):
         sent = mm(spreads[b], rows, ((1,), (0,))).astype(bf16)
@@ -653,9 +643,23 @@
     def cross(x):
         return lax.all_to_all(x, "exp", split_axis=0, concat_axis=0, tiled=True)
 
-    cots = [cotangent[b, 0] for b in range(batches)]
+    def send_cotangents(held):
+        ids = after(routes, *held)
+        for b in range(batches):
+            route_ids = ids[b, 0]
+            hot = route_ids[:, :, None] == expert_ids[None, None, :]
+            used = jnp.any(hot, axis=1)
+            rank = mm(earlier, used.astype(bf16), ((1,), (0,))).astype(jnp.int32)
+            slot = jnp.sum(jnp.where(hot, rank[:, None, :], 0), axis=2) + route_ids * room
+            hold = [slot[None, :, k] == slot_rows[:, None] for k in range(top)]
+            hots.append(hot)
+            slot_of.append(slot)
+            holds.append(hold)
+            spreads.append(functools.reduce(jnp.logical_or, hold).astype(bf16))
+        return jnp.concatenate([dispatch(b, cots[b]) for b in range(batches)], axis=1)
+
     pad = -(experts + 2) % 128
-    left, right, begun, over_exp = gather_rows(
+    left, right, cot_sent, over_exp = gather_rows(
         jnp.concatenate([query_key_value_weight[:, :width], output_projection_weight], axis=1),
         jnp.concatenate(
             [
@@ -667,6 +671,7 @@
             ],
             axis=1,
         ),
+        send_cotangents,
     )
     query_weight = left[:, :width]
     proj_weight = left[:, width:]
@@ -715,8 +720,7 @@
         view = (tiles, queries, kv, kv_back, query_docs[None], key_docs[None], bias_rows)
         state.append(dict(rows=rows, inv_one=inv_one, normed=normed, view=view))
 
-    cot_sent = jnp.concatenate([dispatch(b, cots[b]) for b in range(batches)], axis=1)
-    cot_here = cross(after(cot_sent, *begun))
+    cot_here = cross(after(cot_sent, *over_exp))
     sent = ()
     for b, s in enumerate(state):
         s["view"] = (after(s["view"][0], *sent),) + s["view"][1:]

time: 589 us -> 582 us (0.988)
  waiting for transfers between devices: 123 us -> 115 us
    unnamed x265 -> x255, local copies, waits for them, and re-layouts: 21.5 us -> 22.5 us
  transfers between devices with their start and end apart: 34 -> 34, of which waited for: 17 -> 18; matrix products, arithmetic and copies ran while one was open for 24% -> 24% of each run, Pallas kernels for 29% -> 29%
where the time goes in v6:
time: 582 us; the launch traced here: 572 us
  Pallas kernels  169 us (29%)
  starting transfers between devices  118 us (20%)
  waiting for transfers between devices  115 us (20%)
  other arithmetic  61.8 us (11%)
  matrix products  59.4 us (10%)
  local copies, waits for them, and re-layouts  46.5 us (8%)
    pallas_call x2, Pallas kernels, run_experts(): pl.pallas_call(functools.partial(expert_kernel, more, halves, split, capa...  120 us
    all_to_all x6, waiting for transfers between devices, cross(): return lax.all_to_all(x, 'exp', split_axis=0, concat_axis=0, tiled=True)  79.9 us
    all_to_all x6, starting transfers between devices, cross(): return lax.all_to_all(x, 'exp', split_axis=0, concat_axis=0, tiled=True)  66.4 us
    dot_general x42, matrix products, mm(): return lax.dot_general(a, b, (dims, ((), ())), preferred_element_type=f32)  59.4 us
    ppermute x24, starting transfers between devices, swap(): return lax.ppermute(x, axis, [(i, i ^ bit) for i in range(size)])  44.5 us
    ppermute x24, waiting for transfers between devices, swap(): return lax.ppermute(x, axis, [(i, i ^ bit) for i in range(size)])  34.9 us
    pallas_call x2, Pallas kernels, attend_back(): pl.pallas_call(bwd_kernel, grid_spec=pltpu.PrefetchScalarGridSpec(num_sca...  30.6 us
    unnamed x255, local copies, waits for them, and re-layouts  22.5 us
  transfers between devices with their start and end apart: 34, of which 18 were waited for; matrix products, arithmetic and copies ran while one was open for 24% of the time, Pallas kernels for 29%

profile of v6, /device:TPU:0, one launch (start us, length us, event | category | flops | bytes accessed | tf_op | source)
XLA Modules:
  0.0 572.0 jit_solution(2023576229230389655)
XLA Ops:
  2.2 4.0 collective-permute-start.4
  45.7 6.3 %all-to-all-start = ((bf16[16,192,768]{2,1,0:T(8,128)(2,1)}), bf16[16,192,768]{2,1,0:T(8,128)(2,1)}, u32[]{:S(2)}, u32[]{:S(2)}) async-start(bf16[16,192,768]{2,1,0:T(8,128)(2,1)} %pad_maximum_fusion), calls=%async_computation | async-start | bytes 9437184 | tf_op jit(solution)/shard_map/all_to_all | solution.py:644
  68.6 9.1 %attend.2 = (bf16[512,768]{1,0:T(8,128)(2,1)S(1)}, f32[6,4,256]{2,1,0:T(4,128)S(1)}) custom-call(s32[4]{0:T(128)S(1)} %subtract_clamp_fusion.1.tiles, bf16[512,768]{1,0:T(8,128)(2,1)S(1)} %convolution_convert_fusion.9.q_ref, bf16[512,1536]{1,0:T(8,128)(2,1)S(1)} %convolution_convert_fusion.5.k_ref.v_ref, ...), custom_call_target="tpu_custom_call" | custom-call | flops 3221225472 | bytes 6291456 | tf_op jit(solution)/shard_map/attend/pallas_call | solution.py:254
  87.0 9.3 %attend.3 = (bf16[512,768]{1,0:T(8,128)(2,1)S(1)}, f32[6,4,256]{2,1,0:T(4,128)S(1)}) custom-call(s32[4]{0:T(128)S(1)} %subtract_clamp_fusion.tiles, bf16[512,768]{1,0:T(8,128)(2,1)S(1)} %copy-done.15, bf16[512,1536]{1,0:T(8,128)(2,1)S(1)} %convolution_convert_fusion.4.k_ref.v_ref, bf16[512,1536]{1,0:T(8,128)(2,1)S(1)} %convolution_convert_fusion.4.k_ref.v_ref, ...), custom_call_target="tpu_custom_call" | custom-call | flops 3221225472 | bytes 6291456 | tf_op jit(solution)/shard_map/attend/pallas_call | solution.py:254
  104.4 37.3 %all-to-all-done.cot_ref = bf16[16,192,768]{2,1,0:T(8,128)(2,1)} async-done(((bf16[16,192,768]{2,1,0:T(8,128)(2,1)}), bf16[16,192,768]{2,1,0:T(8,128)(2,1)}, u32[]{:S(2)}, u32[]{:S(2)}) %all-to-all-start) | async-done | bytes 4718624 | tf_op jit(solution)/shard_map/all_to_all | solution.py:644
  141.7 22.5 %all-to-all-start.1 = ((bf16[16,96,768]{2,1,0:T(8,128)(2,1)}), bf16[16,96,768]{2,1,0:T(8,128)(2,1)}, u32[]{:S(2)}, u32[]{:S(2)}) async-start(bf16[16,96,768]{2,1,0:T(8,128)(2,1)} %broadcast_select_fusion.1), calls=%async_computation.1 | async-start | bytes 4718592 | tf_op jit(solution)/shard_map/all_to_all | solution.py:644
  169.1 5.0 pad_maximum_fusion.1.up_ref
  174.2 4.2 pad_maximum_fusion.2.down_ref
  178.3 32.7 %all-to-all-done.1.x_ref = bf16[16,96,768]{2,1,0:T(8,128)(2,1)} async-done(((bf16[16,96,768]{2,1,0:T(8,128)(2,1)}), bf16[16,96,768]{2,1,0:T(8,128)(2,1)}, u32[]{:S(2)}, u32[]{:S(2)}) %all-to-all-start.1) | async-done | bytes 2359328 | tf_op jit(solution)/shard_map/all_to_all | solution.py:644
  211.0 11.1 %all-to-all-start.2 = ((bf16[16,96,768]{2,1,0:T(8,128)(2,1)}), bf16[16,96,768]{2,1,0:T(8,128)(2,1)}, u32[]{:S(2)}, u32[]{:S(2)}) async-start(bf16[16,96,768]{2,1,0:T(8,128)(2,1)} %broadcast_select_fusion), calls=%async_computation.2 | async-start | bytes 4718592 | tf_op jit(solution)/shard_map/all_to_all | solution.py:644
  222.1 58.5 %experts.2 = (bf16[16,192,768]{2,1,0:T(8,128)(2,1)}, bf16[16,96,768]{2,1,0:T(8,128)(2,1)}, f32[768,3072]{1,0:T(8,128)}, f32[3072,768]{1,0:T(8,128)}) custom-call(s32[1]{0:T(128)} %bitcast.51.ctx, bf16[16,96,768]{2,1,0:T(8,128)(2,1)} %all-to-all-done.1.x_ref, bf16[16,192,768]{2,1,0:T(8,128)(2,1)} %all-to-all-done.cot_ref, ...), custom_call_target="tpu_custom_call" | custom-call | flops 65229815808 | bytes 41943040 | tf_op jit(solution)/shard_map/experts/pallas_call | solution.py:457
  280.6 7.5 %all-to-all-start.3 = ((bf16[16,96,768]{2,1,0:T(8,128)(2,1)}), bf16[16,96,768]{2,1,0:T(8,128)(2,1)}, u32[]{:S(2)}, u32[]{:S(2)}) async-start(bf16[16,96,768]{2,1,0:T(8,128)(2,1)} %get-tuple-element.60), calls=%async_computation.3 | async-start | bytes 4718592 | tf_op jit(solution)/shard_map/all_to_all | solution.py:644
  288.1 61.1 %experts.3 = (bf16[16,192,768]{2,1,0:T(8,128)(2,1)}, bf16[16,96,768]{2,1,0:T(8,128)(2,1)}, f32[384,3072]{1,0:T(8,128)}, bf16[384,3072]{1,0:T(8,128)(2,1)}, f32[1...) custom-call(s32[1]{0:T(128)} %bitcast.51.ctx, ...), custom_call_target="tpu_custom_call", output_to_operand_aliasing={{0}: (5, {})} | custom-call | flops 65229815808 | bytes 41943040 | tf_op jit(solution)/shard_map/experts/pallas_call | solution.py:457
  350.7 7.4 %all-to-all-start.4 = ((bf16[16,96,768]{2,1,0:T(8,128)(2,1)}), bf16[16,96,768]{2,1,0:T(8,128)(2,1)}, u32[]{:S(2)}, u32[]{:S(2)}) async-start(bf16[16,96,768]{2,1,0:T(8,128)(2,1)} %get-tuple-element.61), calls=%async_computation.4 | async-start | bytes 4718592 | tf_op jit(solution)/shard_map/all_to_all | solution.py:644
  368.4 14.9 %attend_back.2 = (bf16[512,768]{1,0:T(8,128)(2,1)S(1)}, bf16[2,512,768]{2,1,0:T(8,128)(2,1)S(1)}, bf16[2,512,768]{2,1,0:T(8,128)(2,1)S(1)}, f32[6,1,256]{2,1,0:T(1,128)S(1)}) custom-call(s32[4]{0:T(128)S(1)} %copy-done.22, bf16[512,768]{1,0:T(8,128)(2,1)S(1)} %copy-done.18, bf16[512,1536]{1,0:T(8,128)(2,1)S(1)} %copy-done.3, ...), custom_call_target="tpu_custom_call" | custom-call | flops 1048576 | bytes 1048576 | tf_op jit(solution)/shard_map/attend_back/pallas_call | solution.py:290
  384.9 4.7 add_bitcast_fusion
  389.7 4.8 add_bitcast_fusion.1
  414.0 11.7 %all-to-all-start.5 = ((bf16[16,192,768]{2,1,0:T(8,128)(2,1)}), bf16[16,192,768]{2,1,0:T(8,128)(2,1)}, u32[]{:S(2)}, u32[]{:S(2)}) async-start(bf16[16,192,768]{2,1,0:T(8,128)(2,1)} %get-tuple-element.62), calls=%async_computation.5 | async-start | bytes 9437184 | tf_op jit(solution)/shard_map/all_to_all | solution.py:644
  431.0 15.7 %attend_back.3 = (bf16[512,768]{1,0:T(8,128)(2,1)S(1)}, bf16[2,512,768]{2,1,0:T(8,128)(2,1)S(1)}, bf16[2,512,768]{2,1,0:T(8,128)(2,1)}, f32[6,1,256]{2,1,0:T(1,128)S(1)}) custom-call(s32[4]{0:T(128)S(1)} %copy-done.24, bf16[512,768]{1,0:T(8,128)(2,1)S(1)} %copy-done.16, bf16[512,1536]{1,0:T(8,128)(2,1)S(1)} %copy-done.1, bf16[512,1536]{1,0:T(8,128)(2,1)S(1)} %copy-done.1, ...), custom_call_target="tpu_custom_call" | custom-call | flops 1048576 | bytes 1048576 | tf_op jit(solution)/shard_map/attend_back/pallas_call | solution.py:290
  492.3 4.4 concatenate.76
  505.5 7.9 %all-to-all-done.5 = bf16[16,192,768]{2,1,0:T(8,128)(2,1)} async-done(((bf16[16,192,768]{2,1,0:T(8,128)(2,1)}), bf16[16,192,768]{2,1,0:T(8,128)(2,1)}, u32[]{:S(2)}, u32[]{:S(2)}) %all-to-all-start.5) | async-done | bytes 4718624 | tf_op jit(solution)/shard_map/all_to_all | solution.py:644
  513.4 7.7 %collective-permute-start.17 = (bf16[4,2,24,1664]{3,2,0,1:T(8,128)(2,1)S(1)}, bf16[4,2,24,1664]{3,2,0,1:T(8,128)(2,1)S(1)}, u32[]{:S(2)}, u32[]{:S(2)}) collective-permute-start(bf16[4,2,24,1664]{3,2,0,1:T(8,128)(2,1)S(1)} %fusion.99), channel_id=1, source_target_pairs={{0,2},{1,3},{2,0},{3,1},{4,6},{5,7},{6,4},{7,5},{8,10},{9,11},{10,... | collective-permute-start | bytes 1916936 | tf_op jit(solution)/shard_map/ppermute | solution.py:502
  539.6 4.0 collective-permute-done.18
  543.6 13.3 %collective-permute-start.19 = (bf16[2,24,1664]{2,1,0:T(8,128)(2,1)S(1)}, bf16[2,24,1664]{2,1,0:T(8,128)(2,1)S(1)}, u32[]{:S(2)}, u32[]{:S(2)}) collective-permute-start(bf16[2,24,1664]{2,1,0:T(8,128)(2,1)S(1)} %fusion.139), channel_id=1, source_target_pairs={{0,4},{1,5},{2,6},{3,7},{4,0},{5,1},{6,2},{7,3},{8,12},{9,13},{10,... | collective-permute-start | bytes 479240 | tf_op jit(solution)/shard_map/ppermute | solution.py:502
  (535 shorter events, 204.0 us)
Async XLA Ops:
  2.2 10.6 %collective-permute-start.4 = (bf16[1,24,1536]{2,1,0:T(8,128)(2,1)S(1)}, bf16[1,24,1536]{2,1,0:T(8,128)(2,1)S(1)}, u32[]{:S(2)}, u32[]{:S(2)}) collective-permute-start(bf16[1,24,1536]{2,1,0:T(8,128)(2,1)S(1)} %maximum_bitcast_fusion.4), channel_id=1, source_target_pairs={{0,8},{1,9},{2,10},{3,11},{4,12},{5,13},{6,14},{7,15},{8,0},{9,1},... | collective-permute-start | bytes 221192 | tf_op jit(solution)/shard_map/ppermute | solution.py:502
  22.0 10.5 %collective-permute-start.2 = (bf16[4,24,1664]{2,1,0:T(8,128)(2,1)S(1)}, bf16[4,24,1664]{2,1,0:T(8,128)(2,1)S(1)}, u32[]{:S(2)}, u32[]{:S(2)}) collective-permute-start(bf16[4,24,1664]{2,1,0:T(8,128)(2,1)S(1)} %bitcast.297), channel_id=1, source_target_pairs={{0,1},{1,0},{2,3},{3,2},{4,5},{5,4},{6,7},{7,6},{8,9},{9,8},{10,11... | collective-permute-start | bytes 958472 | tf_op jit(solution)/shard_map/ppermute | solution.py:502
  26.8 18.1 %collective-permute-start.8 = (bf16[4,2,24,1536]{3,2,0,1:T(8,128)(2,1)S(1)}, bf16[4,2,24,1536]{3,2,0,1:T(8,128)(2,1)S(1)}, u32[]{:S(2)}, u32[]{:S(2)}) collective-permute-start(bf16[4,2,24,1536]{3,2,0,1:T(8,128)(2,1)S(1)} %pad_maximum_fusion.11), channel_id=1, source_target_pairs={{0,1},{1,0},{2,3},{3,2},{4,5},{5,4},{6,7},{7,6},{8,9},{9,8},{10,11... | collective-permute-start | bytes 1769480 | tf_op jit(solution)/shard_map/ppermute | solution.py:502
  32.8 11.6 %collective-permute-start.3 = (bf16[4,2,24,1664]{3,2,0,1:T(8,128)(2,1)S(1)}, bf16[4,2,24,1664]{3,2,0,1:T(8,128)(2,1)S(1)}, u32[]{:S(2)}, u32[]{:S(2)}) collective-permute-start(bf16[4,2,24,1664]{3,2,0,1:T(8,128)(2,1)S(1)} %pad_maximum_fusion.10), channel_id=1, source_target_pairs={{0,2},{1,3},{2,0},{3,1},{4,6},{5,7},{6,4},{7,5},{8,10},{9,11},{10,... | collective-permute-start | bytes 1916936 | tf_op jit(solution)/shard_map/ppermute | solution.py:502
  45.2 15.8 %collective-permute-start.9 = (bf16[384,1536]{1,0:T(8,128)(2,1)S(1)}, bf16[384,1536]{1,0:T(8,128)(2,1)}, u32[]{:S(2)}, u32[]{:S(2)}) collective-permute-start(bf16[384,1536]{1,0:T(8,128)(2,1)S(1)} %bitcast.278), channel_id=1, source_target_pairs={{0,16},{16,0},{1,17},{17,1},{2,18},{18,2},{3,19},{19,3},{4,20},{20... | collective-permute-start | bytes 3538952 | tf_op jit(solution)/shard_map/ppermute | solution.py:502
  45.7 96.0 %all-to-all-start = ((bf16[16,192,768]{2,1,0:T(8,128)(2,1)}), bf16[16,192,768]{2,1,0:T(8,128)(2,1)}, u32[]{:S(2)}, u32[]{:S(2)}) async-start(bf16[16,192,768]{2,1,0:T(8,128)(2,1)} %pad_maximum_fusion), calls=%async_computation | async-start | bytes 9437184 | tf_op jit(solution)/shard_map/all_to_all | solution.py:644
  64.1 22.8 %collective-permute-start.11 = (bf16[512,1536]{1,0:T(8,128)(2,1)S(1)}, bf16[512,1536]{1,0:T(8,128)(2,1)S(1)}, u32[]{:S(2)}, u32[]{:S(2)}) collective-permute-start(bf16[512,1536]{1,0:T(8,128)(2,1)S(1)} %convolution_convert_fusion.4.k_ref.v_ref), channel_id=1, source_target_pairs={{0,16},{1,17},{2,18},{3,19},{4,20},{5,21},{6,22},{7,23},{8,24},{9,... | collective-permute-start | bytes 4718600 | tf_op jit(solution)/shard_map/ppermute | solution.py:711
  141.7 69.3 %all-to-all-start.1 = ((bf16[16,96,768]{2,1,0:T(8,128)(2,1)}), bf16[16,96,768]{2,1,0:T(8,128)(2,1)}, u32[]{:S(2)}, u32[]{:S(2)}) async-start(bf16[16,96,768]{2,1,0:T(8,128)(2,1)} %broadcast_select_fusion.1), calls=%async_computation.1 | async-start | bytes 4718592 | tf_op jit(solution)/shard_map/all_to_all | solution.py:644
  164.2 9.9 %collective-permute-start.13 = (bf16[1536,768]{1,0:T(8,128)(2,1)}, bf16[1536,768]{1,0:T(8,128)(2,1)}, u32[]{:S(2)}, u32[]{:S(2)}) collective-permute-start(bf16[1536,768]{1,0:T(8,128)(2,1)} %bitcast.287), channel_id=1, source_target_pairs={{0,16},{16,0},{1,17},{17,1},{2,18},{18,2},{3,19},{19,3},{4,20},{20... | collective-permute-start | bytes 7077896 | tf_op jit(solution)/shard_map/ppermute | solution.py:502
  211.0 69.6 %all-to-all-start.2 = ((bf16[16,96,768]{2,1,0:T(8,128)(2,1)}), bf16[16,96,768]{2,1,0:T(8,128)(2,1)}, u32[]{:S(2)}, u32[]{:S(2)}) async-start(bf16[16,96,768]{2,1,0:T(8,128)(2,1)} %broadcast_select_fusion), calls=%async_computation.2 | async-start | bytes 4718592 | tf_op jit(solution)/shard_map/all_to_all | solution.py:644
  280.6 69.1 %all-to-all-start.3 = ((bf16[16,96,768]{2,1,0:T(8,128)(2,1)}), bf16[16,96,768]{2,1,0:T(8,128)(2,1)}, u32[]{:S(2)}, u32[]{:S(2)}) async-start(bf16[16,96,768]{2,1,0:T(8,128)(2,1)} %get-tuple-element.60), calls=%async_computation.3 | async-start | bytes 4718592 | tf_op jit(solution)/shard_map/all_to_all | solution.py:644
  349.2 35.7 %collective-permute-start.27 = (bf16[1536,768]{1,0:T(8,128)(2,1)}, bf16[1536,768]{1,0:T(8,128)(2,1)}, u32[]{:S(2)}, u32[]{:S(2)}) collective-permute-start(bf16[1536,768]{1,0:T(8,128)(2,1)} %get-tuple-element.79), channel_id=1, source_target_pairs={{0,16},{16,0},{1,17},{17,1},{2,18},{18,2},{3,19},{19,3},{4,20},{20... | collective-permute-start | bytes 7077896 | tf_op jit(solution)/shard_map/ppermute | solution.py:502
  349.2 40.5 %collective-permute-start.26 = (bf16[384,3072]{1,0:T(8,128)(2,1)}, bf16[384,3072]{1,0:T(8,128)(2,1)}, u32[]{:S(2)}, u32[]{:S(2)}) collective-permute-start(bf16[384,3072]{1,0:T(8,128)(2,1)} %get-tuple-element.77), channel_id=1, source_target_pairs={{0,16},{16,0},{1,17},{17,1},{2,18},{18,2},{3,19},{19,3},{4,20},{20... | collective-permute-start | bytes 7077896 | tf_op jit(solution)/shard_map/ppermute | solution.py:502
  350.7 55.0 %all-to-all-start.4 = ((bf16[16,96,768]{2,1,0:T(8,128)(2,1)}), bf16[16,96,768]{2,1,0:T(8,128)(2,1)}, u32[]{:S(2)}, u32[]{:S(2)}) async-start(bf16[16,96,768]{2,1,0:T(8,128)(2,1)} %get-tuple-element.61), calls=%async_computation.4 | async-start | bytes 4718592 | tf_op jit(solution)/shard_map/all_to_all | solution.py:644
  383.4 11.6 %collective-permute-start.14 = (bf16[2,512,768]{2,1,0:T(8,128)(2,1)S(1)}, bf16[2,512,768]{2,1,0:T(8,128)(2,1)S(1)}, u32[]{:S(2)}, u32[]{:S(2)}) collective-permute-start(bf16[2,512,768]{2,1,0:T(8,128)(2,1)S(1)} %get-tuple-element.66), channel_id=1, source_target_pairs={{16,0},{17,1},{18,2},{19,3},{20,4},{21,5},{22,6},{23,7},{24,8},{25... | collective-permute-start | bytes 4718600 | tf_op jit(solution)/shard_map/ppermute | solution.py:803
  414.0 99.4 %all-to-all-start.5 = ((bf16[16,192,768]{2,1,0:T(8,128)(2,1)}), bf16[16,192,768]{2,1,0:T(8,128)(2,1)}, u32[]{:S(2)}, u32[]{:S(2)}) async-start(bf16[16,192,768]{2,1,0:T(8,128)(2,1)} %get-tuple-element.62), calls=%async_computation.5 | async-start | bytes 9437184 | tf_op jit(solution)/shard_map/all_to_all | solution.py:644
  454.6 9.8 %collective-permute-start.16 = (bf16[384,1664]{1,0:T(8,128)(2,1)}, bf16[384,1664]{1,0:T(8,128)(2,1)}, u32[]{:S(2)}, u32[]{:S(2)}) collective-permute-start(bf16[384,1664]{1,0:T(8,128)(2,1)} %pad_maximum_fusion.8), channel_id=1, source_target_pairs={{0,16},{16,0},{1,17},{17,1},{2,18},{18,2},{3,19},{19,3},{4,20},{20... | collective-permute-start | bytes 3833864 | tf_op jit(solution)/shard_map/ppermute | solution.py:502
  454.6 13.3 %collective-permute-start.15 = (bf16[2,512,768]{2,1,0:T(8,128)(2,1)}, bf16[2,512,768]{2,1,0:T(8,128)(2,1)}, u32[]{:S(2)}, u32[]{:S(2)}) collective-permute-start(bf16[2,512,768]{2,1,0:T(8,128)(2,1)} %get-tuple-element.71), channel_id=1, source_target_pairs={{16,0},{17,1},{18,2},{19,3},{20,4},{21,5},{22,6},{23,7},{24,8},{25... | collective-permute-start | bytes 4718600 | tf_op jit(solution)/shard_map/ppermute | solution.py:803
  484.9 16.4 %collective-permute-start.21 = (bf16[384,1664]{1,0:T(8,128)(2,1)}, bf16[384,1664]{1,0:T(8,128)(2,1)}, u32[]{:S(2)}, u32[]{:S(2)}) collective-permute-start(bf16[384,1664]{1,0:T(8,128)(2,1)} %concatenate.77), channel_id=1, source_target_pairs={{0,16},{16,0},{1,17},{17,1},{2,18},{18,2},{3,19},{19,3},{4,20},{20... | collective-permute-start | bytes 3833864 | tf_op jit(solution)/shard_map/ppermute | solution.py:502
  513.4 20.3 %collective-permute-start.17 = (bf16[4,2,24,1664]{3,2,0,1:T(8,128)(2,1)S(1)}, bf16[4,2,24,1664]{3,2,0,1:T(8,128)(2,1)S(1)}, u32[]{:S(2)}, u32[]{:S(2)}) collective-permute-start(bf16[4,2,24,1664]{3,2,0,1:T(8,128)(2,1)S(1)} %fusion.99), channel_id=1, source_target_pairs={{0,2},{1,3},{2,0},{3,1},{4,6},{5,7},{6,4},{7,5},{8,10},{9,11},{10,... | collective-permute-start | bytes 1916936 | tf_op jit(solution)/shard_map/ppermute | solution.py:502
  522.6 16.7 %collective-permute-start.22 = (bf16[4,2,24,1664]{3,2,0,1:T(8,128)(2,1)S(1)}, bf16[4,2,24,1664]{3,2,0,1:T(8,128)(2,1)S(1)}, u32[]{:S(2)}, u32[]{:S(2)}) collective-permute-start(bf16[4,2,24,1664]{3,2,0,1:T(8,128)(2,1)S(1)} %fusion.100), channel_id=1, source_target_pairs={{0,1},{1,0},{2,3},{3,2},{4,5},{5,4},{6,7},{7,6},{8,9},{9,8},{10,11... | collective-permute-start | bytes 1916936 | tf_op jit(solution)/shard_map/ppermute | solution.py:502
  534.0 9.5 %collective-permute-start.18 = (bf16[4,24,1664]{2,1,0:T(8,128)(2,1)S(1)}, bf16[4,24,1664]{2,1,0:T(8,128)(2,1)S(1)}, u32[]{:S(2)}, u32[]{:S(2)}) collective-permute-start(bf16[4,24,1664]{2,1,0:T(8,128)(2,1)S(1)} %fusion.129), channel_id=1, source_target_pairs={{0,1},{1,0},{2,3},{3,2},{4,5},{5,4},{6,7},{7,6},{8,9},{9,8},{10,11... | collective-permute-start | bytes 958472 | tf_op jit(solution)/shard_map/ppermute | solution.py:502
  539.5 17.4 %collective-permute-start.23 = (bf16[4,24,1664]{2,1,0:T(8,128)(2,1)S(1)}, bf16[4,24,1664]{2,1,0:T(8,128)(2,1)S(1)}, u32[]{:S(2)}, u32[]{:S(2)}) collective-permute-start(bf16[4,24,1664]{2,1,0:T(8,128)(2,1)S(1)} %fusion.130), channel_id=1, source_target_pairs={{0,2},{1,3},{2,0},{3,1},{4,6},{5,7},{6,4},{7,5},{8,10},{9,11},{10,... | collective-permute-start | bytes 958472 | tf_op jit(solution)/shard_map/ppermute | solution.py:502
  543.6 17.8 %collective-permute-start.19 = (bf16[2,24,1664]{2,1,0:T(8,128)(2,1)S(1)}, bf16[2,24,1664]{2,1,0:T(8,128)(2,1)S(1)}, u32[]{:S(2)}, u32[]{:S(2)}) collective-permute-start(bf16[2,24,1664]{2,1,0:T(8,128)(2,1)S(1)} %fusion.139), channel_id=1, source_target_pairs={{0,4},{1,5},{2,6},{3,7},{4,0},{5,1},{6,2},{7,3},{8,12},{9,13},{10,... | collective-permute-start | bytes 479240 | tf_op jit(solution)/shard_map/ppermute | solution.py:502
  (135 other events, 1164.9 us)

commit v7 on v6

--- a/solution.py
+++ b/solution.py
@@ -590,7 +590,7 @@
     got = [swap(x.astype(bf16), "ctx", 1) for x in theirs]
     mine = half_of(me)
     bits = bits_of("exp")
-    held = [after(add_received(m, g, e), late) for m, g, e in zip(mine, got, even)]
+    held = [add_received(m, after(g, late), e) for m, g, e in zip(mine, got, even)]
     held = [h.reshape((-1, 2, 2, depth, h.shape[1])) for h in held]
     high, low = bits[-2:]
     held = [halve(held[0], "exp", high, 1, even[0]), halve(held[1], "exp", low, 2, even[1])]

time: 582 us -> 577 us (level)
    unnamed x255 -> x261, local copies, waits for them, and re-layouts: 22.5 us -> 22.3 us
where the time goes in v7:
time: 577 us; the launch traced here: 568 us
  Pallas kernels  167 us (29%)
  starting transfers between devices  118 us (20%)
  waiting for transfers between devices  117 us (20%)
  matrix products  60.6 us (11%)
  other arithmetic  56.4 us (10%)
  local copies, waits for them, and re-layouts  45.2 us (8%)
    pallas_call x2, Pallas kernels, run_experts(): pl.pallas_call(functools.partial(expert_kernel, more, halves, split, capa...  119 us
    all_to_all x6, waiting for transfers between devices, cross(): return lax.all_to_all(x, 'exp', split_axis=0, concat_axis=0, tiled=True)  83.1 us
    all_to_all x6, starting transfers between devices, cross(): return lax.all_to_all(x, 'exp', split_axis=0, concat_axis=0, tiled=True)  66.1 us
    dot_general x42, matrix products, mm(): return lax.dot_general(a, b, (dims, ((), ())), preferred_element_type=f32)  60.6 us
    ppermute x24, starting transfers between devices, swap(): return lax.ppermute(x, axis, [(i, i ^ bit) for i in range(size)])  46 us
    ppermute x24, waiting for transfers between devices, swap(): return lax.ppermute(x, axis, [(i, i ^ bit) for i in range(size)])  33.5 us
    pallas_call x2, Pallas kernels, attend_back(): pl.pallas_call(bwd_kernel, grid_spec=pltpu.PrefetchScalarGridSpec(num_sca...  29.9 us
    unnamed x261, local copies, waits for them, and re-layouts  22.3 us
  transfers between devices with their start and end apart: 34, of which 18 were waited for; matrix products, arithmetic and copies ran while one was open for 24% of the time, Pallas kernels for 29%

profile of v7, /device:TPU:0, one launch (start us, length us, event | category | flops | bytes accessed | tf_op | source)
XLA Modules:
  0.0 567.9 jit_solution(12258618497556797825)
XLA Ops:
  2.2 4.0 collective-permute-start.4
  45.7 6.3 %all-to-all-start = ((bf16[16,192,768]{2,1,0:T(8,128)(2,1)}), bf16[16,192,768]{2,1,0:T(8,128)(2,1)}, u32[]{:S(2)}, u32[]{:S(2)}) async-start(bf16[16,192,768]{2,1,0:T(8,128)(2,1)} %pad_maximum_fusion), calls=%async_computation | async-start | bytes 9437184 | tf_op jit(solution)/shard_map/all_to_all | solution.py:644
  68.4 8.5 %attend.2 = (bf16[512,768]{1,0:T(8,128)(2,1)S(1)}, f32[6,4,256]{2,1,0:T(4,128)S(1)}) custom-call(s32[4]{0:T(128)S(1)} %subtract_clamp_fusion.1.tiles, bf16[512,768]{1,0:T(8,128)(2,1)S(1)} %convolution_convert_fusion.9.q_ref, bf16[512,1536]{1,0:T(8,128)(2,1)S(1)} %convolution_convert_fusion.5.k_ref.v_ref, ...), custom_call_target="tpu_custom_call" | custom-call | flops 3221225472 | bytes 6291456 | tf_op jit(solution)/shard_map/attend/pallas_call | solution.py:254
  86.2 9.5 %attend.3 = (bf16[512,768]{1,0:T(8,128)(2,1)S(1)}, f32[6,4,256]{2,1,0:T(4,128)S(1)}) custom-call(s32[4]{0:T(128)S(1)} %subtract_clamp_fusion.tiles, bf16[512,768]{1,0:T(8,128)(2,1)S(1)} %copy-done.15, bf16[512,1536]{1,0:T(8,128)(2,1)S(1)} %convolution_convert_fusion.4.k_ref.v_ref, bf16[512,1536]{1,0:T(8,128)(2,1)S(1)} %convolution_convert_fusion.4.k_ref.v_ref, ...), custom_call_target="tpu_custom_call" | custom-call | flops 3221225472 | bytes 6291456 | tf_op jit(solution)/shard_map/attend/pallas_call | solution.py:254
  103.9 37.8 %all-to-all-done.cot_ref = bf16[16,192,768]{2,1,0:T(8,128)(2,1)} async-done(((bf16[16,192,768]{2,1,0:T(8,128)(2,1)}), bf16[16,192,768]{2,1,0:T(8,128)(2,1)}, u32[]{:S(2)}, u32[]{:S(2)}) %all-to-all-start) | async-done | bytes 4718624 | tf_op jit(solution)/shard_map/all_to_all | solution.py:644
  141.7 22.5 %all-to-all-start.1 = ((bf16[16,96,768]{2,1,0:T(8,128)(2,1)}), bf16[16,96,768]{2,1,0:T(8,128)(2,1)}, u32[]{:S(2)}, u32[]{:S(2)}) async-start(bf16[16,96,768]{2,1,0:T(8,128)(2,1)} %broadcast_select_fusion.1), calls=%async_computation.1 | async-start | bytes 4718592 | tf_op jit(solution)/shard_map/all_to_all | solution.py:644
  169.1 5.0 pad_maximum_fusion.1.up_ref
  174.2 4.2 pad_maximum_fusion.2.down_ref
  178.3 32.7 %all-to-all-done.1.x_ref = bf16[16,96,768]{2,1,0:T(8,128)(2,1)} async-done(((bf16[16,96,768]{2,1,0:T(8,128)(2,1)}), bf16[16,96,768]{2,1,0:T(8,128)(2,1)}, u32[]{:S(2)}, u32[]{:S(2)}) %all-to-all-start.1) | async-done | bytes 2359328 | tf_op jit(solution)/shard_map/all_to_all | solution.py:644
  211.0 11.0 %all-to-all-start.2 = ((bf16[16,96,768]{2,1,0:T(8,128)(2,1)}), bf16[16,96,768]{2,1,0:T(8,128)(2,1)}, u32[]{:S(2)}, u32[]{:S(2)}) async-start(bf16[16,96,768]{2,1,0:T(8,128)(2,1)} %broadcast_select_fusion), calls=%async_computation.2 | async-start | bytes 4718592 | tf_op jit(solution)/shard_map/all_to_all | solution.py:644
  222.1 58.4 %experts.2 = (bf16[16,192,768]{2,1,0:T(8,128)(2,1)}, bf16[16,96,768]{2,1,0:T(8,128)(2,1)}, f32[768,3072]{1,0:T(8,128)}, f32[3072,768]{1,0:T(8,128)}) custom-call(s32[1]{0:T(128)} %bitcast.51.ctx, bf16[16,96,768]{2,1,0:T(8,128)(2,1)} %all-to-all-done.1.x_ref, bf16[16,192,768]{2,1,0:T(8,128)(2,1)} %all-to-all-done.cot_ref, ...), custom_call_target="tpu_custom_call" | custom-call | flops 65229815808 | bytes 41943040 | tf_op jit(solution)/shard_map/experts/pallas_call | solution.py:457
  280.5 7.3 %all-to-all-start.3 = ((bf16[16,96,768]{2,1,0:T(8,128)(2,1)}), bf16[16,96,768]{2,1,0:T(8,128)(2,1)}, u32[]{:S(2)}, u32[]{:S(2)}) async-start(bf16[16,96,768]{2,1,0:T(8,128)(2,1)} %get-tuple-element.60), calls=%async_computation.3 | async-start | bytes 4718592 | tf_op jit(solution)/shard_map/all_to_all | solution.py:644
  287.8 61.1 %experts.3 = (bf16[16,192,768]{2,1,0:T(8,128)(2,1)}, bf16[16,96,768]{2,1,0:T(8,128)(2,1)}, f32[384,3072]{1,0:T(8,128)}, bf16[384,3072]{1,0:T(8,128)(2,1)}, f32[1...) custom-call(s32[1]{0:T(128)} %bitcast.51.ctx, ...), custom_call_target="tpu_custom_call", output_to_operand_aliasing={{0}: (5, {})} | custom-call | flops 65229815808 | bytes 41943040 | tf_op jit(solution)/shard_map/experts/pallas_call | solution.py:457
  350.4 7.5 %all-to-all-start.4 = ((bf16[16,96,768]{2,1,0:T(8,128)(2,1)}), bf16[16,96,768]{2,1,0:T(8,128)(2,1)}, u32[]{:S(2)}, u32[]{:S(2)}) async-start(bf16[16,96,768]{2,1,0:T(8,128)(2,1)} %get-tuple-element.61), calls=%async_computation.4 | async-start | bytes 4718592 | tf_op jit(solution)/shard_map/all_to_all | solution.py:644
  368.3 14.0 %attend_back.2 = (bf16[512,768]{1,0:T(8,128)(2,1)S(1)}, bf16[2,512,768]{2,1,0:T(8,128)(2,1)S(1)}, bf16[2,512,768]{2,1,0:T(8,128)(2,1)S(1)}, f32[6,1,256]{2,1,0:T(1,128)S(1)}) custom-call(s32[4]{0:T(128)S(1)} %copy-done.22, bf16[512,768]{1,0:T(8,128)(2,1)S(1)} %copy-done.18, bf16[512,1536]{1,0:T(8,128)(2,1)S(1)} %copy-done.3, ...), custom_call_target="tpu_custom_call" | custom-call | flops 1048576 | bytes 1048576 | tf_op jit(solution)/shard_map/attend_back/pallas_call | solution.py:290
  383.9 4.7 add_bitcast_fusion
  388.7 4.8 add_bitcast_fusion.1
  407.5 11.5 %all-to-all-start.5 = ((bf16[16,192,768]{2,1,0:T(8,128)(2,1)}), bf16[16,192,768]{2,1,0:T(8,128)(2,1)}, u32[]{:S(2)}, u32[]{:S(2)}) async-start(bf16[16,192,768]{2,1,0:T(8,128)(2,1)} %get-tuple-element.62), calls=%async_computation.5 | async-start | bytes 9437184 | tf_op jit(solution)/shard_map/all_to_all | solution.py:644
  428.7 15.8 %attend_back.3 = (bf16[512,768]{1,0:T(8,128)(2,1)S(1)}, bf16[2,512,768]{2,1,0:T(8,128)(2,1)S(1)}, bf16[2,512,768]{2,1,0:T(8,128)(2,1)}, f32[6,1,256]{2,1,0:T(1,128)S(1)}) custom-call(s32[4]{0:T(128)S(1)} %copy-done.24, bf16[512,768]{1,0:T(8,128)(2,1)S(1)} %copy-done.16, bf16[512,1536]{1,0:T(8,128)(2,1)S(1)} %copy-done.1, bf16[512,1536]{1,0:T(8,128)(2,1)S(1)} %copy-done.1, ...), custom_call_target="tpu_custom_call" | custom-call | flops 1048576 | bytes 1048576 | tf_op jit(solution)/shard_map/attend_back/pallas_call | solution.py:290
  487.4 4.5 concatenate.76
  496.4 10.2 %all-to-all-done.5 = bf16[16,192,768]{2,1,0:T(8,128)(2,1)} async-done(((bf16[16,192,768]{2,1,0:T(8,128)(2,1)}), bf16[16,192,768]{2,1,0:T(8,128)(2,1)}, u32[]{:S(2)}, u32[]{:S(2)}) %all-to-all-start.5) | async-done | bytes 4718624 | tf_op jit(solution)/shard_map/all_to_all | solution.py:644
  508.6 7.7 %collective-permute-start.17 = (bf16[4,2,24,1664]{3,2,0,1:T(8,128)(2,1)S(1)}, bf16[4,2,24,1664]{3,2,0,1:T(8,128)(2,1)S(1)}, u32[]{:S(2)}, u32[]{:S(2)}) collective-permute-start(bf16[4,2,24,1664]{3,2,0,1:T(8,128)(2,1)S(1)} %fusion.99), channel_id=1, source_target_pairs={{0,2},{1,3},{2,0},{3,1},{4,6},{5,7},{6,4},{7,5},{8,10},{9,11},{10,... | collective-permute-start | bytes 1916936 | tf_op jit(solution)/shard_map/ppermute | solution.py:502
  530.9 4.4 collective-permute-done.22
  539.2 13.3 %collective-permute-start.19 = (bf16[2,24,1664]{2,1,0:T(8,128)(2,1)S(1)}, bf16[2,24,1664]{2,1,0:T(8,128)(2,1)S(1)}, u32[]{:S(2)}, u32[]{:S(2)}) collective-permute-start(bf16[2,24,1664]{2,1,0:T(8,128)(2,1)S(1)} %fusion.139), channel_id=1, source_target_pairs={{0,4},{1,5},{2,6},{3,7},{4,0},{5,1},{6,2},{7,3},{8,12},{9,13},{10,... | collective-permute-start | bytes 479240 | tf_op jit(solution)/shard_map/ppermute | solution.py:502
  (541 shorter events, 197.5 us)
Async XLA Ops:
  2.2 10.6 %collective-permute-start.4 = (bf16[1,24,1536]{2,1,0:T(8,128)(2,1)S(1)}, bf16[1,24,1536]{2,1,0:T(8,128)(2,1)S(1)}, u32[]{:S(2)}, u32[]{:S(2)}) collective-permute-start(bf16[1,24,1536]{2,1,0:T(8,128)(2,1)S(1)} %maximum_bitcast_fusion.4), channel_id=1, source_target_pairs={{0,8},{1,9},{2,10},{3,11},{4,12},{5,13},{6,14},{7,15},{8,0},{9,1},... | collective-permute-start | bytes 221192 | tf_op jit(solution)/shard_map/ppermute | solution.py:502
  22.0 10.5 %collective-permute-start.2 = (bf16[4,24,1664]{2,1,0:T(8,128)(2,1)S(1)}, bf16[4,24,1664]{2,1,0:T(8,128)(2,1)S(1)}, u32[]{:S(2)}, u32[]{:S(2)}) collective-permute-start(bf16[4,24,1664]{2,1,0:T(8,128)(2,1)S(1)} %bitcast.297), channel_id=1, source_target_pairs={{0,1},{1,0},{2,3},{3,2},{4,5},{5,4},{6,7},{7,6},{8,9},{9,8},{10,11... | collective-permute-start | bytes 958472 | tf_op jit(solution)/shard_map/ppermute | solution.py:502
  26.8 18.1 %collective-permute-start.8 = (bf16[4,2,24,1536]{3,2,0,1:T(8,128)(2,1)S(1)}, bf16[4,2,24,1536]{3,2,0,1:T(8,128)(2,1)S(1)}, u32[]{:S(2)}, u32[]{:S(2)}) collective-permute-start(bf16[4,2,24,1536]{3,2,0,1:T(8,128)(2,1)S(1)} %pad_maximum_fusion.11), channel_id=1, source_target_pairs={{0,1},{1,0},{2,3},{3,2},{4,5},{5,4},{6,7},{7,6},{8,9},{9,8},{10,11... | collective-permute-start | bytes 1769480 | tf_op jit(solution)/shard_map/ppermute | solution.py:502
  32.8 11.6 %collective-permute-start.3 = (bf16[4,2,24,1664]{3,2,0,1:T(8,128)(2,1)S(1)}, bf16[4,2,24,1664]{3,2,0,1:T(8,128)(2,1)S(1)}, u32[]{:S(2)}, u32[]{:S(2)}) collective-permute-start(bf16[4,2,24,1664]{3,2,0,1:T(8,128)(2,1)S(1)} %pad_maximum_fusion.10), channel_id=1, source_target_pairs={{0,2},{1,3},{2,0},{3,1},{4,6},{5,7},{6,4},{7,5},{8,10},{9,11},{10,... | collective-permute-start | bytes 1916936 | tf_op jit(solution)/shard_map/ppermute | solution.py:502
  45.2 15.9 %collective-permute-start.9 = (bf16[384,1536]{1,0:T(8,128)(2,1)S(1)}, bf16[384,1536]{1,0:T(8,128)(2,1)}, u32[]{:S(2)}, u32[]{:S(2)}) collective-permute-start(bf16[384,1536]{1,0:T(8,128)(2,1)S(1)} %bitcast.278), channel_id=1, source_target_pairs={{0,16},{16,0},{1,17},{17,1},{2,18},{18,2},{3,19},{19,3},{4,20},{20... | collective-permute-start | bytes 3538952 | tf_op jit(solution)/shard_map/ppermute | solution.py:502
  45.7 96.0 %all-to-all-start = ((bf16[16,192,768]{2,1,0:T(8,128)(2,1)}), bf16[16,192,768]{2,1,0:T(8,128)(2,1)}, u32[]{:S(2)}, u32[]{:S(2)}) async-start(bf16[16,192,768]{2,1,0:T(8,128)(2,1)} %pad_maximum_fusion), calls=%async_computation | async-start | bytes 9437184 | tf_op jit(solution)/shard_map/all_to_all | solution.py:644
  64.2 22.0 %collective-permute-start.11 = (bf16[512,1536]{1,0:T(8,128)(2,1)S(1)}, bf16[512,1536]{1,0:T(8,128)(2,1)S(1)}, u32[]{:S(2)}, u32[]{:S(2)}) collective-permute-start(bf16[512,1536]{1,0:T(8,128)(2,1)S(1)} %convolution_convert_fusion.4.k_ref.v_ref), channel_id=1, source_target_pairs={{0,16},{1,17},{2,18},{3,19},{4,20},{5,21},{6,22},{7,23},{8,24},{9,... | collective-permute-start | bytes 4718600 | tf_op jit(solution)/shard_map/ppermute | solution.py:711
  141.7 69.3 %all-to-all-start.1 = ((bf16[16,96,768]{2,1,0:T(8,128)(2,1)}), bf16[16,96,768]{2,1,0:T(8,128)(2,1)}, u32[]{:S(2)}, u32[]{:S(2)}) async-start(bf16[16,96,768]{2,1,0:T(8,128)(2,1)} %broadcast_select_fusion.1), calls=%async_computation.1 | async-start | bytes 4718592 | tf_op jit(solution)/shard_map/all_to_all | solution.py:644
  164.2 9.9 %collective-permute-start.13 = (bf16[1536,768]{1,0:T(8,128)(2,1)}, bf16[1536,768]{1,0:T(8,128)(2,1)}, u32[]{:S(2)}, u32[]{:S(2)}) collective-permute-start(bf16[1536,768]{1,0:T(8,128)(2,1)} %bitcast.287), channel_id=1, source_target_pairs={{0,16},{16,0},{1,17},{17,1},{2,18},{18,2},{3,19},{19,3},{4,20},{20... | collective-permute-start | bytes 7077896 | tf_op jit(solution)/shard_map/ppermute | solution.py:502
  211.0 69.5 %all-to-all-start.2 = ((bf16[16,96,768]{2,1,0:T(8,128)(2,1)}), bf16[16,96,768]{2,1,0:T(8,128)(2,1)}, u32[]{:S(2)}, u32[]{:S(2)}) async-start(bf16[16,96,768]{2,1,0:T(8,128)(2,1)} %broadcast_select_fusion), calls=%async_computation.2 | async-start | bytes 4718592 | tf_op jit(solution)/shard_map/all_to_all | solution.py:644
  280.5 68.9 %all-to-all-start.3 = ((bf16[16,96,768]{2,1,0:T(8,128)(2,1)}), bf16[16,96,768]{2,1,0:T(8,128)(2,1)}, u32[]{:S(2)}, u32[]{:S(2)}) async-start(bf16[16,96,768]{2,1,0:T(8,128)(2,1)} %get-tuple-element.60), calls=%async_computation.3 | async-start | bytes 4718592 | tf_op jit(solution)/shard_map/all_to_all | solution.py:644
  348.9 35.0 %collective-permute-start.27 = (bf16[1536,768]{1,0:T(8,128)(2,1)}, bf16[1536,768]{1,0:T(8,128)(2,1)}, u32[]{:S(2)}, u32[]{:S(2)}) collective-permute-start(bf16[1536,768]{1,0:T(8,128)(2,1)} %get-tuple-element.79), channel_id=1, source_target_pairs={{0,16},{16,0},{1,17},{17,1},{2,18},{18,2},{3,19},{19,3},{4,20},{20... | collective-permute-start | bytes 7077896 | tf_op jit(solution)/shard_map/ppermute | solution.py:502
  348.9 39.7 %collective-permute-start.26 = (bf16[384,3072]{1,0:T(8,128)(2,1)}, bf16[384,3072]{1,0:T(8,128)(2,1)}, u32[]{:S(2)}, u32[]{:S(2)}) collective-permute-start(bf16[384,3072]{1,0:T(8,128)(2,1)} %get-tuple-element.77), channel_id=1, source_target_pairs={{0,16},{16,0},{1,17},{17,1},{2,18},{18,2},{3,19},{19,3},{4,20},{20... | collective-permute-start | bytes 7077896 | tf_op jit(solution)/shard_map/ppermute | solution.py:502
  350.4 55.1 %all-to-all-start.4 = ((bf16[16,96,768]{2,1,0:T(8,128)(2,1)}), bf16[16,96,768]{2,1,0:T(8,128)(2,1)}, u32[]{:S(2)}, u32[]{:S(2)}) async-start(bf16[16,96,768]{2,1,0:T(8,128)(2,1)} %get-tuple-element.61), calls=%async_computation.4 | async-start | bytes 4718592 | tf_op jit(solution)/shard_map/all_to_all | solution.py:644
  382.3 12.1 %collective-permute-start.14 = (bf16[2,512,768]{2,1,0:T(8,128)(2,1)S(1)}, bf16[2,512,768]{2,1,0:T(8,128)(2,1)S(1)}, u32[]{:S(2)}, u32[]{:S(2)}) collective-permute-start(bf16[2,512,768]{2,1,0:T(8,128)(2,1)S(1)} %get-tuple-element.66), channel_id=1, source_target_pairs={{16,0},{17,1},{18,2},{19,3},{20,4},{21,5},{22,6},{23,7},{24,8},{25... | collective-permute-start | bytes 4718600 | tf_op jit(solution)/shard_map/ppermute | solution.py:803
  407.5 99.1 %all-to-all-start.5 = ((bf16[16,192,768]{2,1,0:T(8,128)(2,1)}), bf16[16,192,768]{2,1,0:T(8,128)(2,1)}, u32[]{:S(2)}, u32[]{:S(2)}) async-start(bf16[16,192,768]{2,1,0:T(8,128)(2,1)} %get-tuple-element.62), calls=%async_computation.5 | async-start | bytes 9437184 | tf_op jit(solution)/shard_map/all_to_all | solution.py:644
  452.5 43.9 %collective-permute-start.16 = (bf16[384,1664]{1,0:T(8,128)(2,1)}, bf16[384,1664]{1,0:T(8,128)(2,1)}, u32[]{:S(2)}, u32[]{:S(2)}) collective-permute-start(bf16[384,1664]{1,0:T(8,128)(2,1)} %pad_maximum_fusion.8), channel_id=1, source_target_pairs={{0,16},{16,0},{1,17},{17,1},{2,18},{18,2},{3,19},{19,3},{4,20},{20... | collective-permute-start | bytes 3833864 | tf_op jit(solution)/shard_map/ppermute | solution.py:502
  452.5 10.4 %collective-permute-start.15 = (bf16[2,512,768]{2,1,0:T(8,128)(2,1)}, bf16[2,512,768]{2,1,0:T(8,128)(2,1)}, u32[]{:S(2)}, u32[]{:S(2)}) collective-permute-start(bf16[2,512,768]{2,1,0:T(8,128)(2,1)} %get-tuple-element.71), channel_id=1, source_target_pairs={{16,0},{17,1},{18,2},{19,3},{20,4},{21,5},{22,6},{23,7},{24,8},{25... | collective-permute-start | bytes 4718600 | tf_op jit(solution)/shard_map/ppermute | solution.py:803
  480.0 36.4 %collective-permute-start.21 = (bf16[384,1664]{1,0:T(8,128)(2,1)}, bf16[384,1664]{1,0:T(8,128)(2,1)}, u32[]{:S(2)}, u32[]{:S(2)}) collective-permute-start(bf16[384,1664]{1,0:T(8,128)(2,1)} %concatenate.77), channel_id=1, source_target_pairs={{0,16},{16,0},{1,17},{17,1},{2,18},{18,2},{3,19},{19,3},{4,20},{20... | collective-permute-start | bytes 3833864 | tf_op jit(solution)/shard_map/ppermute | solution.py:502
  508.6 20.3 %collective-permute-start.17 = (bf16[4,2,24,1664]{3,2,0,1:T(8,128)(2,1)S(1)}, bf16[4,2,24,1664]{3,2,0,1:T(8,128)(2,1)S(1)}, u32[]{:S(2)}, u32[]{:S(2)}) collective-permute-start(bf16[4,2,24,1664]{3,2,0,1:T(8,128)(2,1)S(1)} %fusion.99), channel_id=1, source_target_pairs={{0,2},{1,3},{2,0},{3,1},{4,6},{5,7},{6,4},{7,5},{8,10},{9,11},{10,... | collective-permute-start | bytes 1916936 | tf_op jit(solution)/shard_map/ppermute | solution.py:502
  518.2 17.1 %collective-permute-start.22 = (bf16[4,2,24,1664]{3,2,0,1:T(8,128)(2,1)S(1)}, bf16[4,2,24,1664]{3,2,0,1:T(8,128)(2,1)S(1)}, u32[]{:S(2)}, u32[]{:S(2)}) collective-permute-start(bf16[4,2,24,1664]{3,2,0,1:T(8,128)(2,1)S(1)} %fusion.100), channel_id=1, source_target_pairs={{0,1},{1,0},{2,3},{3,2},{4,5},{5,4},{6,7},{7,6},{8,9},{9,8},{10,11... | collective-permute-start | bytes 1916936 | tf_op jit(solution)/shard_map/ppermute | solution.py:502
  529.1 10.0 %collective-permute-start.18 = (bf16[4,24,1664]{2,1,0:T(8,128)(2,1)S(1)}, bf16[4,24,1664]{2,1,0:T(8,128)(2,1)S(1)}, u32[]{:S(2)}, u32[]{:S(2)}) collective-permute-start(bf16[4,24,1664]{2,1,0:T(8,128)(2,1)S(1)} %fusion.129), channel_id=1, source_target_pairs={{0,1},{1,0},{2,3},{3,2},{4,5},{5,4},{6,7},{7,6},{8,9},{9,8},{10,11... | collective-permute-start | bytes 958472 | tf_op jit(solution)/shard_map/ppermute | solution.py:502
  535.5 17.0 %collective-permute-start.23 = (bf16[4,24,1664]{2,1,0:T(8,128)(2,1)S(1)}, bf16[4,24,1664]{2,1,0:T(8,128)(2,1)S(1)}, u32[]{:S(2)}, u32[]{:S(2)}) collective-permute-start(bf16[4,24,1664]{2,1,0:T(8,128)(2,1)S(1)} %fusion.130), channel_id=1, source_target_pairs={{0,2},{1,3},{2,0},{3,1},{4,6},{5,7},{6,4},{7,5},{8,10},{9,11},{10,... | collective-permute-start | bytes 958472 | tf_op jit(solution)/shard_map/ppermute | solution.py:502
  539.2 17.8 %collective-permute-start.19 = (bf16[2,24,1664]{2,1,0:T(8,128)(2,1)S(1)}, bf16[2,24,1664]{2,1,0:T(8,128)(2,1)S(1)}, u32[]{:S(2)}, u32[]{:S(2)}) collective-permute-start(bf16[2,24,1664]{2,1,0:T(8,128)(2,1)S(1)} %fusion.139), channel_id=1, source_target_pairs={{0,4},{1,5},{2,6},{3,7},{4,0},{5,1},{6,2},{7,3},{8,12},{9,13},{10,... | collective-permute-start | bytes 479240 | tf_op jit(solution)/shard_map/ppermute | solution.py:502
  (138 other events, 1212.1 us)
